TPU v7x, 512 devices: a whole 4x4x16 slice. The times are simulated.
512 devices in a mesh: tp: 8 (over y, core), cp: 64 (over x, z).
Axes of the slice: x: 4, y: 4, z: 16, core: 2. Of those that a mesh axis runs over, the one named last changes fastest.
Arguments:
- features: bfloat16 [3, 8704, 8192], P(None, 'cp', 'tp'), may hold values from -6 to 6
- short_filter: float32 [3, 3, 8192], P(None, None, 'tp'), may hold values from -4 to 4
- long_filter: float32 [128, 8192], P(None, 'tp'), may hold values from -0.5 to 0.5
- skip_scale: float32 [8192], P('tp'), may hold values from -4 to 4
- out_weight: bfloat16 [8192, 8192], P('tp', 'cp'), may hold values from -0.1875 to 0.1875
Outputs:
- mixed: bfloat16 [8704, 8192], P('cp', 'tp')
All inputs are finite; a program needn't handle non-finite values.
Results may differ from a plain program's by a relative error of at most 0.017.
Values may be sent and summed in bfloat16 or wider, within the bound.
No kernel may reach another device: no remote copies, remote signals or barrier semaphores. Data moves between devices by JAX's collectives and lax.ppermute only.
A program may use at most 64 MiB of HBM per device.

v0:
```python
import jax
import jax.numpy as jnp
from jax import lax
from jax.sharding import PartitionSpec as P

TAPS = 128
SHORT = 3


def from_behind(block, axis, distance):
    devices = range(lax.axis_size(axis))
    route = [(i - distance, i) for i in devices if i - distance in devices]
    return lax.ppermute(block, axis, route)


def short_conv(extended, short_filter):
    out_rows = extended.shape[1] - (SHORT - 1)
    summed = jnp.zeros((extended.shape[0], out_rows, extended.shape[2]), jnp.float32)
    for lag in range(SHORT):
        begin = SHORT - 1 - lag
        summed = summed + short_filter[:, lag, None, :] * extended[:, begin : begin + out_rows, :]
    return summed


def long_conv(product_ext, long_filter, skip_scale):
    out_rows = product_ext.shape[0] - (TAPS - 1)
    summed = skip_scale[None, :] * product_ext[TAPS - 1 :]
    for lag in range(TAPS):
        begin = TAPS - 1 - lag
        summed = summed + long_filter[lag][None, :] * product_ext[begin : begin + out_rows]
    return summed


def local(features, short_filter, long_filter, skip_scale, out_weight):
    tok_rows = features.shape[1]
    tail_rows = TAPS + SHORT - 2
    earlier = from_behind(features[:, tok_rows - tail_rows :, :], "cp", 1)
    extended = jnp.concatenate((earlier, features), axis=1).astype(jnp.float32)
    shorted = short_conv(extended, short_filter)
    product_ext = shorted[1] * shorted[2]
    filtered = long_conv(product_ext, long_filter, skip_scale)
    gated = (shorted[0, TAPS - 1 :] * filtered).astype(jnp.bfloat16)
    partial_value = jnp.dot(
        gated,
        lax.all_gather(out_weight, "cp", axis=1, tiled=True),
        preferred_element_type=jnp.float32,
    )
    mixed = lax.psum_scatter(
        partial_value.astype(jnp.bfloat16), "tp", scatter_dimension=1, tiled=True
    )
    return mixed


def solution(mesh):
    return jax.shard_map(
        local,
        mesh=mesh,
        in_specs=(P(None, "cp", "tp"), P(None, None, "tp"), P(None, "tp"), P("tp"), P("tp", "cp")),
        out_specs=P("cp", "tp"),
        check_vma=False,
    )
```

profile of v0, /device:TPU:24, one launch (start us, length us, event | category | flops | bytes accessed | tf_op | source)
XLA Modules:
  0.0 333.6 jit_solution(2530894244873419933)
XLA Ops:
  6.5 0.0 copy-start
  6.5 0.0 all-gather.2.cloned.1.call-start
  6.5 0.7 all-gather.2.cloned.1.call-update
  7.3 0.0 reduce-scatter.2.cloned.1.call-start
  7.3 1.4 slice.1184
  8.7 3.9 %collective-permute-start = (bf16[3,129,1024]{2,1,0:T(8,128)(2,1)S(1)}, bf16[3,129,1024]{2,1,0:T(8,128)(2,1)S(1)}, u32[]{:S(2)}, u32[]{:S(2)}) collective-permute-start(bf16[3,129,1024]{2,1,0:T(8,128)(2,1)S(1)} %slice.1184), channel_id=1, source_target_pairs={{0,1},{1,2},{2,3},{3,4},{4,5},{5,6},{6,7},{7,8},{8,9},{9,10},{10,1... | collective-permute-start | bytes 2377736 | tf_op jit(solution)/shard_map/ppermute | solution.py:13
  12.6 0.9 fusion.267
  13.5 1.1 fusion.266
  14.7 1.4 fusion.264
  16.0 1.4 fusion.263
  17.4 1.4 fusion.265
  18.8 0.7 add.523
  19.5 2.0 fusion.262
  21.5 2.0 fusion.261
  23.5 2.0 fusion.260
  25.5 4.8 %collective-permute-done = bf16[3,129,1024]{2,1,0:T(8,128)(2,1)S(1)} collective-permute-done((bf16[3,129,1024]{2,1,0:T(8,128)(2,1)S(1)}, bf16[3,129,1024]{2,1,0:T(8,128)(2,1)S(1)}, u32[]{:S(2)}, u32[]{:S(2)}) %collective-permute-start) | collective-permute-done | bytes 792608 | tf_op jit(solution)/shard_map/ppermute | solution.py:13
  30.3 0.0 copy-done
  30.3 0.5 maximum_convert_fusion
  30.8 0.9 fusion
  31.8 1.2 slice_multiply_fusion.3
  33.0 199.6 %all-gather.2.cloned.1.call-done = bf16[1024,8192]{1,0:T(8,128)(2,1)} async-done(((bf16[1024,128]{1,0:T(8,128)(2,1)}), bf16[1024,8192]{1,0:T(8,128)(2,1)}) %all-gather.2.cloned.1.call-update) | async-done | bytes 16777232 | tf_op jit(solution)/shard_map/all_gather | solution.py:45
  232.6 61.1 %convolution_convert_fusion = bf16[136,8192]{1,0:T(8,128)(2,1)} fusion(bf16[1024,8192]{1,0:T(8,128)(2,1)} %all-gather.2.cloned.1.call-done, f32[1,263,1024]{2,1,0:T(8,128)} %slice_multiply_fusion.3, f32[3,263,1024]{2,1,0:T(8,128)S(1)} %fusion, f32[1024]{0:T(1024)S(1)} %add.523, f32[1024]{0:T(1024)S(1)} %bitcast.1306, f32[1024]{0:T(1024)S(1)} %bitcast.1307, ...), kind=kOutput, calls=%fused_computation | convolution fusion | flops 2318606336 | bytes 91389952 | tf_op jit(solution)/shard_map/dot_general | solution.py:43
  293.7 0.0 reduce-scatter.2.cloned.1.call-update
  293.7 33.1 %reduce-scatter.2.cloned.1.call-done = bf16[136,1024]{1,0:T(8,128)(2,1)} async-done(((bf16[136,8192]{1,0:T(8,128)(2,1)}), bf16[136,1024]{1,0:T(8,128)(2,1)}) %reduce-scatter.2.cloned.1.call-update) | async-done | bytes 278544 | tf_op jit(solution)/shard_map/reduce_scatter | solution.py:48
  (2 shorter events, 0.0 us)
Async XLA Ops:
  6.5 23.8 %copy-start = (bf16[3,136,1024]{2,1,0:T(8,128)(2,1)S(1)}, bf16[3,136,1024]{2,1,0:T(8,128)(2,1)}, u32[]{:S(2)}) copy-start(bf16[3,136,1024]{2,1,0:T(8,128)(2,1)} %param.5) | copy-start | bytes 2506756
  6.5 226.1 %all-gather.2.cloned.1.call-start = ((), (), s32[]{:S(2)}) async-start(), calls=%async_computation.1 | async-start | bytes 17039360 | tf_op jit(solution)/shard_map/all_gather | solution.py:45
  7.3 319.5 %reduce-scatter.2.cloned.1.call-start = ((), (), s32[]{:S(2)}) async-start(), calls=%async_computation.2 | async-start | bytes 2506752 | tf_op jit(solution)/shard_map/reduce_scatter | solution.py:48
  8.7 21.7 %collective-permute-start = (bf16[3,129,1024]{2,1,0:T(8,128)(2,1)S(1)}, bf16[3,129,1024]{2,1,0:T(8,128)(2,1)S(1)}, u32[]{:S(2)}, u32[]{:S(2)}) collective-permute-start(bf16[3,129,1024]{2,1,0:T(8,128)(2,1)S(1)} %slice.1184), channel_id=1, source_target_pairs={{0,1},{1,2},{2,3},{3,4},{4,5},{5,6},{6,7},{7,8},{8,9},{9,10},{10,1... | collective-permute-start | bytes 2377736 | tf_op jit(solution)/shard_map/ppermute | solution.py:13
Sparse Core Ops, SparseCore 0:
  10.3 222.2 all-gather.1
  293.8 32.9 reduce-scatter.1
where the time goes:
time: 338 us; the launch traced here: 334 us
  waiting for transfers between devices  238 us (70%)
  matrix products  61.1 us (18%)
  local copies, waits for them, and re-layouts  13.6 us (4%)
  between operations  13.5 us (4%)
  starting transfers between devices  3.91 us (1%)
    all_gather x1, waiting for transfers between devices, local(): lax.all_gather(out_weight, 'cp', axis=1, tiled=True)  200 us
    dot_general x1, matrix products, local(): jnp.dot(gated, lax.all_gather(out_weight, 'cp', axis=1, tiled=True), pref...  61.1 us
    reduce_scatter x1, waiting for transfers between devices, local(): lax.psum_scatter(partial_value.astype(jnp.bfloat16), 'tp', scatter_dimens...  33.1 us
    slice x7, local copies, waits for them, and re-layouts, long_conv(): long_filter[lag][None, :] * product_ext[begin:begin + out_rows]  11.2 us
  transfers between devices with their start and end apart: 3, of which 3 were waited for; matrix products, arithmetic and copies ran while one was open for 5% of the time, Pallas kernels for 0%

commit v1 on v0

v1 whole, which is shorter than its diff:
```python
import jax
import jax.numpy as jnp
from jax import lax
from jax.experimental import pallas as pl
from jax.experimental.pallas import tpu as pltpu
from jax.sharding import PartitionSpec as P

TAPS = 128
SHORT = 3
NX, NY, NZ, NC = 4, 4, 16, 2
ROWS = 136
LANES = 128
TILES = ROWS // 8
HALO = 144
BF = jnp.bfloat16
F32 = jnp.float32


def short_rows(ext, taps, i, rows):
    summed = taps[i, 0:1, :] * ext[i, 8 : 8 + rows, :]
    for lag in range(1, SHORT):
        summed = summed + taps[i, lag : lag + 1, :] * ext[i, 8 - lag : 8 - lag + rows, :]
    return summed


def pack_kernel(x_ref, taps_ref, out_ref, ext):
    ext[:, 0:8, :] = jnp.zeros((3, 8, LANES), F32)
    ext[:, 8 : 8 + ROWS, :] = x_ref[...].astype(F32)
    k = short_rows(ext, taps_ref, 1, ROWS)
    v = short_rows(ext, taps_ref, 2, ROWS)
    out_ref[0:128, :] = (k * v)[8:ROWS].astype(BF)
    row = lax.broadcasted_iota(jnp.int32, (8, LANES), 0)
    tails = [pltpu.roll(ext[i, ROWS : ROWS + 8, :], 2 + 2 * i, 0) for i in range(3)]
    tile = jnp.where(row < 2, tails[0], jnp.where(row < 4, tails[1], jnp.where(row < 6, tails[2], 0.0)))
    out_ref[128:144, :] = jnp.concatenate((tile, jnp.zeros((8, LANES), F32)), 0).astype(BF)


def conv_kernel(x_ref, halo_ref, taps_ref, long_ref, skip_ref, out_ref, ext, prod):
    tails = halo_ref[128:144, :].astype(F32)[0:8]
    for i in range(3):
        ext[i, 0:8, :] = pltpu.roll(tails, 6 - 2 * i, 0)
    ext[:, 8 : 8 + ROWS, :] = x_ref[...].astype(F32)
    k = short_rows(ext, taps_ref, 1, ROWS)
    v = short_rows(ext, taps_ref, 2, ROWS)
    prod[0:128, :] = halo_ref[0:128, :].astype(F32)
    prod[128 : 128 + ROWS, :] = k * v
    skip = skip_ref[...]
    start = tuple(skip * prod[128 + 8 * m : 136 + 8 * m, :] for m in range(TILES))

    def step(r, acc):
        acc = list(acc)
        taps = [jnp.broadcast_to(long_ref[pl.ds(8 * a + r, 1), :], (8, LANES)) for a in range(16)]
        for n in range(-15, TILES):
            part = prod[pl.ds(128 + 8 * n - r, 8), :]
            for a in range(16):
                if 0 <= n + a < TILES:
                    acc[n + a] = acc[n + a] + taps[a] * part
        return tuple(acc)

    acc = lax.fori_loop(0, 8, step, start)
    q = short_rows(ext, taps_ref, 0, ROWS)
    out_ref[...] = (q * jnp.concatenate(acc, 0)).astype(BF)


def run_pack(features, short_filter):
    return pl.pallas_call(
        pack_kernel,
        grid=(1024 // LANES,),
        in_specs=[
            pl.BlockSpec((3, ROWS, LANES), lambda i: (0, 0, i)),
            pl.BlockSpec((3, SHORT, LANES), lambda i: (0, 0, i)),
        ],
        out_specs=pl.BlockSpec((HALO, LANES), lambda i: (0, i)),
        out_shape=jax.ShapeDtypeStruct((HALO, 1024), BF),
        scratch_shapes=[pltpu.VMEM((3, 8 + ROWS, LANES), F32)],
        cost_estimate=pl.CostEstimate(flops=3000000, bytes_accessed=1200000, transcendentals=0),
        name="pack",
    )(features, short_filter)


def run_conv(features, halo, short_filter, long_filter, skip_scale):
    return pl.pallas_call(
        conv_kernel,
        grid=(1024 // LANES,),
        in_specs=[
            pl.BlockSpec((3, ROWS, LANES), lambda i: (0, 0, i)),
            pl.BlockSpec((HALO, LANES), lambda i: (0, i)),
            pl.BlockSpec((3, SHORT, LANES), lambda i: (0, 0, i)),
            pl.BlockSpec((TAPS, LANES), lambda i: (0, i)),
            pl.BlockSpec((1, LANES), lambda i: (0, i)),
        ],
        out_specs=pl.BlockSpec((ROWS, LANES), lambda i: (0, i)),
        out_shape=jax.ShapeDtypeStruct((ROWS, 1024), BF),
        scratch_shapes=[
            pltpu.VMEM((3, 8 + ROWS, LANES), F32),
            pltpu.VMEM((128 + ROWS, LANES), F32),
        ],
        cost_estimate=pl.CostEstimate(flops=36000000, bytes_accessed=2000000, transcendentals=0),
        name="conv",
    )(features, halo, short_filter, long_filter, skip_scale)


def mm_kernel(half_ref, a_ref, w_ref, out_ref):
    w = jnp.concatenate((w_ref[0], w_ref[1]), axis=1)
    c = jnp.dot(a_ref[...], w, preferred_element_type=F32)
    for m in range(NX):
        out_ref[m] = c[m * ROWS : (m + 1) * ROWS].astype(out_ref.dtype)


def run_mm(a, w, half, dtype):
    return pl.pallas_call(
        mm_kernel,
        grid_spec=pltpu.PrefetchScalarGridSpec(
            num_scalar_prefetch=1,
            grid=(4,),
            in_specs=[
                pl.BlockSpec((NX * ROWS, 1024), lambda j, h: (0, 0)),
                pl.BlockSpec((2, 1024, 128), lambda j, h: (h[0] * 4 + j, 0, 0)),
            ],
            out_specs=pl.BlockSpec((NX, ROWS, 256), lambda j, h: (0, 0, j)),
        ),
        out_shape=jax.ShapeDtypeStruct((NX, ROWS, 1024), dtype),
        cost_estimate=pl.CostEstimate(flops=1140000000, bytes_accessed=5000000, transcendentals=0),
        compiler_params=pltpu.CompilerParams(vmem_limit_bytes=32 * 1024 * 1024),
        name="mm",
    )(half, a, w)


def permute(block, axes, sizes, target):
    names = axes if len(axes) > 1 else axes[0]
    pairs = []
    for t in range(sizes[0]):
        for u in range(sizes[1]) if len(sizes) > 1 else (None,):
            if u is None:
                pairs.append((t, target(t)))
            else:
                d = target(t, u)
                pairs.append((t * sizes[1] + u, d[0] * sizes[1] + d[1]))
    return lax.ppermute(block, names, pairs)


def local(features, short_filter, long_filter, skip_scale, out_weight):
    tp, cp = lax.axis_index("tp"), lax.axis_index("cp")
    y, core = tp // NC, tp % NC

    weights = lax.all_gather(
        out_weight, "cp", axis=0, axis_index_groups=[[x * NZ + z for z in range(NZ)] for x in range(NX)]
    )

    packed = run_pack(features, short_filter)
    halo = lax.ppermute(packed, "cp", [(i, i + 1) for i in range(NX * NZ - 1)])
    gated = run_conv(features, halo, short_filter, long_filter, skip_scale[None, :])

    def from_x(shift):
        return permute(gated, ("cp",), (NX * NZ,), lambda i: (i + shift * NZ) % (NX * NZ))

    blocks = [gated, from_x(3), from_x(2), from_x(1)]
    twice = jnp.concatenate(blocks + blocks[:3], axis=0)
    a = lax.dynamic_slice_in_dim(twice, ROWS * y, NX * ROWS, 0)

    away = run_mm(a, weights, (1 - core)[None].astype(jnp.int32), BF)
    swapped = permute(away, ("tp",), (NY * NC,), lambda t: t ^ 1)
    here = run_mm(a, weights, core[None].astype(jnp.int32), F32)

    total = None
    for m in range(NX):
        piece = (here[m] + swapped[m].astype(F32)).astype(BF)

        def target(t, i, m=m):
            x, z = divmod(i, NZ)
            return x * NC + t % NC, (x + t // NC + m) % NX * NZ + z

        got = permute(piece, ("tp", "cp"), (NY * NC, NX * NZ), target).astype(F32)
        total = got if total is None else total + got
    return total.astype(BF)


def solution(mesh):
    return jax.shard_map(
        local,
        mesh=mesh,
        in_specs=(P(None, "cp", "tp"), P(None, None, "tp"), P(None, "tp"), P("tp"), P("tp", "cp")),
        out_specs=P("cp", "tp"),
        check_vma=False,
    )
```

time: 338 us -> 142 us (0.42)
  the two profiles are of different devices: /device:TPU:24 before, /device:TPU:8 now
where the time goes in v1:
time: 142 us; the launch traced here: 141 us
  waiting for transfers between devices  64.2 us (45%)
  starting transfers between devices  41.1 us (29%)
  Pallas kernels  17.2 us (12%)
  between operations  13.6 us (10%)
  local copies, waits for them, and re-layouts  4.1 us (3%)
    ppermute x8, starting transfers between devices, permute(): return lax.ppermute(block, names, pairs)  37.3 us
    all_gather x1, waiting for transfers between devices, local(): lax.all_gather(out_weight, 'cp', axis=0, axis_index_groups=[[x * NZ + z f...  30.3 us
    ppermute x8, waiting for transfers between devices, permute(): return lax.ppermute(block, names, pairs)  26.6 us
    pallas_call x1, Pallas kernels, run_conv(): pl.pallas_call(conv_kernel, grid=(1024 // LANES,), in_specs=[pl.BlockSpec...  8.18 us
    ppermute x1, waiting for transfers between devices, local(): halo = lax.ppermute(packed, 'cp', [(i, i + 1) for i in range(NX * NZ - 1)])  6.55 us
    pallas_call x1, Pallas kernels, run_pack(): pl.pallas_call(pack_kernel, grid=(1024 // LANES,), in_specs=[pl.BlockSpec...  5.07 us
    unnamed x14, local copies, waits for them, and re-layouts  3.99 us
    pallas_call x2, Pallas kernels, run_mm(): pl.pallas_call(mm_kernel, grid_spec=pltpu.PrefetchScalarGridSpec(num_scal...  3.93 us
  transfers between devices with their start and end apart: 10, of which 9 were waited for; matrix products, arithmetic and copies ran while one was open for 1% of the time, Pallas kernels for 11%

profile of v1, /device:TPU:8, one launch (start us, length us, event | category | flops | bytes accessed | tf_op | source)
XLA Modules:
  0.0 141.4 jit_solution(2434775175232243782)
XLA Ops:
  6.5 0.0 all-gather.3.cloned.1.call-start
  6.5 0.7 all-gather.3.cloned.1.call-update
  7.3 5.1 %pack.1 = bf16[144,1024]{1,0:T(8,128)(2,1)} custom-call(bf16[3,136,1024]{2,1,0:T(8,128)(2,1)} %x_ref.3, f32[3,3,1024]{2,1,0:T(4,128)} %taps_ref.3), custom_call_target="tpu_custom_call" | custom-call | flops 3000000 | bytes 1200000 | tf_op jit(solution)/shard_map/pack/pallas_call | solution.py:66
  12.3 3.8 %collective-permute-start = (bf16[144,1024]{1,0:T(8,128)(2,1)}, bf16[144,1024]{1,0:T(8,128)(2,1)S(1)}, u32[]{:S(2)}, u32[]{:S(2)}) collective-permute-start(bf16[144,1024]{1,0:T(8,128)(2,1)} %pack.1), channel_id=1, source_target_pairs={{0,1},{1,2},{2,3},{3,4},{4,5},{5,6},{6,7},{7,8},{8,9},{9,10},{10,1... | collective-permute-start | bytes 884744 | tf_op jit(solution)/shard_map/ppermute | solution.py:151
  16.2 6.5 %collective-permute-done.halo_ref = bf16[144,1024]{1,0:T(8,128)(2,1)S(1)} collective-permute-done((bf16[144,1024]{1,0:T(8,128)(2,1)}, bf16[144,1024]{1,0:T(8,128)(2,1)S(1)}, u32[]{:S(2)}, u32[]{:S(2)}) %collective-permute-start) | collective-permute-done | bytes 294944 | tf_op jit(solution)/shard_map/ppermute | solution.py:151
  22.7 0.0 copy-start.3
  22.7 0.7 copy-done.3
  23.4 8.2 %conv.1 = bf16[136,1024]{1,0:T(8,128)(2,1)} custom-call(bf16[3,136,1024]{2,1,0:T(8,128)(2,1)} %x_ref.3, bf16[144,1024]{1,0:T(8,128)(2,1)} %copy-done.3, f32[3,3,1024]{2,1,0:T(4,128)} %taps_ref.3, f32[128,1024]{1,0:T(8,128)} %long_ref.1, f32[1,1024]{1,0:T(1,128)} %bitcast.14), custom_call_target="tpu_custom_call" | custom-call | flops 36000000 | bytes 2000000 | tf_op jit(solution)/shard_map/conv/pallas_call | solution.py:82
  31.6 0.0 copy-start.2
  31.6 13.3 %collective-permute-start.1 = (bf16[136,1024]{1,0:T(8,128)(2,1)}, bf16[136,1024]{1,0:T(8,128)(2,1)S(1)}, u32[]{:S(2)}, u32[]{:S(2)}) collective-permute-start(bf16[136,1024]{1,0:T(8,128)(2,1)} %conv.1), channel_id=1, source_target_pairs={{0,48},{1,49},{2,50},{3,51},{4,52},{5,53},{6,54},{7,55},{8,56},{9,... | collective-permute-start | bytes 835592 | tf_op jit(solution)/shard_map/ppermute | solution.py:139
  44.9 2.4 %collective-permute-start.2 = (bf16[136,1024]{1,0:T(8,128)(2,1)}, bf16[136,1024]{1,0:T(8,128)(2,1)S(1)}, u32[]{:S(2)}, u32[]{:S(2)}) collective-permute-start(bf16[136,1024]{1,0:T(8,128)(2,1)} %conv.1), channel_id=1, source_target_pairs={{0,32},{1,33},{2,34},{3,35},{4,36},{5,37},{6,38},{7,39},{8,40},{9,... | collective-permute-start | bytes 835592 | tf_op jit(solution)/shard_map/ppermute | solution.py:139
  47.3 2.8 %collective-permute-start.3 = (bf16[136,1024]{1,0:T(8,128)(2,1)}, bf16[136,1024]{1,0:T(8,128)(2,1)S(1)}, u32[]{:S(2)}, u32[]{:S(2)}) collective-permute-start(bf16[136,1024]{1,0:T(8,128)(2,1)} %conv.1), channel_id=1, source_target_pairs={{0,16},{1,17},{2,18},{3,19},{4,20},{5,21},{6,22},{7,23},{8,24},{9,... | collective-permute-start | bytes 835592 | tf_op jit(solution)/shard_map/ppermute | solution.py:139
  50.1 1.0 constant_dynamic-update-slice_fusion.6
  51.1 5.4 %collective-permute-done.1 = bf16[136,1024]{1,0:T(8,128)(2,1)S(1)} collective-permute-done((bf16[136,1024]{1,0:T(8,128)(2,1)}, bf16[136,1024]{1,0:T(8,128)(2,1)S(1)}, u32[]{:S(2)}, u32[]{:S(2)}) %collective-permute-start.1) | collective-permute-done | bytes 278560 | tf_op jit(solution)/shard_map/ppermute | solution.py:139
  56.5 1.6 %collective-permute-done.2 = bf16[136,1024]{1,0:T(8,128)(2,1)S(1)} collective-permute-done((bf16[136,1024]{1,0:T(8,128)(2,1)}, bf16[136,1024]{1,0:T(8,128)(2,1)S(1)}, u32[]{:S(2)}, u32[]{:S(2)}) %collective-permute-start.2) | collective-permute-done | bytes 278560 | tf_op jit(solution)/shard_map/ppermute | solution.py:139
  58.2 3.9 %collective-permute-done.3 = bf16[136,1024]{1,0:T(8,128)(2,1)S(1)} collective-permute-done((bf16[136,1024]{1,0:T(8,128)(2,1)}, bf16[136,1024]{1,0:T(8,128)(2,1)S(1)}, u32[]{:S(2)}, u32[]{:S(2)}) %collective-permute-start.3) | collective-permute-done | bytes 278560 | tf_op jit(solution)/shard_map/ppermute | solution.py:139
  62.1 0.0 copy-done.2
  62.2 0.1 constant_dynamic-slice_fusion.a_ref
  62.2 30.3 %all-gather.3.cloned.1.call-done = bf16[16384,128]{1,0:T(8,128)(2,1)} async-done(((bf16[1024,128]{1,0:T(8,128)(2,1)}), bf16[16384,128]{1,0:T(8,128)(2,1)}) %all-gather.3.cloned.1.call-update) | async-done | bytes 4194320 | tf_op jit(solution)/shard_map/all_gather | solution.py:146
  92.6 0.0 copy-start
  92.6 2.2 %copy-done = bf16[16384,128]{1,0:T(8,128)(2,1)S(1)} copy-done((bf16[16384,128]{1,0:T(8,128)(2,1)S(1)}, bf16[16384,128]{1,0:T(8,128)(2,1)}, u32[]{:S(2)}) %copy-start) | copy-done | bytes 4194328
  94.8 0.0 copy-start.1
  94.8 1.9 %mm.3 = bf16[4,136,1024]{2,1,0:T(8,128)(2,1)S(1)} custom-call(s32[1]{0:T(128)} %bitcast.3.half_ref, bf16[544,1024]{1,0:T(8,128)(2,1)S(1)} %constant_dynamic-slice_fusion.a_ref, bf16[16,1024,128]{2,1,0:T(8,128)(2,1)S(1)} %bitcast.12), custom_call_target="tpu_custom_call" | custom-call | flops 1140000000 | bytes 5000000 | tf_op jit(solution)/shard_map/mm/pallas_call | solution.py:111
  96.7 1.9 %collective-permute-start.4 = (bf16[4,136,1024]{2,1,0:T(8,128)(2,1)S(1)}, bf16[4,136,1024]{2,1,0:T(8,128)(2,1)S(1)}, u32[]{:S(2)}, u32[]{:S(2)}) collective-permute-start(bf16[4,136,1024]{2,1,0:T(8,128)(2,1)S(1)} %mm.3), channel_id=1, source_target_pairs={{0,64},{64,0},{128,192},{192,128},{256,320},{320,256},{384,448},{4... | collective-permute-start | bytes 3342344 | tf_op jit(solution)/shard_map/ppermute | solution.py:139
  98.6 0.0 copy-done.1
  98.7 2.0 %mm.2 = f32[4,136,1024]{2,1,0:T(8,128)S(1)} custom-call(s32[1]{0:T(128)} %bitcast.half_ref, bf16[544,1024]{1,0:T(8,128)(2,1)S(1)} %constant_dynamic-slice_fusion.a_ref, bf16[16,1024,128]{2,1,0:T(8,128)(2,1)S(1)} %bitcast.13), custom_call_target="tpu_custom_call" | custom-call | flops 1140000000 | bytes 5000000 | tf_op jit(solution)/shard_map/mm/pallas_call | solution.py:111
  100.7 0.7 collective-permute-done.4
  101.4 0.4 fusion.4
  101.7 3.4 %collective-permute-start.5 = (bf16[136,1024]{1,0:T(8,128)(2,1)S(1)}, bf16[136,1024]{1,0:T(8,128)(2,1)S(1)}, u32[]{:S(2)}, u32[]{:S(2)}) collective-permute-start(bf16[136,1024]{1,0:T(8,128)(2,1)S(1)} %get-tuple-element.5), channel_id=1, source_target_pairs={{0,0},{1,1},{2,2},{3,3},{4,4},{5,5},{6,6},{7,7},{8,8},{9,9},{10,10... | collective-permute-start | bytes 835592 | tf_op jit(solution)/shard_map/ppermute | solution.py:139
  105.2 6.4 %collective-permute-start.6 = (bf16[136,1024]{1,0:T(8,128)(2,1)S(1)}, bf16[136,1024]{1,0:T(8,128)(2,1)S(1)}, u32[]{:S(2)}, u32[]{:S(2)}) collective-permute-start(bf16[136,1024]{1,0:T(8,128)(2,1)S(1)} %get-tuple-element.8), channel_id=1, source_target_pairs={{0,16},{1,17},{2,18},{3,19},{4,20},{5,21},{6,22},{7,23},{8,24},{9,... | collective-permute-start | bytes 835592 | tf_op jit(solution)/shard_map/ppermute | solution.py:139
  111.6 3.8 %collective-permute-start.7 = (bf16[136,1024]{1,0:T(8,128)(2,1)S(1)}, bf16[136,1024]{1,0:T(8,128)(2,1)S(1)}, u32[]{:S(2)}, u32[]{:S(2)}) collective-permute-start(bf16[136,1024]{1,0:T(8,128)(2,1)S(1)} %get-tuple-element.7), channel_id=1, source_target_pairs={{0,32},{1,33},{2,34},{3,35},{4,36},{5,37},{6,38},{7,39},{8,40},{9,... | collective-permute-start | bytes 835592 | tf_op jit(solution)/shard_map/ppermute | solution.py:139
  115.4 3.2 %collective-permute-start.8 = (bf16[136,1024]{1,0:T(8,128)(2,1)S(1)}, bf16[136,1024]{1,0:T(8,128)(2,1)S(1)}, u32[]{:S(2)}, u32[]{:S(2)}) collective-permute-start(bf16[136,1024]{1,0:T(8,128)(2,1)S(1)} %get-tuple-element.6), channel_id=1, source_target_pairs={{0,48},{1,49},{2,50},{3,51},{4,52},{5,53},{6,54},{7,55},{8,56},{9,... | collective-permute-start | bytes 835592 | tf_op jit(solution)/shard_map/ppermute | solution.py:139
  118.7 0.0 collective-permute-done.5
  118.7 2.0 %collective-permute-done.6 = bf16[136,1024]{1,0:T(8,128)(2,1)S(1)} collective-permute-done((bf16[136,1024]{1,0:T(8,128)(2,1)S(1)}, bf16[136,1024]{1,0:T(8,128)(2,1)S(1)}, u32[]{:S(2)}, u32[]{:S(2)}) %collective-permute-start.6) | collective-permute-done | bytes 278560 | tf_op jit(solution)/shard_map/ppermute | solution.py:139
  120.7 2.9 %collective-permute-done.7 = bf16[136,1024]{1,0:T(8,128)(2,1)S(1)} collective-permute-done((bf16[136,1024]{1,0:T(8,128)(2,1)S(1)}, bf16[136,1024]{1,0:T(8,128)(2,1)S(1)}, u32[]{:S(2)}, u32[]{:S(2)}) %collective-permute-start.7) | collective-permute-done | bytes 278560 | tf_op jit(solution)/shard_map/ppermute | solution.py:139
  123.6 10.1 %collective-permute-done.8 = bf16[136,1024]{1,0:T(8,128)(2,1)S(1)} collective-permute-done((bf16[136,1024]{1,0:T(8,128)(2,1)S(1)}, bf16[136,1024]{1,0:T(8,128)(2,1)S(1)}, u32[]{:S(2)}, u32[]{:S(2)}) %collective-permute-start.8) | collective-permute-done | bytes 278560 | tf_op jit(solution)/shard_map/ppermute | solution.py:139
  133.7 0.9 add_convert_fusion
  (6 shorter events, 0.1 us)
Async XLA Ops:
  6.5 86.0 %all-gather.3.cloned.1.call-start = ((), (), s32[]{:S(2)}) async-start(), calls=%async_computation | async-start | bytes 4456448 | tf_op jit(solution)/shard_map/all_gather | solution.py:146
  12.3 10.4 %collective-permute-start = (bf16[144,1024]{1,0:T(8,128)(2,1)}, bf16[144,1024]{1,0:T(8,128)(2,1)S(1)}, u32[]{:S(2)}, u32[]{:S(2)}) collective-permute-start(bf16[144,1024]{1,0:T(8,128)(2,1)} %pack.1), channel_id=1, source_target_pairs={{0,1},{1,2},{2,3},{3,4},{4,5},{5,6},{6,7},{7,8},{8,9},{9,10},{10,1... | collective-permute-start | bytes 884744 | tf_op jit(solution)/shard_map/ppermute | solution.py:151
  22.7 0.7 copy-start.3
  31.6 30.5 %copy-start.2 = (bf16[136,1024]{1,0:T(8,128)(2,1)S(1)}, bf16[136,1024]{1,0:T(8,128)(2,1)}, u32[]{:S(2)}) copy-start(bf16[136,1024]{1,0:T(8,128)(2,1)} %conv.1) | copy-start | bytes 835588
  31.6 24.9 %collective-permute-start.1 = (bf16[136,1024]{1,0:T(8,128)(2,1)}, bf16[136,1024]{1,0:T(8,128)(2,1)S(1)}, u32[]{:S(2)}, u32[]{:S(2)}) collective-permute-start(bf16[136,1024]{1,0:T(8,128)(2,1)} %conv.1), channel_id=1, source_target_pairs={{0,48},{1,49},{2,50},{3,51},{4,52},{5,53},{6,54},{7,55},{8,56},{9,... | collective-permute-start | bytes 835592 | tf_op jit(solution)/shard_map/ppermute | solution.py:139
  44.9 13.2 %collective-permute-start.2 = (bf16[136,1024]{1,0:T(8,128)(2,1)}, bf16[136,1024]{1,0:T(8,128)(2,1)S(1)}, u32[]{:S(2)}, u32[]{:S(2)}) collective-permute-start(bf16[136,1024]{1,0:T(8,128)(2,1)} %conv.1), channel_id=1, source_target_pairs={{0,32},{1,33},{2,34},{3,35},{4,36},{5,37},{6,38},{7,39},{8,40},{9,... | collective-permute-start | bytes 835592 | tf_op jit(solution)/shard_map/ppermute | solution.py:139
  47.3 14.7 %collective-permute-start.3 = (bf16[136,1024]{1,0:T(8,128)(2,1)}, bf16[136,1024]{1,0:T(8,128)(2,1)S(1)}, u32[]{:S(2)}, u32[]{:S(2)}) collective-permute-start(bf16[136,1024]{1,0:T(8,128)(2,1)} %conv.1), channel_id=1, source_target_pairs={{0,16},{1,17},{2,18},{3,19},{4,20},{5,21},{6,22},{7,23},{8,24},{9,... | collective-permute-start | bytes 835592 | tf_op jit(solution)/shard_map/ppermute | solution.py:139
  92.6 2.2 %copy-start = (bf16[16384,128]{1,0:T(8,128)(2,1)S(1)}, bf16[16384,128]{1,0:T(8,128)(2,1)}, u32[]{:S(2)}) copy-start(bf16[16384,128]{1,0:T(8,128)(2,1)} %all-gather.3.cloned.1.call-done) | copy-start | bytes 12582916
  94.8 3.9 %copy-start.1 = (bf16[16384,128]{1,0:T(8,128)(2,1)S(1)}, bf16[16384,128]{1,0:T(8,128)(2,1)}, u32[]{:S(2)}) copy-start(bf16[16384,128]{1,0:T(8,128)(2,1)} %all-gather.3.cloned.1.call-done) | copy-start | bytes 12582916
  96.7 4.6 %collective-permute-start.4 = (bf16[4,136,1024]{2,1,0:T(8,128)(2,1)S(1)}, bf16[4,136,1024]{2,1,0:T(8,128)(2,1)S(1)}, u32[]{:S(2)}, u32[]{:S(2)}) collective-permute-start(bf16[4,136,1024]{2,1,0:T(8,128)(2,1)S(1)} %mm.3), channel_id=1, source_target_pairs={{0,64},{64,0},{128,192},{192,128},{256,320},{320,256},{384,448},{4... | collective-permute-start | bytes 3342344 | tf_op jit(solution)/shard_map/ppermute | solution.py:139
  101.7 16.9 %collective-permute-start.5 = (bf16[136,1024]{1,0:T(8,128)(2,1)S(1)}, bf16[136,1024]{1,0:T(8,128)(2,1)S(1)}, u32[]{:S(2)}, u32[]{:S(2)}) collective-permute-start(bf16[136,1024]{1,0:T(8,128)(2,1)S(1)} %get-tuple-element.5), channel_id=1, source_target_pairs={{0,0},{1,1},{2,2},{3,3},{4,4},{5,5},{6,6},{7,7},{8,8},{9,9},{10,10... | collective-permute-start | bytes 835592 | tf_op jit(solution)/shard_map/ppermute | solution.py:139
  105.2 15.6 %collective-permute-start.6 = (bf16[136,1024]{1,0:T(8,128)(2,1)S(1)}, bf16[136,1024]{1,0:T(8,128)(2,1)S(1)}, u32[]{:S(2)}, u32[]{:S(2)}) collective-permute-start(bf16[136,1024]{1,0:T(8,128)(2,1)S(1)} %get-tuple-element.8), channel_id=1, source_target_pairs={{0,16},{1,17},{2,18},{3,19},{4,20},{5,21},{6,22},{7,23},{8,24},{9,... | collective-permute-start | bytes 835592 | tf_op jit(solution)/shard_map/ppermute | solution.py:139
  111.6 12.0 %collective-permute-start.7 = (bf16[136,1024]{1,0:T(8,128)(2,1)S(1)}, bf16[136,1024]{1,0:T(8,128)(2,1)S(1)}, u32[]{:S(2)}, u32[]{:S(2)}) collective-permute-start(bf16[136,1024]{1,0:T(8,128)(2,1)S(1)} %get-tuple-element.7), channel_id=1, source_target_pairs={{0,32},{1,33},{2,34},{3,35},{4,36},{5,37},{6,38},{7,39},{8,40},{9,... | collective-permute-start | bytes 835592 | tf_op jit(solution)/shard_map/ppermute | solution.py:139
  115.4 18.3 %collective-permute-start.8 = (bf16[136,1024]{1,0:T(8,128)(2,1)S(1)}, bf16[136,1024]{1,0:T(8,128)(2,1)S(1)}, u32[]{:S(2)}, u32[]{:S(2)}) collective-permute-start(bf16[136,1024]{1,0:T(8,128)(2,1)S(1)} %get-tuple-element.6), channel_id=1, source_target_pairs={{0,48},{1,49},{2,50},{3,51},{4,52},{5,53},{6,54},{7,55},{8,56},{9,... | collective-permute-start | bytes 835592 | tf_op jit(solution)/shard_map/ppermute | solution.py:139
Sparse Core Ops, SparseCore 0:
  9.4 83.0 all-gather.2

commit v2 on v1

v2 whole, which is shorter than its diff:
```python
import jax
import jax.numpy as jnp
from jax import lax
from jax.experimental import pallas as pl
from jax.experimental.pallas import tpu as pltpu
from jax.sharding import PartitionSpec as P

TAPS = 128
SHORT = 3
NX, NY, NZ, NC = 4, 4, 16, 2
ROWS = 136
LANES = 128
WIDE = 256
TILES = ROWS // 8
HALO = 144
CHUNKS = ((0, 4), (4, 4))
BF = jnp.bfloat16
F32 = jnp.float32


def short_rows(ext, taps, i, first, rows):
    summed = taps[i, 0:1, :] * ext[i, first : first + rows, :]
    for lag in range(1, SHORT):
        summed = summed + taps[i, lag : lag + 1, :] * ext[i, first - lag : first - lag + rows, :]
    return summed


def pack_kernel(x_ref, taps_ref, out_ref, ext):
    ext[...] = x_ref[...].astype(F32)
    k = short_rows(ext, taps_ref, 1, 8, 128)
    v = short_rows(ext, taps_ref, 2, 8, 128)
    out_ref[0:128, :] = (k * v).astype(BF)
    row = lax.broadcasted_iota(jnp.int32, (8, WIDE), 0)
    tails = [pltpu.roll(ext[i, ROWS - 8 : ROWS, :], 2 + 2 * i, 0) for i in range(3)]
    tile = jnp.where(row < 2, tails[0], jnp.where(row < 4, tails[1], jnp.where(row < 6, tails[2], 0.0)))
    out_ref[128:144, :] = jnp.concatenate((tile, jnp.zeros((8, WIDE), F32)), 0).astype(BF)


def conv_kernel(x_ref, halo_ref, taps_ref, long_ref, skip_ref, out_ref, ext, prod):
    tails = halo_ref[128:144, :].astype(F32)[0:8]
    for i in range(3):
        ext[i, 0:8, :] = pltpu.roll(tails, 6 - 2 * i, 0)
    ext[:, 8 : 8 + ROWS, :] = x_ref[...].astype(F32)
    k = short_rows(ext, taps_ref, 1, 8, ROWS)
    v = short_rows(ext, taps_ref, 2, 8, ROWS)
    prod[0:128, :] = halo_ref[0:128, :].astype(F32)
    prod[128 : 128 + ROWS, :] = k * v
    skip = skip_ref[...]
    start = tuple(skip * prod[128 + 8 * m : 136 + 8 * m, :] for m in range(TILES))

    def step(r, acc):
        acc = list(acc)
        taps = [jnp.broadcast_to(long_ref[pl.ds(8 * a + r, 1), :], (8, LANES)) for a in range(16)]
        for n in range(-15, TILES):
            part = prod[pl.ds(128 + 8 * n - r, 8), :]
            for a in range(16):
                if 0 <= n + a < TILES:
                    acc[n + a] = acc[n + a] + taps[a] * part
        return tuple(acc)

    acc = lax.fori_loop(0, 8, step, start)
    q = short_rows(ext, taps_ref, 0, 8, ROWS)
    out_ref[...] = (q * jnp.concatenate(acc, 0)).astype(BF)


def run_pack(features, short_filter):
    return pl.pallas_call(
        pack_kernel,
        grid=(1024 // WIDE,),
        in_specs=[
            pl.BlockSpec((3, ROWS, WIDE), lambda i: (0, 0, i)),
            pl.BlockSpec((3, SHORT, WIDE), lambda i: (0, 0, i)),
        ],
        out_specs=pl.BlockSpec((HALO, WIDE), lambda i: (0, i)),
        out_shape=jax.ShapeDtypeStruct((HALO, 1024), BF),
        scratch_shapes=[pltpu.VMEM((3, ROWS, WIDE), F32)],
        cost_estimate=pl.CostEstimate(flops=3000000, bytes_accessed=6000000, transcendentals=0),
        name="pack",
    )(features, short_filter)


def run_conv(features, halo, short_filter, long_filter, skip_scale):
    return pl.pallas_call(
        conv_kernel,
        grid=(1024 // LANES,),
        in_specs=[
            pl.BlockSpec((3, ROWS, LANES), lambda i: (0, 0, i)),
            pl.BlockSpec((HALO, LANES), lambda i: (0, i)),
            pl.BlockSpec((3, SHORT, LANES), lambda i: (0, 0, i)),
            pl.BlockSpec((TAPS, LANES), lambda i: (0, i)),
            pl.BlockSpec((1, LANES), lambda i: (0, i)),
        ],
        out_specs=pl.BlockSpec((ROWS, LANES), lambda i: (0, i)),
        out_shape=jax.ShapeDtypeStruct((ROWS, 1024), BF),
        scratch_shapes=[
            pltpu.VMEM((3, 8 + ROWS, LANES), F32),
            pltpu.VMEM((128 + ROWS, LANES), F32),
        ],
        cost_estimate=pl.CostEstimate(flops=36000000, bytes_accessed=20000000, transcendentals=0),
        name="conv",
    )(features, halo, short_filter, long_filter, skip_scale)


def mm_kernel(where_ref, a_ref, w_ref, *rest):
    outs, (held, sem) = rest[:NX], rest[NX:]
    y, core = where_ref[0], where_ref[1]

    def copy(k, chunk):
        begin, size = CHUNKS[chunk]
        return pltpu.make_async_copy(
            w_ref.at[pl.ds(NZ * k + 8 * core + begin, size)], held.at[pl.ds(8 * k + begin, size)], sem.at[chunk, k]
        )

    for chunk in range(len(CHUNKS)):
        for k in range(NC):
            copy(k, chunk).start()
    for chunk, (begin, size) in enumerate(CHUNKS):
        c = None
        for k in range(NC):
            copy(k, chunk).wait()
            w = jnp.concatenate([held[8 * k + begin + i] for i in range(size)], axis=1)
            part = jnp.dot(a_ref[k], w, preferred_element_type=F32)
            c = part if c is None else c + part
        parts = [c[s * ROWS : (s + 1) * ROWS].astype(BF) for s in range(NX)]
        for row in range(NY):

            @pl.when(y == row)
            def _(row=row, parts=parts, begin=begin, size=size):
                for m in range(NX):
                    outs[m][:, 128 * begin : 128 * (begin + size)] = jnp.where(core == 0, parts[row ^ m], parts[row ^ m ^ 2])


def run_mm(where, a, w):
    vmem = pl.BlockSpec(memory_space=pltpu.VMEM)
    return pl.pallas_call(
        mm_kernel,
        in_specs=[pl.BlockSpec(memory_space=pltpu.SMEM), vmem, pl.BlockSpec(memory_space=pltpu.HBM)],
        out_specs=[vmem] * NX,
        out_shape=[jax.ShapeDtypeStruct((ROWS, 1024), BF)] * NX,
        scratch_shapes=[pltpu.VMEM((16, 1024, 128), BF), pltpu.SemaphoreType.DMA((len(CHUNKS), NC))],
        cost_estimate=pl.CostEstimate(flops=2280000000, bytes_accessed=7000000, transcendentals=0),
        compiler_params=pltpu.CompilerParams(vmem_limit_bytes=50 * 1024 * 1024),
        name="mm",
    )(where, a, w)


def permute(block, target):
    pairs = []
    for t in range(NY * NC):
        for i in range(NX * NZ):
            to = target(t // NC, t % NC, i // NZ, i % NZ)
            if to is not None:
                y, c, x, z = to
                pairs.append((t * NX * NZ + i, (y * NC + c) * NX * NZ + x * NZ + z))
    return lax.ppermute(block, ("tp", "cp"), pairs)


def local(features, short_filter, long_filter, skip_scale, out_weight):
    tp = lax.axis_index("tp")
    y, core = tp // NC, tp % NC

    groups = [
        [(gy * NC + c) * NX * NZ + gx * NZ + gz for c in range(NC) for gz in range(NZ)]
        for gy in range(NY)
        for gx in range(NX)
    ]
    weights = lax.all_gather(out_weight, ("tp", "cp"), axis=0, axis_index_groups=groups)

    packed = run_pack(features, short_filter)
    halo = lax.ppermute(packed, "cp", [(i, i + 1) for i in range(NX * NZ - 1)])
    gated = run_conv(features, halo, short_filter, long_filter, skip_scale[None, :])

    from_x = [gated] + [permute(gated, lambda y, c, x, z, s=s: (y, c, x ^ s, z)) for s in range(1, NX)]
    mine = jnp.concatenate(from_x, axis=0)
    other = permute(mine, lambda y, c, x, z: (y, 1 - c, x, z))
    a = jnp.stack((jnp.where(core == 0, mine, other), jnp.where(core == 0, other, mine)))

    pieces = run_mm(jnp.stack((y, core)).astype(jnp.int32), a, weights)
    total = None
    for m, piece in enumerate(pieces):
        got = permute(piece, lambda y, c, x, z, m=m: (x, c, x ^ y ^ m ^ (2 * c), z)).astype(F32)
        total = got if total is None else total + got
    return total.astype(BF)


def solution(mesh):
    return jax.shard_map(
        local,
        mesh=mesh,
        in_specs=(P(None, "cp", "tp"), P(None, None, "tp"), P(None, "tp"), P("tp"), P("tp", "cp")),
        out_specs=P("cp", "tp"),
        check_vma=False,
    )
```

time: 142 us -> 133 us (0.937)
  the two profiles are of different devices: /device:TPU:8 before, /device:TPU:24 now
where the time goes in v2:
time: 133 us; the launch traced here: 132 us
  waiting for transfers between devices  57.7 us (43%)
  starting transfers between devices  41.1 us (31%)
  Pallas kernels  16.7 us (13%)
  between operations  13.5 us (10%)
  other arithmetic  2.73 us (2%)
    ppermute x8, starting transfers between devices, permute(): return lax.ppermute(block, ('tp', 'cp'), pairs)  37.3 us
    ppermute x8, waiting for transfers between devices, permute(): return lax.ppermute(block, ('tp', 'cp'), pairs)  25.7 us
    all_gather x1, waiting for transfers between devices, local(): lax.all_gather(out_weight, ('tp', 'cp'), axis=0, axis_index_groups=groups)  24.7 us
    pallas_call x1, Pallas kernels, run_conv(): pl.pallas_call(conv_kernel, grid=(1024 // LANES,), in_specs=[pl.BlockSpec...  8.18 us
    ppermute x1, waiting for transfers between devices, local(): halo = lax.ppermute(packed, 'cp', [(i, i + 1) for i in range(NX * NZ - 1)])  6.55 us
    pallas_call x1, Pallas kernels, run_mm(): pl.pallas_call(mm_kernel, in_specs=[pl.BlockSpec(memory_space=pltpu.SMEM)...  5.09 us
    ppermute x1, starting transfers between devices, local(): halo = lax.ppermute(packed, 'cp', [(i, i + 1) for i in range(NX * NZ - 1)])  3.83 us
    pallas_call x1, Pallas kernels, run_pack(): pl.pallas_call(pack_kernel, grid=(1024 // WIDE,), in_specs=[pl.BlockSpec(...  3.45 us
  transfers between devices with their start and end apart: 10, of which 9 were waited for; matrix products, arithmetic and copies ran while one was open for 1% of the time, Pallas kernels for 9%

profile of v2, /device:TPU:24, one launch (start us, length us, event | category | flops | bytes accessed | tf_op | source)
XLA Modules:
  0.0 132.5 jit_solution(4893919167130455382)
XLA Ops:
  6.5 0.0 all-gather.3.cloned.1.call-start
  6.5 0.7 all-gather.3.cloned.1.call-update
  7.3 3.4 %pack.1 = bf16[144,1024]{1,0:T(8,128)(2,1)} custom-call(bf16[3,136,1024]{2,1,0:T(8,128)(2,1)} %x_ref.3, f32[3,3,1024]{2,1,0:T(4,128)} %taps_ref.3), custom_call_target="tpu_custom_call" | custom-call | flops 3000000 | bytes 6000000 | tf_op jit(solution)/shard_map/pack/pallas_call | solution.py:67
  10.7 3.8 %collective-permute-start = (bf16[144,1024]{1,0:T(8,128)(2,1)}, bf16[144,1024]{1,0:T(8,128)(2,1)S(1)}, u32[]{:S(2)}, u32[]{:S(2)}) collective-permute-start(bf16[144,1024]{1,0:T(8,128)(2,1)} %pack.1), channel_id=1, source_target_pairs={{0,1},{1,2},{2,3},{3,4},{4,5},{5,6},{6,7},{7,8},{8,9},{9,10},{10,1... | collective-permute-start | bytes 884744 | tf_op jit(solution)/shard_map/ppermute | solution.py:170
  14.5 6.5 %collective-permute-done.halo_ref = bf16[144,1024]{1,0:T(8,128)(2,1)S(1)} collective-permute-done((bf16[144,1024]{1,0:T(8,128)(2,1)}, bf16[144,1024]{1,0:T(8,128)(2,1)S(1)}, u32[]{:S(2)}, u32[]{:S(2)}) %collective-permute-start) | collective-permute-done | bytes 294944 | tf_op jit(solution)/shard_map/ppermute | solution.py:170
  21.1 0.0 copy-start.1
  21.1 0.7 copy-done.1
  21.8 8.2 %conv.1 = bf16[136,1024]{1,0:T(8,128)(2,1)} custom-call(bf16[3,136,1024]{2,1,0:T(8,128)(2,1)} %x_ref.3, bf16[144,1024]{1,0:T(8,128)(2,1)} %copy-done.1, f32[3,3,1024]{2,1,0:T(4,128)} %taps_ref.3, f32[128,1024]{1,0:T(8,128)} %long_ref.1, f32[1,1024]{1,0:T(1,128)} %bitcast.9), custom_call_target="tpu_custom_call" | custom-call | flops 36000000 | bytes 20000000 | tf_op jit(solution)/shard_map/conv/pallas_call | solution.py:83
  30.0 0.0 copy-start
  30.0 11.7 %collective-permute-start.1 = (bf16[136,1024]{1,0:T(8,128)(2,1)}, bf16[136,1024]{1,0:T(8,128)(2,1)S(1)}, u32[]{:S(2)}, u32[]{:S(2)}) collective-permute-start(bf16[136,1024]{1,0:T(8,128)(2,1)} %conv.1), channel_id=1, source_target_pairs={{0,16},{1,17},{2,18},{3,19},{4,20},{5,21},{6,22},{7,23},{8,24},{9,... | collective-permute-start | bytes 835592 | tf_op jit(solution)/shard_map/ppermute | solution.py:155
  41.7 4.9 %collective-permute-start.2 = (bf16[136,1024]{1,0:T(8,128)(2,1)}, bf16[136,1024]{1,0:T(8,128)(2,1)S(1)}, u32[]{:S(2)}, u32[]{:S(2)}) collective-permute-start(bf16[136,1024]{1,0:T(8,128)(2,1)} %conv.1), channel_id=1, source_target_pairs={{0,32},{1,33},{2,34},{3,35},{4,36},{5,37},{6,38},{7,39},{8,40},{9,... | collective-permute-start | bytes 835592 | tf_op jit(solution)/shard_map/ppermute | solution.py:155
  46.6 1.9 %collective-permute-start.3 = (bf16[136,1024]{1,0:T(8,128)(2,1)}, bf16[136,1024]{1,0:T(8,128)(2,1)S(1)}, u32[]{:S(2)}, u32[]{:S(2)}) collective-permute-start(bf16[136,1024]{1,0:T(8,128)(2,1)} %conv.1), channel_id=1, source_target_pairs={{0,48},{1,49},{2,50},{3,51},{4,52},{5,53},{6,54},{7,55},{8,56},{9,... | collective-permute-start | bytes 835592 | tf_op jit(solution)/shard_map/ppermute | solution.py:155
  48.6 0.9 collective-permute-done.1
  49.5 7.4 %collective-permute-done.2 = bf16[136,1024]{1,0:T(8,128)(2,1)S(1)} collective-permute-done((bf16[136,1024]{1,0:T(8,128)(2,1)}, bf16[136,1024]{1,0:T(8,128)(2,1)S(1)}, u32[]{:S(2)}, u32[]{:S(2)}) %collective-permute-start.2) | collective-permute-done | bytes 278560 | tf_op jit(solution)/shard_map/ppermute | solution.py:155
  56.9 5.3 %collective-permute-done.3 = bf16[136,1024]{1,0:T(8,128)(2,1)S(1)} collective-permute-done((bf16[136,1024]{1,0:T(8,128)(2,1)}, bf16[136,1024]{1,0:T(8,128)(2,1)S(1)}, u32[]{:S(2)}, u32[]{:S(2)}) %collective-permute-start.3) | collective-permute-done | bytes 278560 | tf_op jit(solution)/shard_map/ppermute | solution.py:155
  62.2 1.0 pad_maximum_fusion.1
  63.2 1.9 %collective-permute-start.4 = (bf16[544,1024]{1,0:T(8,128)(2,1)S(1)}, bf16[544,1024]{1,0:T(8,128)(2,1)S(1)}, u32[]{:S(2)}, u32[]{:S(2)}) collective-permute-start(bf16[544,1024]{1,0:T(8,128)(2,1)S(1)} %pad_maximum_fusion.1), channel_id=1, source_target_pairs={{0,64},{1,65},{2,66},{3,67},{4,68},{5,69},{6,70},{7,71},{8,72},{9,... | collective-permute-start | bytes 3342344 | tf_op jit(solution)/shard_map/ppermute | solution.py:155
  65.1 0.1 pad_add_fusion.where_ref
  65.2 2.6 %collective-permute-done.4 = bf16[544,1024]{1,0:T(8,128)(2,1)S(1)} collective-permute-done((bf16[544,1024]{1,0:T(8,128)(2,1)S(1)}, bf16[544,1024]{1,0:T(8,128)(2,1)S(1)}, u32[]{:S(2)}, u32[]{:S(2)}) %collective-permute-start.4) | collective-permute-done | bytes 1114144 | tf_op jit(solution)/shard_map/ppermute | solution.py:155
  67.8 0.0 copy-done
  67.9 0.5 select_bitcast_fusion.1
  68.4 0.2 pad_maximum_fusion.a_ref
  68.6 24.7 %all-gather.3.cloned.1.call-done = bf16[32768,128]{1,0:T(8,128)(2,1)} async-done(((bf16[1024,128]{1,0:T(8,128)(2,1)}), bf16[32768,128]{1,0:T(8,128)(2,1)}) %all-gather.3.cloned.1.call-update) | async-done | bytes 8388624 | tf_op jit(solution)/shard_map/all_gather | solution.py:167
  93.3 5.1 %mm.1 = (bf16[136,1024]{1,0:T(8,128)(2,1)S(1)}, bf16[136,1024]{1,0:T(8,128)(2,1)S(1)}, bf16[136,1024]{1,0:T(8,128)(2,1)S(1)}, bf16[136,1024]{1,0:T(8,128)(2,1)S(1)}) custom-call(s32[2]{0:T(128)S(1)} %pad_add_fusion.where_ref, bf16[2,544,1024]{2,1,0:T(8,128)(2,1)S(1)} %pad_maximum_fusion.a_ref, bf16[32,1024,128]{2,1,0:T(8,128)(2,1)} %bitcast.8), custom_call_target="tpu_custom_call" | custom-call | flops 2280000000 | bytes 7000000 | tf_op jit(solution)/shard_map/mm/pallas_call | solution.py:135
  98.4 4.5 %collective-permute-start.5 = (bf16[136,1024]{1,0:T(8,128)(2,1)S(1)}, bf16[136,1024]{1,0:T(8,128)(2,1)S(1)}, u32[]{:S(2)}, u32[]{:S(2)}) collective-permute-start(bf16[136,1024]{1,0:T(8,128)(2,1)S(1)} %get-tuple-element.9), channel_id=1, source_target_pairs={{0,0},{1,1},{2,2},{3,3},{4,4},{5,5},{6,6},{7,7},{8,8},{9,9},{10,10... | collective-permute-start | bytes 835592 | tf_op jit(solution)/shard_map/ppermute | solution.py:155
  102.9 5.3 %collective-permute-start.6 = (bf16[136,1024]{1,0:T(8,128)(2,1)S(1)}, bf16[136,1024]{1,0:T(8,128)(2,1)S(1)}, u32[]{:S(2)}, u32[]{:S(2)}) collective-permute-start(bf16[136,1024]{1,0:T(8,128)(2,1)S(1)} %get-tuple-element.10), channel_id=1, source_target_pairs={{0,16},{1,17},{2,18},{3,19},{4,20},{5,21},{6,22},{7,23},{8,24},{9,... | collective-permute-start | bytes 835592 | tf_op jit(solution)/shard_map/ppermute | solution.py:155
  108.2 1.9 %collective-permute-start.7 = (bf16[136,1024]{1,0:T(8,128)(2,1)S(1)}, bf16[136,1024]{1,0:T(8,128)(2,1)S(1)}, u32[]{:S(2)}, u32[]{:S(2)}) collective-permute-start(bf16[136,1024]{1,0:T(8,128)(2,1)S(1)} %get-tuple-element.11), channel_id=1, source_target_pairs={{0,32},{1,33},{2,34},{3,35},{4,36},{5,37},{6,38},{7,39},{8,40},{9,... | collective-permute-start | bytes 835592 | tf_op jit(solution)/shard_map/ppermute | solution.py:155
  110.1 5.1 %collective-permute-start.8 = (bf16[136,1024]{1,0:T(8,128)(2,1)S(1)}, bf16[136,1024]{1,0:T(8,128)(2,1)S(1)}, u32[]{:S(2)}, u32[]{:S(2)}) collective-permute-start(bf16[136,1024]{1,0:T(8,128)(2,1)S(1)} %get-tuple-element.12), channel_id=1, source_target_pairs={{0,48},{1,49},{2,50},{3,51},{4,52},{5,53},{6,54},{7,55},{8,56},{9,... | collective-permute-start | bytes 835592 | tf_op jit(solution)/shard_map/ppermute | solution.py:155
  115.2 0.0 collective-permute-done.5
  115.2 1.2 collective-permute-done.6
  116.4 7.7 %collective-permute-done.7 = bf16[136,1024]{1,0:T(8,128)(2,1)S(1)} collective-permute-done((bf16[136,1024]{1,0:T(8,128)(2,1)S(1)}, bf16[136,1024]{1,0:T(8,128)(2,1)S(1)}, u32[]{:S(2)}, u32[]{:S(2)}) %collective-permute-start.7) | collective-permute-done | bytes 278560 | tf_op jit(solution)/shard_map/ppermute | solution.py:155
  124.1 0.6 collective-permute-done.8
  124.7 0.9 add_convert_fusion
Async XLA Ops:
  6.5 86.7 %all-gather.3.cloned.1.call-start = ((), (), s32[]{:S(2)}) async-start(), calls=%async_computation | async-start | bytes 8650752 | tf_op jit(solution)/shard_map/all_gather | solution.py:167
  10.7 10.4 %collective-permute-start = (bf16[144,1024]{1,0:T(8,128)(2,1)}, bf16[144,1024]{1,0:T(8,128)(2,1)S(1)}, u32[]{:S(2)}, u32[]{:S(2)}) collective-permute-start(bf16[144,1024]{1,0:T(8,128)(2,1)} %pack.1), channel_id=1, source_target_pairs={{0,1},{1,2},{2,3},{3,4},{4,5},{5,6},{6,7},{7,8},{8,9},{9,10},{10,1... | collective-permute-start | bytes 884744 | tf_op jit(solution)/shard_map/ppermute | solution.py:170
  21.1 0.7 copy-start.1
  30.0 37.9 %copy-start = (bf16[136,1024]{1,0:T(8,128)(2,1)S(1)}, bf16[136,1024]{1,0:T(8,128)(2,1)}, u32[]{:S(2)}) copy-start(bf16[136,1024]{1,0:T(8,128)(2,1)} %conv.1) | copy-start | bytes 835588
  30.0 19.5 %collective-permute-start.1 = (bf16[136,1024]{1,0:T(8,128)(2,1)}, bf16[136,1024]{1,0:T(8,128)(2,1)S(1)}, u32[]{:S(2)}, u32[]{:S(2)}) collective-permute-start(bf16[136,1024]{1,0:T(8,128)(2,1)} %conv.1), channel_id=1, source_target_pairs={{0,16},{1,17},{2,18},{3,19},{4,20},{5,21},{6,22},{7,23},{8,24},{9,... | collective-permute-start | bytes 835592 | tf_op jit(solution)/shard_map/ppermute | solution.py:155
  41.7 15.2 %collective-permute-start.2 = (bf16[136,1024]{1,0:T(8,128)(2,1)}, bf16[136,1024]{1,0:T(8,128)(2,1)S(1)}, u32[]{:S(2)}, u32[]{:S(2)}) collective-permute-start(bf16[136,1024]{1,0:T(8,128)(2,1)} %conv.1), channel_id=1, source_target_pairs={{0,32},{1,33},{2,34},{3,35},{4,36},{5,37},{6,38},{7,39},{8,40},{9,... | collective-permute-start | bytes 835592 | tf_op jit(solution)/shard_map/ppermute | solution.py:155
  46.6 15.5 %collective-permute-start.3 = (bf16[136,1024]{1,0:T(8,128)(2,1)}, bf16[136,1024]{1,0:T(8,128)(2,1)S(1)}, u32[]{:S(2)}, u32[]{:S(2)}) collective-permute-start(bf16[136,1024]{1,0:T(8,128)(2,1)} %conv.1), channel_id=1, source_target_pairs={{0,48},{1,49},{2,50},{3,51},{4,52},{5,53},{6,54},{7,55},{8,56},{9,... | collective-permute-start | bytes 835592 | tf_op jit(solution)/shard_map/ppermute | solution.py:155
  63.2 4.6 %collective-permute-start.4 = (bf16[544,1024]{1,0:T(8,128)(2,1)S(1)}, bf16[544,1024]{1,0:T(8,128)(2,1)S(1)}, u32[]{:S(2)}, u32[]{:S(2)}) collective-permute-start(bf16[544,1024]{1,0:T(8,128)(2,1)S(1)} %pad_maximum_fusion.1), channel_id=1, source_target_pairs={{0,64},{1,65},{2,66},{3,67},{4,68},{5,69},{6,70},{7,71},{8,72},{9,... | collective-permute-start | bytes 3342344 | tf_op jit(solution)/shard_map/ppermute | solution.py:155
  98.4 16.8 %collective-permute-start.5 = (bf16[136,1024]{1,0:T(8,128)(2,1)S(1)}, bf16[136,1024]{1,0:T(8,128)(2,1)S(1)}, u32[]{:S(2)}, u32[]{:S(2)}) collective-permute-start(bf16[136,1024]{1,0:T(8,128)(2,1)S(1)} %get-tuple-element.9), channel_id=1, source_target_pairs={{0,0},{1,1},{2,2},{3,3},{4,4},{5,5},{6,6},{7,7},{8,8},{9,9},{10,10... | collective-permute-start | bytes 835592 | tf_op jit(solution)/shard_map/ppermute | solution.py:155
  102.9 13.5 %collective-permute-start.6 = (bf16[136,1024]{1,0:T(8,128)(2,1)S(1)}, bf16[136,1024]{1,0:T(8,128)(2,1)S(1)}, u32[]{:S(2)}, u32[]{:S(2)}) collective-permute-start(bf16[136,1024]{1,0:T(8,128)(2,1)S(1)} %get-tuple-element.10), channel_id=1, source_target_pairs={{0,16},{1,17},{2,18},{3,19},{4,20},{5,21},{6,22},{7,23},{8,24},{9,... | collective-permute-start | bytes 835592 | tf_op jit(solution)/shard_map/ppermute | solution.py:155
  108.2 16.0 %collective-permute-start.7 = (bf16[136,1024]{1,0:T(8,128)(2,1)S(1)}, bf16[136,1024]{1,0:T(8,128)(2,1)S(1)}, u32[]{:S(2)}, u32[]{:S(2)}) collective-permute-start(bf16[136,1024]{1,0:T(8,128)(2,1)S(1)} %get-tuple-element.11), channel_id=1, source_target_pairs={{0,32},{1,33},{2,34},{3,35},{4,36},{5,37},{6,38},{7,39},{8,40},{9,... | collective-permute-start | bytes 835592 | tf_op jit(solution)/shard_map/ppermute | solution.py:155
  110.1 14.6 %collective-permute-start.8 = (bf16[136,1024]{1,0:T(8,128)(2,1)S(1)}, bf16[136,1024]{1,0:T(8,128)(2,1)S(1)}, u32[]{:S(2)}, u32[]{:S(2)}) collective-permute-start(bf16[136,1024]{1,0:T(8,128)(2,1)S(1)} %get-tuple-element.12), channel_id=1, source_target_pairs={{0,48},{1,49},{2,50},{3,51},{4,52},{5,53},{6,54},{7,55},{8,56},{9,... | collective-permute-start | bytes 835592 | tf_op jit(solution)/shard_map/ppermute | solution.py:155
Sparse Core Ops, SparseCore 0:
  9.5 83.7 all-gather.2

commit v3 on v2

v3 whole, which is shorter than its diff:
```python
import jax
import jax.numpy as jnp
from jax import lax
from jax.experimental import pallas as pl
from jax.experimental.pallas import tpu as pltpu
from jax.sharding import PartitionSpec as P

TAPS = 128
SHORT = 3
NX, NY, NZ, NC = 4, 4, 16, 2
ROWS = 136
LANES = 128
CONV = 512
WIDE = 512
TILES = ROWS // 8
HALO = 144
ORDER = (0, 3, 1, 2)
ROUND = 60000000
OFFSETS = (0, -1, 1, -2, 2, -3, 3, -4)
BF = jnp.bfloat16
F32 = jnp.float32


def short_rows(ext, taps, i, first, rows):
    summed = taps[i, 0:1, :] * ext[i, first : first + rows, :]
    for lag in range(1, SHORT):
        summed = summed + taps[i, lag : lag + 1, :] * ext[i, first - lag : first - lag + rows, :]
    return summed


def pack_kernel(x_ref, taps_ref, out_ref, ext):
    ext[...] = x_ref[...].astype(F32)
    k = short_rows(ext, taps_ref, 1, 8, 128)
    v = short_rows(ext, taps_ref, 2, 8, 128)
    out_ref[0:128, :] = (k * v).astype(BF)
    row = lax.broadcasted_iota(jnp.int32, (8, WIDE), 0)
    tails = [pltpu.roll(ext[i, ROWS - 8 : ROWS, :], 2 + 2 * i, 0) for i in range(3)]
    tile = jnp.where(row < 2, tails[0], jnp.where(row < 4, tails[1], jnp.where(row < 6, tails[2], 0.0)))
    out_ref[128:144, :] = jnp.concatenate((tile, jnp.zeros((8, WIDE), F32)), 0).astype(BF)


def conv_kernel(x_ref, halo_ref, taps_ref, long_ref, skip_ref, out_ref, ext, prod, filt):
    def lanes(t, carry):
        here = pl.ds(pl.multiple_of(LANES * t, LANES), LANES)
        tails = halo_ref[128:144, here].astype(F32)[0:8]
        for i in range(3):
            ext[i, 0:8, :] = pltpu.roll(tails, 6 - 2 * i, 0)
            ext[i, 8 : 8 + ROWS, :] = x_ref[i, :, here].astype(F32)
        taps = taps_ref[:, :, here]
        k = short_rows(ext, taps, 1, 8, ROWS)
        v = short_rows(ext, taps, 2, 8, ROWS)
        prod[0:128, :] = halo_ref[0:128, here].astype(F32)
        prod[128 : 128 + ROWS, :] = k * v
        filt[...] = long_ref[:, here]
        skip = skip_ref[:, here]
        start = tuple(skip * prod[128 + 8 * m : 136 + 8 * m, :] for m in range(TILES))

        def step(r, acc):
            acc = list(acc)
            weights = [jnp.broadcast_to(filt[pl.ds(8 * a + r, 1), :], (8, LANES)) for a in range(16)]
            for n in range(-15, TILES):
                part = prod[pl.ds(128 + 8 * n - r, 8), :]
                for a in range(16):
                    if 0 <= n + a < TILES:
                        acc[n + a] = acc[n + a] + weights[a] * part
            return tuple(acc)

        acc = lax.fori_loop(0, 8, step, start)
        q = short_rows(ext, taps, 0, 8, ROWS)
        out_ref[:, here] = (q * jnp.concatenate(acc, 0)).astype(BF)
        return carry

    lax.fori_loop(0, CONV // LANES, lanes, 0)


def run_pack(features, short_filter):
    return pl.pallas_call(
        pack_kernel,
        grid=(1024 // WIDE,),
        in_specs=[
            pl.BlockSpec((3, ROWS, WIDE), lambda i: (0, 0, i)),
            pl.BlockSpec((3, SHORT, WIDE), lambda i: (0, 0, i)),
        ],
        out_specs=pl.BlockSpec((HALO, WIDE), lambda i: (0, i)),
        out_shape=jax.ShapeDtypeStruct((HALO, 1024), BF),
        scratch_shapes=[pltpu.VMEM((3, ROWS, WIDE), F32)],
        cost_estimate=pl.CostEstimate(flops=3000000, bytes_accessed=6000000, transcendentals=0),
        name="pack",
    )(features, short_filter)


def run_conv(features, halo, short_filter, long_filter, skip_scale):
    return pl.pallas_call(
        conv_kernel,
        grid=(1024 // CONV,),
        in_specs=[
            pl.BlockSpec((3, ROWS, CONV), lambda i: (0, 0, i)),
            pl.BlockSpec((HALO, CONV), lambda i: (0, i)),
            pl.BlockSpec((3, SHORT, CONV), lambda i: (0, 0, i)),
            pl.BlockSpec((TAPS, CONV), lambda i: (0, i)),
            pl.BlockSpec((1, CONV), lambda i: (0, i)),
        ],
        out_specs=pl.BlockSpec((ROWS, CONV), lambda i: (0, i)),
        out_shape=jax.ShapeDtypeStruct((ROWS, 1024), BF),
        scratch_shapes=[
            pltpu.VMEM((3, 8 + ROWS, LANES), F32),
            pltpu.VMEM((128 + ROWS, LANES), F32),
            pltpu.VMEM((TAPS, LANES), F32),
        ],
        cost_estimate=pl.CostEstimate(flops=36000000, bytes_accessed=20000000, transcendentals=0),
        name="conv",
    )(features, halo, short_filter, long_filter, skip_scale)


def mm_kernel(where_ref, a_ref, *rest):
    w_refs, out_ref = rest[: len(OFFSETS)], rest[len(OFFSETS)]
    rows = a_ref[...]
    for first in range(0, len(OFFSETS), 4):
        w = jnp.concatenate([w_refs[first + i][...] for i in range(4)], axis=1)
        c = jnp.dot(rows, w, preferred_element_type=F32).astype(BF)
        for i in range(4):
            column = pl.multiple_of(128 * ((where_ref[NX] + OFFSETS[first + i]) % 8), 128)
            for s in range(NX):
                out_ref[where_ref[s], :, pl.ds(column, 128)] = c[s * ROWS : (s + 1) * ROWS, 128 * i : 128 * i + 128]


def run_mm(where, a, blocks):
    vmem = pl.BlockSpec(memory_space=pltpu.VMEM)
    return pl.pallas_call(
        mm_kernel,
        in_specs=[pl.BlockSpec(memory_space=pltpu.SMEM)] + [vmem] * (1 + len(OFFSETS)),
        out_specs=vmem,
        out_shape=jax.ShapeDtypeStruct((NX, ROWS, 1024), BF),
        cost_estimate=pl.CostEstimate(flops=1140000000, bytes_accessed=5000000, transcendentals=0),
        compiler_params=pltpu.CompilerParams(vmem_limit_bytes=32 * 1024 * 1024),
        name="mm",
    )(where, a, *blocks)


def pass_kernel(*refs):
    pass


def run_pass(first, second):
    anywhere = pl.BlockSpec(memory_space=pl.ANY)
    return pl.pallas_call(
        pass_kernel,
        in_specs=[anywhere, anywhere],
        out_specs=[anywhere, anywhere],
        out_shape=[jax.ShapeDtypeStruct(first.shape, BF)] * 2,
        input_output_aliases={0: 0, 1: 1},
        cost_estimate=pl.CostEstimate(flops=1000, bytes_accessed=ROUND, transcendentals=0),
        name="hand_on",
    )(first, second)


def join_kernel(late_ref, keep_ref, other_ref, out_ref):
    late = late_ref[0] == 1
    for i in range(4):
        part = slice(128 * i, 128 * i + 128)
        keep, other = keep_ref[:, part], other_ref[:, part]
        out_ref[:, 256 * i : 256 * i + 128] = jnp.where(late, other, keep)
        out_ref[:, 256 * i + 128 : 256 * i + 256] = jnp.where(late, keep, other)


def run_join(late, keep, other):
    vmem = pl.BlockSpec(memory_space=pltpu.VMEM)
    return pl.pallas_call(
        join_kernel,
        in_specs=[pl.BlockSpec(memory_space=pltpu.SMEM), vmem, vmem],
        out_specs=vmem,
        out_shape=jax.ShapeDtypeStruct((ROWS, 1024), BF),
        cost_estimate=pl.CostEstimate(flops=1000, bytes_accessed=600000, transcendentals=0),
        name="join",
    )(late, keep, other)


def permute(block, target):
    pairs = []
    for t in range(NY * NC):
        for i in range(NX * NZ):
            to = target(t // NC, t % NC, i // NZ, i % NZ)
            if to is not None:
                y, c, x, z = to
                pairs.append((t * NX * NZ + i, (y * NC + c) * NX * NZ + x * NZ + z))
    return lax.ppermute(block, ("tp", "cp"), pairs)


def local(features, short_filter, long_filter, skip_scale, out_weight):
    tp, cp = lax.axis_index("tp"), lax.axis_index("cp")
    y, core, z = tp // NC, tp % NC, cp % NZ

    blocks = [out_weight]
    behind = ahead = out_weight
    for r in range(1, 5):
        behind = permute(behind, lambda y, c, x, z: (y, c, x, (z + 2) % NZ))
        if r < 4:
            ahead = permute(ahead, lambda y, c, x, z: (y, c, x, (z - 2) % NZ))
            behind, ahead = run_pass(behind, ahead)
            blocks += [behind, ahead]
    blocks.append(behind)

    packed = run_pack(features, short_filter)
    halo = lax.ppermute(packed, "cp", [(i, i + 1) for i in range(NX * NZ - 1)])
    gated = run_conv(features, halo, short_filter, long_filter, skip_scale[None, :])

    across = permute(gated, lambda y, c, x, z: (y, c, x, z ^ 1))

    def from_x(block):
        others = [
            permute(block, lambda y, c, x, z, i=i: (y, c, x ^ (ORDER[i] if c else i), z)) for i in range(1, NX)
        ]
        return jnp.concatenate([block] + others, axis=0)

    core, y = core.astype(jnp.int32), y.astype(jnp.int32)
    sources = jnp.where(core == 1, jnp.array(ORDER, jnp.int32), jnp.arange(NX, dtype=jnp.int32)) ^ y
    column = (z // 2).astype(jnp.int32)[None]
    near = run_mm(jnp.concatenate((sources, column)), from_x(gated), blocks)
    far = run_mm(jnp.concatenate((sources ^ 2, column)), from_x(across), blocks)

    away = permute(jnp.where(core == 0, far, near), lambda y, c, x, z: (y, 1 - c, x, z))
    keep = jnp.where(core == 0, near, far)
    got = []
    for m in range(NX):
        piece = (keep[m].astype(F32) + away[m].astype(F32)).astype(BF)
        got.append(permute(piece, lambda y, c, x, z, m=m: (x, c, x ^ y ^ m ^ (2 * c), z ^ c)))

    def half(start):
        part = [lax.dynamic_slice_in_dim(g, start, 512, 1).astype(F32) for g in got]
        return ((part[0] + part[1]) + (part[2] + part[3])).astype(BF)

    away = half(512 * (1 - core))
    other = permute(away, lambda y, c, x, z: (y, 1 - c, x, z))
    keep = half(512 * core)
    late = (z % 2) ^ core
    return run_join(late.astype(jnp.int32)[None], keep, other)


def solution(mesh):
    return jax.shard_map(
        local,
        mesh=mesh,
        in_specs=(P(None, "cp", "tp"), P(None, None, "tp"), P(None, "tp"), P("tp"), P("tp", "cp")),
        out_specs=P("cp", "tp"),
        check_vma=False,
    )
```

time: 133 us -> 132 us (level)
  starting transfers between devices: 41.1 us -> 82.2 us
  waiting for transfers between devices: 57.7 us -> 27.1 us
  between operations: 13.5 us -> 0.52 us
  local copies, waits for them, and re-layouts: 0.72 us -> 3.54 us
    ppermute x8 -> x20, starting transfers between devices: 37.3 us -> 79.3 us  [permute(): return lax.ppermute(block, ('tp', 'cp'), pairs)]
    all_gather x1 -> x0, waiting for transfers between devices: 24.7 us -> none  [local(): lax.all_gather(out_weight, ('tp', 'cp'), axis=0, axis_index_groups=groups)]
    ppermute x1, waiting for transfers between devices: 6.55 us -> 0.01 us  [local(): halo = lax.ppermute(packed, 'cp', [(i, i + 1) for i in range(NX * NZ - 1)])]
    unnamed x4 -> x34, local copies, waits for them, and re-layouts: 0.72 us -> 3.54 us
    ppermute x8 -> x20, waiting for transfers between devices: 25.7 us -> 27.1 us  [permute(): return lax.ppermute(block, ('tp', 'cp'), pairs)]
    pallas_call x1 -> x5, Pallas kernels: 8.18 us -> 9.41 us  [the longest x1 7.68 us: run_conv(): pl.pallas_call(conv_kernel, grid=(1024 // CONV,), in_specs=[pl.BlockSpec(...]
    pallas_call x1 -> x2, Pallas kernels: 5.09 us -> 4.16 us  [run_mm(): pl.pallas_call(mm_kernel, in_specs=[pl.BlockSpec(memory_space=pltpu.SMEM)...]
  transfers between devices with their start and end apart: 10 -> 21, of which waited for: 9 -> 10; matrix products, arithmetic and copies ran while one was open for 1% -> 0% of each run, Pallas kernels for 9% -> 8%
where the time goes in v3:
time: 132 us; the launch traced here: 131 us
  starting transfers between devices  82.2 us (62%)
  waiting for transfers between devices  27.1 us (21%)
  Pallas kernels  15.9 us (12%)
  local copies, waits for them, and re-layouts  3.54 us (3%)
  other arithmetic  1.69 us (1%)
    ppermute x20, starting transfers between devices, permute(): return lax.ppermute(block, ('tp', 'cp'), pairs)  79.3 us
    ppermute x20, waiting for transfers between devices, permute(): return lax.ppermute(block, ('tp', 'cp'), pairs)  27.1 us
    pallas_call x1, Pallas kernels, run_conv(): pl.pallas_call(conv_kernel, grid=(1024 // CONV,), in_specs=[pl.BlockSpec(...  7.68 us
    pallas_call x2, Pallas kernels, run_mm(): pl.pallas_call(mm_kernel, in_specs=[pl.BlockSpec(memory_space=pltpu.SMEM)...  4.16 us
    unnamed x34, local copies, waits for them, and re-layouts  3.54 us
    ppermute x1, starting transfers between devices, local(): halo = lax.ppermute(packed, 'cp', [(i, i + 1) for i in range(NX * NZ - 1)])  2.93 us
  transfers between devices with their start and end apart: 21, of which 10 were waited for; matrix products, arithmetic and copies ran while one was open for 0% of the time, Pallas kernels for 8%

profile of v3, /device:TPU:24, one launch (start us, length us, event | category | flops | bytes accessed | tf_op | source)
XLA Modules:
  0.0 131.0 jit_solution(17440628613861875206)
XLA Ops:
  0.0 5.2 %collective-permute-start.4 = (bf16[1024,128]{1,0:T(8,128)(2,1)}, bf16[1024,128]{1,0:T(8,128)(2,1)S(1)}, u32[]{:S(2)}, u32[]{:S(2)}) collective-permute-start(bf16[1024,128]{1,0:T(8,128)(2,1)} %rest_0_.3), channel_id=1, source_target_pairs={{0,2},{1,3},{2,4},{3,5},{4,6},{5,7},{6,8},{7,9},{8,10},{9,11},{10,... | collective-permute-start | bytes 786440 | tf_op jit(solution)/shard_map/ppermute | solution.py:186
  5.2 8.6 %collective-permute-start.5 = (bf16[1024,128]{1,0:T(8,128)(2,1)}, bf16[1024,128]{1,0:T(8,128)(2,1)S(1)}, u32[]{:S(2)}, u32[]{:S(2)}) collective-permute-start(bf16[1024,128]{1,0:T(8,128)(2,1)} %rest_0_.3), channel_id=1, source_target_pairs={{0,14},{1,15},{2,0},{3,1},{4,2},{5,3},{6,4},{7,5},{8,6},{9,7},{10,... | collective-permute-start | bytes 786440 | tf_op jit(solution)/shard_map/ppermute | solution.py:186
  13.8 2.3 %pack.1 = bf16[144,1024]{1,0:T(8,128)(2,1)} custom-call(bf16[3,136,1024]{2,1,0:T(8,128)(2,1)} %x_ref.3, f32[3,3,1024]{2,1,0:T(4,128)} %taps_ref.3), custom_call_target="tpu_custom_call" | custom-call | flops 3000000 | bytes 6000000 | tf_op jit(solution)/shard_map/pack/pallas_call | solution.py:77
  16.1 2.9 %collective-permute-start = (bf16[144,1024]{1,0:T(8,128)(2,1)}, bf16[144,1024]{1,0:T(8,128)(2,1)S(1)}, u32[]{:S(2)}, u32[]{:S(2)}) collective-permute-start(bf16[144,1024]{1,0:T(8,128)(2,1)} %pack.1), channel_id=1, source_target_pairs={{0,1},{1,2},{2,3},{3,4},{4,5},{5,6},{6,7},{7,8},{8,9},{9,10},{10,1... | collective-permute-start | bytes 884744 | tf_op jit(solution)/shard_map/ppermute | solution.py:204
  19.0 1.6 %collective-permute-done.4.refs_0_ = bf16[1024,128]{1,0:T(8,128)(2,1)S(1)} collective-permute-done((bf16[1024,128]{1,0:T(8,128)(2,1)}, bf16[1024,128]{1,0:T(8,128)(2,1)S(1)}, u32[]{:S(2)}, u32[]{:S(2)}) %collective-permute-start.4) | collective-permute-done | bytes 262176 | tf_op jit(solution)/shard_map/ppermute | solution.py:186
  20.6 4.7 %collective-permute-done.5.refs_1_ = bf16[1024,128]{1,0:T(8,128)(2,1)S(1)} collective-permute-done((bf16[1024,128]{1,0:T(8,128)(2,1)}, bf16[1024,128]{1,0:T(8,128)(2,1)S(1)}, u32[]{:S(2)}, u32[]{:S(2)}) %collective-permute-start.5) | collective-permute-done | bytes 262176 | tf_op jit(solution)/shard_map/ppermute | solution.py:186
  25.3 0.7 copy-done.10
  26.0 3.9 %collective-permute-start.6 = (bf16[1024,128]{1,0:T(8,128)(2,1)}, bf16[1024,128]{1,0:T(8,128)(2,1)S(1)}, u32[]{:S(2)}, u32[]{:S(2)}) collective-permute-start(bf16[1024,128]{1,0:T(8,128)(2,1)} %get-tuple-element.11.rest_1_), channel_id=1, source_target_pairs={{0,2},{1,3},{2,4},{3,5},{4,6},{5,7},{6,8},{7,9},{8,10},{9,11},{10,... | collective-permute-start | bytes 786440 | tf_op jit(solution)/shard_map/ppermute | solution.py:186
  29.9 4.4 %collective-permute-start.7 = (bf16[1024,128]{1,0:T(8,128)(2,1)}, bf16[1024,128]{1,0:T(8,128)(2,1)S(1)}, u32[]{:S(2)}, u32[]{:S(2)}) collective-permute-start(bf16[1024,128]{1,0:T(8,128)(2,1)} %get-tuple-element.12.rest_2_), channel_id=1, source_target_pairs={{0,14},{1,15},{2,0},{3,1},{4,2},{5,3},{6,4},{7,5},{8,6},{9,7},{10,... | collective-permute-start | bytes 786440 | tf_op jit(solution)/shard_map/ppermute | solution.py:186
  34.3 0.7 copy-done.14
  35.0 7.7 %conv.1 = bf16[136,1024]{1,0:T(8,128)(2,1)} custom-call(bf16[3,136,1024]{2,1,0:T(8,128)(2,1)} %x_ref.3, bf16[144,1024]{1,0:T(8,128)(2,1)} %copy-done.14, f32[3,3,1024]{2,1,0:T(4,128)} %taps_ref.3, f32[128,1024]{1,0:T(8,128)} %long_ref.1, f32[1,1024]{1,0:T(1,128)} %bitcast.11), custom_call_target="tpu_custom_call" | custom-call | flops 36000000 | bytes 20000000 | tf_op jit(solution)/shard_map/conv/pallas_call | solution.py:93
  42.7 4.8 %collective-permute-start.3 = (bf16[136,1024]{1,0:T(8,128)(2,1)}, bf16[136,1024]{1,0:T(8,128)(2,1)S(1)}, u32[]{:S(2)}, u32[]{:S(2)}) collective-permute-start(bf16[136,1024]{1,0:T(8,128)(2,1)} %conv.1), channel_id=1, source_target_pairs={{0,48},{1,49},{2,50},{3,51},{4,52},{5,53},{6,54},{7,55},{8,56},{9,... | collective-permute-start | bytes 835592 | tf_op jit(solution)/shard_map/ppermute | solution.py:186
  47.5 2.0 %collective-permute-start.11 = (bf16[136,1024]{1,0:T(8,128)(2,1)}, bf16[136,1024]{1,0:T(8,128)(2,1)S(1)}, u32[]{:S(2)}, u32[]{:S(2)}) collective-permute-start(bf16[136,1024]{1,0:T(8,128)(2,1)} %conv.1), channel_id=1, source_target_pairs={{0,1},{1,0},{2,3},{3,2},{4,5},{5,4},{6,7},{7,6},{8,9},{9,8},{10,11... | collective-permute-start | bytes 835592 | tf_op jit(solution)/shard_map/ppermute | solution.py:186
  49.6 0.7 copy-done.4
  50.3 0.7 copy-done.6
  51.0 3.2 %collective-permute-start.8 = (bf16[1024,128]{1,0:T(8,128)(2,1)}, bf16[1024,128]{1,0:T(8,128)(2,1)S(1)}, u32[]{:S(2)}, u32[]{:S(2)}) collective-permute-start(bf16[1024,128]{1,0:T(8,128)(2,1)} %get-tuple-element.13.rest_3_), channel_id=1, source_target_pairs={{0,2},{1,3},{2,4},{3,5},{4,6},{5,7},{6,8},{7,9},{8,10},{9,11},{10,... | collective-permute-start | bytes 786440 | tf_op jit(solution)/shard_map/ppermute | solution.py:186
  54.2 4.7 %collective-permute-start.9 = (bf16[1024,128]{1,0:T(8,128)(2,1)}, bf16[1024,128]{1,0:T(8,128)(2,1)S(1)}, u32[]{:S(2)}, u32[]{:S(2)}) collective-permute-start(bf16[1024,128]{1,0:T(8,128)(2,1)} %get-tuple-element.14.rest_4_), channel_id=1, source_target_pairs={{0,14},{1,15},{2,0},{3,1},{4,2},{5,3},{6,4},{7,5},{8,6},{9,7},{10,... | collective-permute-start | bytes 786440 | tf_op jit(solution)/shard_map/ppermute | solution.py:186
  59.0 3.2 %collective-permute-start.2 = (bf16[136,1024]{1,0:T(8,128)(2,1)}, bf16[136,1024]{1,0:T(8,128)(2,1)S(1)}, u32[]{:S(2)}, u32[]{:S(2)}) collective-permute-start(bf16[136,1024]{1,0:T(8,128)(2,1)} %conv.1), channel_id=1, source_target_pairs={{0,32},{1,33},{2,34},{3,35},{4,36},{5,37},{6,38},{7,39},{8,40},{9,... | collective-permute-start | bytes 835592 | tf_op jit(solution)/shard_map/ppermute | solution.py:186
  62.1 2.4 %collective-permute-start.1 = (bf16[136,1024]{1,0:T(8,128)(2,1)}, bf16[136,1024]{1,0:T(8,128)(2,1)S(1)}, u32[]{:S(2)}, u32[]{:S(2)}) collective-permute-start(bf16[136,1024]{1,0:T(8,128)(2,1)} %conv.1), channel_id=1, source_target_pairs={{0,16},{1,17},{2,18},{3,19},{4,20},{5,21},{6,22},{7,23},{8,24},{9,... | collective-permute-start | bytes 835592 | tf_op jit(solution)/shard_map/ppermute | solution.py:186
  64.6 4.2 %collective-permute-start.14 = (bf16[136,1024]{1,0:T(8,128)(2,1)S(1)}, bf16[136,1024]{1,0:T(8,128)(2,1)S(1)}, u32[]{:S(2)}, u32[]{:S(2)}) collective-permute-start(bf16[136,1024]{1,0:T(8,128)(2,1)S(1)} %collective-permute-done.11), channel_id=1, source_target_pairs={{0,48},{1,49},{2,50},{3,51},{4,52},{5,53},{6,54},{7,55},{8,56},{9,... | collective-permute-start | bytes 835592 | tf_op jit(solution)/shard_map/ppermute | solution.py:186
  68.8 0.5 collective-permute-done.8.refs_0_
  69.3 2.7 %collective-permute-start.13 = (bf16[136,1024]{1,0:T(8,128)(2,1)S(1)}, bf16[136,1024]{1,0:T(8,128)(2,1)S(1)}, u32[]{:S(2)}, u32[]{:S(2)}) collective-permute-start(bf16[136,1024]{1,0:T(8,128)(2,1)S(1)} %collective-permute-done.11), channel_id=1, source_target_pairs={{0,32},{1,33},{2,34},{3,35},{4,36},{5,37},{6,38},{7,39},{8,40},{9,... | collective-permute-start | bytes 835592 | tf_op jit(solution)/shard_map/ppermute | solution.py:186
  72.0 3.1 %collective-permute-start.12 = (bf16[136,1024]{1,0:T(8,128)(2,1)S(1)}, bf16[136,1024]{1,0:T(8,128)(2,1)S(1)}, u32[]{:S(2)}, u32[]{:S(2)}) collective-permute-start(bf16[136,1024]{1,0:T(8,128)(2,1)S(1)} %collective-permute-done.11), channel_id=1, source_target_pairs={{0,16},{1,17},{2,18},{3,19},{4,20},{5,21},{6,22},{7,23},{8,24},{9,... | collective-permute-start | bytes 835592 | tf_op jit(solution)/shard_map/ppermute | solution.py:186
  75.2 0.1 pad_add_fusion
  75.3 2.4 %collective-permute-start.10 = (bf16[1024,128]{1,0:T(8,128)(2,1)}, bf16[1024,128]{1,0:T(8,128)(2,1)S(1)}, u32[]{:S(2)}, u32[]{:S(2)}) collective-permute-start(bf16[1024,128]{1,0:T(8,128)(2,1)} %get-tuple-element.15.rest_5_), channel_id=1, source_target_pairs={{0,2},{1,3},{2,4},{3,5},{4,6},{5,7},{6,8},{7,9},{8,10},{9,11},{10,... | collective-permute-start | bytes 786440 | tf_op jit(solution)/shard_map/ppermute | solution.py:186
  77.7 0.1 pad_maximum_fusion.a_ref
  77.8 0.0 copy-start.12
  77.8 3.8 %collective-permute-done.14 = bf16[136,1024]{1,0:T(8,128)(2,1)S(1)} collective-permute-done((bf16[136,1024]{1,0:T(8,128)(2,1)S(1)}, bf16[136,1024]{1,0:T(8,128)(2,1)S(1)}, u32[]{:S(2)}, u32[]{:S(2)}) %collective-permute-start.14) | collective-permute-done | bytes 278560 | tf_op jit(solution)/shard_map/ppermute | solution.py:186
  81.7 1.2 collective-permute-done.12
  82.9 0.1 pad_maximum_fusion.1.a_ref
  83.0 5.6 %collective-permute-done.10.rest_7_ = bf16[1024,128]{1,0:T(8,128)(2,1)S(1)} collective-permute-done((bf16[1024,128]{1,0:T(8,128)(2,1)}, bf16[1024,128]{1,0:T(8,128)(2,1)S(1)}, u32[]{:S(2)}, u32[]{:S(2)}) %collective-permute-start.10) | collective-permute-done | bytes 262176 | tf_op jit(solution)/shard_map/ppermute | solution.py:186
  88.6 2.1 %mm.2 = bf16[4,136,1024]{2,1,0:T(8,128)(2,1)S(1)} custom-call(s32[5]{0:T(128)S(1)} %get-tuple-element.27.where_ref, bf16[544,1024]{1,0:T(8,128)(2,1)S(1)} %pad_maximum_fusion.a_ref, bf16[1024,128]{1,0:T(8,128)(2,1)S(1)} %copy-done.12, bf16[1024,128]{1,0:T(8,128)(2,1)S(1)} %copy-done.9, bf16[1024,128]{1,0:T(8,128)(2,1)S(1)} %copy-done.11, ...), custom_call_target="tpu_custom_call" | custom-call | flops 1140000000 | bytes 5000000 | tf_op jit(solution)/shard_map/mm/pallas_call | solution.py:129
  90.7 2.1 %mm.3 = bf16[4,136,1024]{2,1,0:T(8,128)(2,1)S(1)} custom-call(s32[5]{0:T(128)S(1)} %get-tuple-element.28.where_ref, bf16[544,1024]{1,0:T(8,128)(2,1)S(1)} %pad_maximum_fusion.1.a_ref, bf16[1024,128]{1,0:T(8,128)(2,1)S(1)} %copy-done.12, bf16[1024,128]{1,0:T(8,128)(2,1)S(1)} %copy-done.9, bf16[1024,128]{1,0:T(8,128)(2,1)S(1)} %copy-done.11, ...), custom_call_target="tpu_custom_call" | custom-call | flops 1140000000 | bytes 5000000 | tf_op jit(solution)/shard_map/mm/pallas_call | solution.py:129
  92.8 0.2 broadcast_select_fusion.1
  92.9 1.9 %collective-permute-start.15 = (bf16[4,136,1024]{2,1,0:T(8,128)(2,1)S(1)}, bf16[4,136,1024]{2,1,0:T(8,128)(2,1)S(1)}, u32[]{:S(2)}, u32[]{:S(2)}) collective-permute-start(bf16[4,136,1024]{2,1,0:T(8,128)(2,1)S(1)} %get-tuple-element.24), channel_id=1, source_target_pairs={{0,64},{1,65},{2,66},{3,67},{4,68},{5,69},{6,70},{7,71},{8,72},{9,... | collective-permute-start | bytes 3342344 | tf_op jit(solution)/shard_map/ppermute | solution.py:186
  94.9 2.7 %collective-permute-done.15 = bf16[4,136,1024]{2,1,0:T(8,128)(2,1)S(1)} collective-permute-done((bf16[4,136,1024]{2,1,0:T(8,128)(2,1)S(1)}, bf16[4,136,1024]{2,1,0:T(8,128)(2,1)S(1)}, u32[]{:S(2)}, u32[]{:S(2)}) %collective-permute-start.15) | collective-permute-done | bytes 1114144 | tf_op jit(solution)/shard_map/ppermute | solution.py:186
  97.6 0.4 fusion
  98.0 2.1 %collective-permute-start.19 = (bf16[136,1024]{1,0:T(8,128)(2,1)S(1)}, bf16[136,1024]{1,0:T(8,128)(2,1)S(1)}, u32[]{:S(2)}, u32[]{:S(2)}) collective-permute-start(bf16[136,1024]{1,0:T(8,128)(2,1)S(1)} %get-tuple-element.20), channel_id=1, source_target_pairs={{0,48},{1,49},{2,50},{3,51},{4,52},{5,53},{6,54},{7,55},{8,56},{9,... | collective-permute-start | bytes 835592 | tf_op jit(solution)/shard_map/ppermute | solution.py:186
  100.2 7.1 %collective-permute-start.18 = (bf16[136,1024]{1,0:T(8,128)(2,1)S(1)}, bf16[136,1024]{1,0:T(8,128)(2,1)S(1)}, u32[]{:S(2)}, u32[]{:S(2)}) collective-permute-start(bf16[136,1024]{1,0:T(8,128)(2,1)S(1)} %get-tuple-element.21), channel_id=1, source_target_pairs={{0,32},{1,33},{2,34},{3,35},{4,36},{5,37},{6,38},{7,39},{8,40},{9,... | collective-permute-start | bytes 835592 | tf_op jit(solution)/shard_map/ppermute | solution.py:186
  107.2 5.2 %collective-permute-start.17 = (bf16[136,1024]{1,0:T(8,128)(2,1)S(1)}, bf16[136,1024]{1,0:T(8,128)(2,1)S(1)}, u32[]{:S(2)}, u32[]{:S(2)}) collective-permute-start(bf16[136,1024]{1,0:T(8,128)(2,1)S(1)} %get-tuple-element.22), channel_id=1, source_target_pairs={{0,16},{1,17},{2,18},{3,19},{4,20},{5,21},{6,22},{7,23},{8,24},{9,... | collective-permute-start | bytes 835592 | tf_op jit(solution)/shard_map/ppermute | solution.py:186
  112.4 3.6 %collective-permute-start.16 = (bf16[136,1024]{1,0:T(8,128)(2,1)S(1)}, bf16[136,1024]{1,0:T(8,128)(2,1)S(1)}, u32[]{:S(2)}, u32[]{:S(2)}) collective-permute-start(bf16[136,1024]{1,0:T(8,128)(2,1)S(1)} %get-tuple-element.19), channel_id=1, source_target_pairs={{0,0},{1,1},{2,2},{3,3},{4,4},{5,5},{6,6},{7,7},{8,8},{9,9},{10,10... | collective-permute-start | bytes 835592 | tf_op jit(solution)/shard_map/ppermute | solution.py:186
  116.0 1.7 %collective-permute-done.17 = bf16[136,1024]{1,0:T(8,128)(2,1)S(1)} collective-permute-done((bf16[136,1024]{1,0:T(8,128)(2,1)S(1)}, bf16[136,1024]{1,0:T(8,128)(2,1)S(1)}, u32[]{:S(2)}, u32[]{:S(2)}) %collective-permute-start.17) | collective-permute-done | bytes 278560 | tf_op jit(solution)/shard_map/ppermute | solution.py:186
  117.8 4.3 %collective-permute-done.16 = bf16[136,1024]{1,0:T(8,128)(2,1)S(1)} collective-permute-done((bf16[136,1024]{1,0:T(8,128)(2,1)S(1)}, bf16[136,1024]{1,0:T(8,128)(2,1)S(1)}, u32[]{:S(2)}, u32[]{:S(2)}) %collective-permute-start.16) | collective-permute-done | bytes 278560 | tf_op jit(solution)/shard_map/ppermute | solution.py:186
  122.1 0.9 add_convert_fusion.4
  123.0 4.6 %collective-permute-start.20 = (bf16[136,512]{1,0:T(8,128)(2,1)S(1)}, bf16[136,512]{1,0:T(8,128)(2,1)S(1)}, u32[]{:S(2)}, u32[]{:S(2)}) collective-permute-start(bf16[136,512]{1,0:T(8,128)(2,1)S(1)} %get-tuple-element.25), channel_id=1, source_target_pairs={{0,64},{1,65},{2,66},{3,67},{4,68},{5,69},{6,70},{7,71},{8,72},{9,... | collective-permute-start | bytes 417800 | tf_op jit(solution)/shard_map/ppermute | solution.py:186
  127.6 1.0 collective-permute-done.20.other_ref
  128.6 0.7 copy-done.15
  129.2 1.7 %join.1 = bf16[136,1024]{1,0:T(8,128)(2,1)} custom-call(s32[1]{0:T(128)} %bitcast.late_ref, bf16[136,512]{1,0:T(8,128)(2,1)} %get-tuple-element.26.keep_ref, bf16[136,512]{1,0:T(8,128)(2,1)} %copy-done.15), custom_call_target="tpu_custom_call" | custom-call | flops 1000 | bytes 600000 | tf_op jit(solution)/shard_map/join/pallas_call | solution.py:168
  (43 shorter events, 0.1 us)
Async XLA Ops:
  0.0 20.6 %collective-permute-start.4 = (bf16[1024,128]{1,0:T(8,128)(2,1)}, bf16[1024,128]{1,0:T(8,128)(2,1)S(1)}, u32[]{:S(2)}, u32[]{:S(2)}) collective-permute-start(bf16[1024,128]{1,0:T(8,128)(2,1)} %rest_0_.3), channel_id=1, source_target_pairs={{0,2},{1,3},{2,4},{3,5},{4,6},{5,7},{6,8},{7,9},{8,10},{9,11},{10,... | collective-permute-start | bytes 786440 | tf_op jit(solution)/shard_map/ppermute | solution.py:186
  5.2 20.1 %collective-permute-start.5 = (bf16[1024,128]{1,0:T(8,128)(2,1)}, bf16[1024,128]{1,0:T(8,128)(2,1)S(1)}, u32[]{:S(2)}, u32[]{:S(2)}) collective-permute-start(bf16[1024,128]{1,0:T(8,128)(2,1)} %rest_0_.3), channel_id=1, source_target_pairs={{0,14},{1,15},{2,0},{3,1},{4,2},{5,3},{6,4},{7,5},{8,6},{9,7},{10,... | collective-permute-start | bytes 786440 | tf_op jit(solution)/shard_map/ppermute | solution.py:186
  16.1 18.2 %collective-permute-start = (bf16[144,1024]{1,0:T(8,128)(2,1)}, bf16[144,1024]{1,0:T(8,128)(2,1)S(1)}, u32[]{:S(2)}, u32[]{:S(2)}) collective-permute-start(bf16[144,1024]{1,0:T(8,128)(2,1)} %pack.1), channel_id=1, source_target_pairs={{0,1},{1,2},{2,3},{3,4},{4,5},{5,6},{6,7},{7,8},{8,9},{9,10},{10,1... | collective-permute-start | bytes 884744 | tf_op jit(solution)/shard_map/ppermute | solution.py:204
  20.6 4.7 %copy-start.8 = (bf16[1024,128]{1,0:T(8,128)(2,1)}, bf16[1024,128]{1,0:T(8,128)(2,1)S(1)}, u32[]{:S(2)}) copy-start(bf16[1024,128]{1,0:T(8,128)(2,1)S(1)} %collective-permute-done.4.refs_0_) | copy-start | bytes 786436
  25.3 0.7 copy-start.10
  26.0 23.6 %collective-permute-start.6 = (bf16[1024,128]{1,0:T(8,128)(2,1)}, bf16[1024,128]{1,0:T(8,128)(2,1)S(1)}, u32[]{:S(2)}, u32[]{:S(2)}) collective-permute-start(bf16[1024,128]{1,0:T(8,128)(2,1)} %get-tuple-element.11.rest_1_), channel_id=1, source_target_pairs={{0,2},{1,3},{2,4},{3,5},{4,6},{5,7},{6,8},{7,9},{8,10},{9,11},{10,... | collective-permute-start | bytes 786440 | tf_op jit(solution)/shard_map/ppermute | solution.py:186
  29.9 19.7 %collective-permute-start.7 = (bf16[1024,128]{1,0:T(8,128)(2,1)}, bf16[1024,128]{1,0:T(8,128)(2,1)S(1)}, u32[]{:S(2)}, u32[]{:S(2)}) collective-permute-start(bf16[1024,128]{1,0:T(8,128)(2,1)} %get-tuple-element.12.rest_2_), channel_id=1, source_target_pairs={{0,14},{1,15},{2,0},{3,1},{4,2},{5,3},{6,4},{7,5},{8,6},{9,7},{10,... | collective-permute-start | bytes 786440 | tf_op jit(solution)/shard_map/ppermute | solution.py:186
  34.3 0.7 copy-start.14
  35.0 40.1 %copy-start.16 = (s32[4]{0:T(128)S(1)}, s32[4]{0:T(128)}, u32[]{:S(2)}) copy-start(s32[4]{0:T(128)} %constant.63.clone) | copy-start | bytes 52
  42.7 35.0 %copy-start.13 = (bf16[136,1024]{1,0:T(8,128)(2,1)S(1)}, bf16[136,1024]{1,0:T(8,128)(2,1)}, u32[]{:S(2)}) copy-start(bf16[136,1024]{1,0:T(8,128)(2,1)} %conv.1) | copy-start | bytes 835588
  42.7 19.4 %collective-permute-start.3 = (bf16[136,1024]{1,0:T(8,128)(2,1)}, bf16[136,1024]{1,0:T(8,128)(2,1)S(1)}, u32[]{:S(2)}, u32[]{:S(2)}) collective-permute-start(bf16[136,1024]{1,0:T(8,128)(2,1)} %conv.1), channel_id=1, source_target_pairs={{0,48},{1,49},{2,50},{3,51},{4,52},{5,53},{6,54},{7,55},{8,56},{9,... | collective-permute-start | bytes 835592 | tf_op jit(solution)/shard_map/ppermute | solution.py:186
  47.5 17.1 %collective-permute-start.11 = (bf16[136,1024]{1,0:T(8,128)(2,1)}, bf16[136,1024]{1,0:T(8,128)(2,1)S(1)}, u32[]{:S(2)}, u32[]{:S(2)}) collective-permute-start(bf16[136,1024]{1,0:T(8,128)(2,1)} %conv.1), channel_id=1, source_target_pairs={{0,1},{1,0},{2,3},{3,2},{4,5},{5,4},{6,7},{7,6},{8,9},{9,8},{10,11... | collective-permute-start | bytes 835592 | tf_op jit(solution)/shard_map/ppermute | solution.py:186
  49.5 0.7 copy-start.4
  50.3 0.7 copy-start.6
  51.0 18.3 %collective-permute-start.8 = (bf16[1024,128]{1,0:T(8,128)(2,1)}, bf16[1024,128]{1,0:T(8,128)(2,1)S(1)}, u32[]{:S(2)}, u32[]{:S(2)}) collective-permute-start(bf16[1024,128]{1,0:T(8,128)(2,1)} %get-tuple-element.13.rest_3_), channel_id=1, source_target_pairs={{0,2},{1,3},{2,4},{3,5},{4,6},{5,7},{6,8},{7,9},{8,10},{9,11},{10,... | collective-permute-start | bytes 786440 | tf_op jit(solution)/shard_map/ppermute | solution.py:186
  54.2 17.8 %collective-permute-start.9 = (bf16[1024,128]{1,0:T(8,128)(2,1)}, bf16[1024,128]{1,0:T(8,128)(2,1)S(1)}, u32[]{:S(2)}, u32[]{:S(2)}) collective-permute-start(bf16[1024,128]{1,0:T(8,128)(2,1)} %get-tuple-element.14.rest_4_), channel_id=1, source_target_pairs={{0,14},{1,15},{2,0},{3,1},{4,2},{5,3},{6,4},{7,5},{8,6},{9,7},{10,... | collective-permute-start | bytes 786440 | tf_op jit(solution)/shard_map/ppermute | solution.py:186
  59.0 16.3 %collective-permute-start.2 = (bf16[136,1024]{1,0:T(8,128)(2,1)}, bf16[136,1024]{1,0:T(8,128)(2,1)S(1)}, u32[]{:S(2)}, u32[]{:S(2)}) collective-permute-start(bf16[136,1024]{1,0:T(8,128)(2,1)} %conv.1), channel_id=1, source_target_pairs={{0,32},{1,33},{2,34},{3,35},{4,36},{5,37},{6,38},{7,39},{8,40},{9,... | collective-permute-start | bytes 835592 | tf_op jit(solution)/shard_map/ppermute | solution.py:186
  62.1 15.5 %collective-permute-start.1 = (bf16[136,1024]{1,0:T(8,128)(2,1)}, bf16[136,1024]{1,0:T(8,128)(2,1)S(1)}, u32[]{:S(2)}, u32[]{:S(2)}) collective-permute-start(bf16[136,1024]{1,0:T(8,128)(2,1)} %conv.1), channel_id=1, source_target_pairs={{0,16},{1,17},{2,18},{3,19},{4,20},{5,21},{6,22},{7,23},{8,24},{9,... | collective-permute-start | bytes 835592 | tf_op jit(solution)/shard_map/ppermute | solution.py:186
  64.6 17.1 %collective-permute-start.14 = (bf16[136,1024]{1,0:T(8,128)(2,1)S(1)}, bf16[136,1024]{1,0:T(8,128)(2,1)S(1)}, u32[]{:S(2)}, u32[]{:S(2)}) collective-permute-start(bf16[136,1024]{1,0:T(8,128)(2,1)S(1)} %collective-permute-done.11), channel_id=1, source_target_pairs={{0,48},{1,49},{2,50},{3,51},{4,52},{5,53},{6,54},{7,55},{8,56},{9,... | collective-permute-start | bytes 835592 | tf_op jit(solution)/shard_map/ppermute | solution.py:186
  69.3 6.0 %copy-start = (bf16[1024,128]{1,0:T(8,128)(2,1)}, bf16[1024,128]{1,0:T(8,128)(2,1)S(1)}, u32[]{:S(2)}) copy-start(bf16[1024,128]{1,0:T(8,128)(2,1)S(1)} %collective-permute-done.8.refs_0_) | copy-start | bytes 786436
  69.3 12.4 %collective-permute-start.13 = (bf16[136,1024]{1,0:T(8,128)(2,1)S(1)}, bf16[136,1024]{1,0:T(8,128)(2,1)S(1)}, u32[]{:S(2)}, u32[]{:S(2)}) collective-permute-start(bf16[136,1024]{1,0:T(8,128)(2,1)S(1)} %collective-permute-done.11), channel_id=1, source_target_pairs={{0,32},{1,33},{2,34},{3,35},{4,36},{5,37},{6,38},{7,39},{8,40},{9,... | collective-permute-start | bytes 835592 | tf_op jit(solution)/shard_map/ppermute | solution.py:186
  72.0 3.2 %copy-start.2 = (bf16[1024,128]{1,0:T(8,128)(2,1)}, bf16[1024,128]{1,0:T(8,128)(2,1)S(1)}, u32[]{:S(2)}) copy-start(bf16[1024,128]{1,0:T(8,128)(2,1)S(1)} %collective-permute-done.9.refs_1_) | copy-start | bytes 786436
  72.0 10.9 %collective-permute-start.12 = (bf16[136,1024]{1,0:T(8,128)(2,1)S(1)}, bf16[136,1024]{1,0:T(8,128)(2,1)S(1)}, u32[]{:S(2)}, u32[]{:S(2)}) collective-permute-start(bf16[136,1024]{1,0:T(8,128)(2,1)S(1)} %collective-permute-done.11), channel_id=1, source_target_pairs={{0,16},{1,17},{2,18},{3,19},{4,20},{5,21},{6,22},{7,23},{8,24},{9,... | collective-permute-start | bytes 835592 | tf_op jit(solution)/shard_map/ppermute | solution.py:186
  75.3 13.3 %collective-permute-start.10 = (bf16[1024,128]{1,0:T(8,128)(2,1)}, bf16[1024,128]{1,0:T(8,128)(2,1)S(1)}, u32[]{:S(2)}, u32[]{:S(2)}) collective-permute-start(bf16[1024,128]{1,0:T(8,128)(2,1)} %get-tuple-element.15.rest_5_), channel_id=1, source_target_pairs={{0,2},{1,3},{2,4},{3,5},{4,6},{5,7},{6,8},{7,9},{8,10},{9,11},{10,... | collective-permute-start | bytes 786440 | tf_op jit(solution)/shard_map/ppermute | solution.py:186
  77.8 10.8 %copy-start.1 = (bf16[1024,128]{1,0:T(8,128)(2,1)S(1)}, bf16[1024,128]{1,0:T(8,128)(2,1)}, u32[]{:S(2)}) copy-start(bf16[1024,128]{1,0:T(8,128)(2,1)} %get-tuple-element.15.rest_5_) | copy-start | bytes 786436
  77.8 10.8 %copy-start.3 = (bf16[1024,128]{1,0:T(8,128)(2,1)S(1)}, bf16[1024,128]{1,0:T(8,128)(2,1)}, u32[]{:S(2)}) copy-start(bf16[1024,128]{1,0:T(8,128)(2,1)} %get-tuple-element.16.rest_6_) | copy-start | bytes 786436
  77.8 10.8 %copy-start.5 = (bf16[1024,128]{1,0:T(8,128)(2,1)S(1)}, bf16[1024,128]{1,0:T(8,128)(2,1)}, u32[]{:S(2)}) copy-start(bf16[1024,128]{1,0:T(8,128)(2,1)} %get-tuple-element.13.rest_3_) | copy-start | bytes 786436
  77.8 10.8 %copy-start.7 = (bf16[1024,128]{1,0:T(8,128)(2,1)S(1)}, bf16[1024,128]{1,0:T(8,128)(2,1)}, u32[]{:S(2)}) copy-start(bf16[1024,128]{1,0:T(8,128)(2,1)} %get-tuple-element.14.rest_4_) | copy-start | bytes 786436
  77.8 10.8 %copy-start.9 = (bf16[1024,128]{1,0:T(8,128)(2,1)S(1)}, bf16[1024,128]{1,0:T(8,128)(2,1)}, u32[]{:S(2)}) copy-start(bf16[1024,128]{1,0:T(8,128)(2,1)} %get-tuple-element.11.rest_1_) | copy-start | bytes 786436
  77.8 10.8 %copy-start.11 = (bf16[1024,128]{1,0:T(8,128)(2,1)S(1)}, bf16[1024,128]{1,0:T(8,128)(2,1)}, u32[]{:S(2)}) copy-start(bf16[1024,128]{1,0:T(8,128)(2,1)} %get-tuple-element.12.rest_2_) | copy-start | bytes 786436
  77.8 10.8 %copy-start.12 = (bf16[1024,128]{1,0:T(8,128)(2,1)S(1)}, bf16[1024,128]{1,0:T(8,128)(2,1)}, u32[]{:S(2)}) copy-start(bf16[1024,128]{1,0:T(8,128)(2,1)} %rest_0_.3) | copy-start | bytes 786436
  92.9 4.6 %collective-permute-start.15 = (bf16[4,136,1024]{2,1,0:T(8,128)(2,1)S(1)}, bf16[4,136,1024]{2,1,0:T(8,128)(2,1)S(1)}, u32[]{:S(2)}, u32[]{:S(2)}) collective-permute-start(bf16[4,136,1024]{2,1,0:T(8,128)(2,1)S(1)} %get-tuple-element.24), channel_id=1, source_target_pairs={{0,64},{1,65},{2,66},{3,67},{4,68},{5,69},{6,70},{7,71},{8,72},{9,... | collective-permute-start | bytes 3342344 | tf_op jit(solution)/shard_map/ppermute | solution.py:186
  98.0 18.0 %collective-permute-start.19 = (bf16[136,1024]{1,0:T(8,128)(2,1)S(1)}, bf16[136,1024]{1,0:T(8,128)(2,1)S(1)}, u32[]{:S(2)}, u32[]{:S(2)}) collective-permute-start(bf16[136,1024]{1,0:T(8,128)(2,1)S(1)} %get-tuple-element.20), channel_id=1, source_target_pairs={{0,48},{1,49},{2,50},{3,51},{4,52},{5,53},{6,54},{7,55},{8,56},{9,... | collective-permute-start | bytes 835592 | tf_op jit(solution)/shard_map/ppermute | solution.py:186
  100.2 15.9 %collective-permute-start.18 = (bf16[136,1024]{1,0:T(8,128)(2,1)S(1)}, bf16[136,1024]{1,0:T(8,128)(2,1)S(1)}, u32[]{:S(2)}, u32[]{:S(2)}) collective-permute-start(bf16[136,1024]{1,0:T(8,128)(2,1)S(1)} %get-tuple-element.21), channel_id=1, source_target_pairs={{0,32},{1,33},{2,34},{3,35},{4,36},{5,37},{6,38},{7,39},{8,40},{9,... | collective-permute-start | bytes 835592 | tf_op jit(solution)/shard_map/ppermute | solution.py:186
  107.2 10.6 %collective-permute-start.17 = (bf16[136,1024]{1,0:T(8,128)(2,1)S(1)}, bf16[136,1024]{1,0:T(8,128)(2,1)S(1)}, u32[]{:S(2)}, u32[]{:S(2)}) collective-permute-start(bf16[136,1024]{1,0:T(8,128)(2,1)S(1)} %get-tuple-element.22), channel_id=1, source_target_pairs={{0,16},{1,17},{2,18},{3,19},{4,20},{5,21},{6,22},{7,23},{8,24},{9,... | collective-permute-start | bytes 835592 | tf_op jit(solution)/shard_map/ppermute | solution.py:186
  112.4 9.7 %collective-permute-start.16 = (bf16[136,1024]{1,0:T(8,128)(2,1)S(1)}, bf16[136,1024]{1,0:T(8,128)(2,1)S(1)}, u32[]{:S(2)}, u32[]{:S(2)}) collective-permute-start(bf16[136,1024]{1,0:T(8,128)(2,1)S(1)} %get-tuple-element.19), channel_id=1, source_target_pairs={{0,0},{1,1},{2,2},{3,3},{4,4},{5,5},{6,6},{7,7},{8,8},{9,9},{10,10... | collective-permute-start | bytes 835592 | tf_op jit(solution)/shard_map/ppermute | solution.py:186
  123.0 5.6 %collective-permute-start.20 = (bf16[136,512]{1,0:T(8,128)(2,1)S(1)}, bf16[136,512]{1,0:T(8,128)(2,1)S(1)}, u32[]{:S(2)}, u32[]{:S(2)}) collective-permute-start(bf16[136,512]{1,0:T(8,128)(2,1)S(1)} %get-tuple-element.25), channel_id=1, source_target_pairs={{0,64},{1,65},{2,66},{3,67},{4,68},{5,69},{6,70},{7,71},{8,72},{9,... | collective-permute-start | bytes 417800 | tf_op jit(solution)/shard_map/ppermute | solution.py:186
  128.6 0.7 copy-start.15

commit v4 on v3

--- a/solution.py
+++ b/solution.py
@@ -14,7 +14,7 @@
 WIDE = 512
 TILES = ROWS // 8
 HALO = 144
-ORDER = (0, 3, 1, 2)
+ORDER = (0, 2, 3, 1)
 ROUND = 60000000
 OFFSETS = (0, -1, 1, -2, 2, -3, 3, -4)
 BF = jnp.bfloat16

time: 132 us -> 132 us (level)
  the two profiles are of different devices: /device:TPU:24 before, /device:TPU:7 now
where the time goes in v4:
time: 132 us
  starting transfers between devices  81.1 us (61%)
  waiting for transfers between devices  28.9 us (22%)
  Pallas kernels  15.9 us (12%)
  local copies, waits for them, and re-layouts  3.54 us (3%)
  other arithmetic  1.69 us (1%)
    ppermute x20, starting transfers between devices, permute(): return lax.ppermute(block, ('tp', 'cp'), pairs)  78.4 us
    ppermute x20, waiting for transfers between devices, permute(): return lax.ppermute(block, ('tp', 'cp'), pairs)  28.9 us
    pallas_call x1, Pallas kernels, run_conv(): pl.pallas_call(conv_kernel, grid=(1024 // CONV,), in_specs=[pl.BlockSpec(...  7.68 us
    pallas_call x2, Pallas kernels, run_mm(): pl.pallas_call(mm_kernel, in_specs=[pl.BlockSpec(memory_space=pltpu.SMEM)...  4.15 us
    unnamed x34, local copies, waits for them, and re-layouts  3.54 us
  transfers between devices with their start and end apart: 21, of which 10 were waited for; matrix products, arithmetic and copies ran while one was open for 0% of the time, Pallas kernels for 8%

profile of v4, /device:TPU:7, one launch (start us, length us, event | category | flops | bytes accessed | tf_op | source)
XLA Modules:
  0.0 131.5 jit_solution(12102686824859934092)
XLA Ops:
  0.0 4.9 %collective-permute-start.4 = (bf16[1024,128]{1,0:T(8,128)(2,1)}, bf16[1024,128]{1,0:T(8,128)(2,1)S(1)}, u32[]{:S(2)}, u32[]{:S(2)}) collective-permute-start(bf16[1024,128]{1,0:T(8,128)(2,1)} %rest_0_.3), channel_id=1, source_target_pairs={{0,2},{1,3},{2,4},{3,5},{4,6},{5,7},{6,8},{7,9},{8,10},{9,11},{10,... | collective-permute-start | bytes 786440 | tf_op jit(solution)/shard_map/ppermute | solution.py:186
  4.9 8.6 %collective-permute-start.5 = (bf16[1024,128]{1,0:T(8,128)(2,1)}, bf16[1024,128]{1,0:T(8,128)(2,1)S(1)}, u32[]{:S(2)}, u32[]{:S(2)}) collective-permute-start(bf16[1024,128]{1,0:T(8,128)(2,1)} %rest_0_.3), channel_id=1, source_target_pairs={{0,14},{1,15},{2,0},{3,1},{4,2},{5,3},{6,4},{7,5},{8,6},{9,7},{10,... | collective-permute-start | bytes 786440 | tf_op jit(solution)/shard_map/ppermute | solution.py:186
  13.5 2.3 %pack.1 = bf16[144,1024]{1,0:T(8,128)(2,1)} custom-call(bf16[3,136,1024]{2,1,0:T(8,128)(2,1)} %x_ref.3, f32[3,3,1024]{2,1,0:T(4,128)} %taps_ref.3), custom_call_target="tpu_custom_call" | custom-call | flops 3000000 | bytes 6000000 | tf_op jit(solution)/shard_map/pack/pallas_call | solution.py:77
  15.8 2.6 %collective-permute-start = (bf16[144,1024]{1,0:T(8,128)(2,1)}, bf16[144,1024]{1,0:T(8,128)(2,1)S(1)}, u32[]{:S(2)}, u32[]{:S(2)}) collective-permute-start(bf16[144,1024]{1,0:T(8,128)(2,1)} %pack.1), channel_id=1, source_target_pairs={{0,1},{1,2},{2,3},{3,4},{4,5},{5,6},{6,7},{7,8},{8,9},{9,10},{10,1... | collective-permute-start | bytes 884744 | tf_op jit(solution)/shard_map/ppermute | solution.py:204
  18.4 0.9 collective-permute-done.4.refs_0_
  19.3 3.8 %collective-permute-done.5.refs_1_ = bf16[1024,128]{1,0:T(8,128)(2,1)S(1)} collective-permute-done((bf16[1024,128]{1,0:T(8,128)(2,1)}, bf16[1024,128]{1,0:T(8,128)(2,1)S(1)}, u32[]{:S(2)}, u32[]{:S(2)}) %collective-permute-start.5) | collective-permute-done | bytes 262176 | tf_op jit(solution)/shard_map/ppermute | solution.py:186
  23.1 0.7 copy-done.10
  23.8 4.6 %collective-permute-start.6 = (bf16[1024,128]{1,0:T(8,128)(2,1)}, bf16[1024,128]{1,0:T(8,128)(2,1)S(1)}, u32[]{:S(2)}, u32[]{:S(2)}) collective-permute-start(bf16[1024,128]{1,0:T(8,128)(2,1)} %get-tuple-element.11.rest_1_), channel_id=1, source_target_pairs={{0,2},{1,3},{2,4},{3,5},{4,6},{5,7},{6,8},{7,9},{8,10},{9,11},{10,... | collective-permute-start | bytes 786440 | tf_op jit(solution)/shard_map/ppermute | solution.py:186
  28.4 5.0 %collective-permute-start.7 = (bf16[1024,128]{1,0:T(8,128)(2,1)}, bf16[1024,128]{1,0:T(8,128)(2,1)S(1)}, u32[]{:S(2)}, u32[]{:S(2)}) collective-permute-start(bf16[1024,128]{1,0:T(8,128)(2,1)} %get-tuple-element.12.rest_2_), channel_id=1, source_target_pairs={{0,14},{1,15},{2,0},{3,1},{4,2},{5,3},{6,4},{7,5},{8,6},{9,7},{10,... | collective-permute-start | bytes 786440 | tf_op jit(solution)/shard_map/ppermute | solution.py:186
  33.5 0.7 copy-done.14
  34.2 7.7 %conv.1 = bf16[136,1024]{1,0:T(8,128)(2,1)} custom-call(bf16[3,136,1024]{2,1,0:T(8,128)(2,1)} %x_ref.3, bf16[144,1024]{1,0:T(8,128)(2,1)} %copy-done.14, f32[3,3,1024]{2,1,0:T(4,128)} %taps_ref.3, f32[128,1024]{1,0:T(8,128)} %long_ref.1, f32[1,1024]{1,0:T(1,128)} %bitcast.11), custom_call_target="tpu_custom_call" | custom-call | flops 36000000 | bytes 20000000 | tf_op jit(solution)/shard_map/conv/pallas_call | solution.py:93
  41.9 2.6 %collective-permute-start.3 = (bf16[136,1024]{1,0:T(8,128)(2,1)}, bf16[136,1024]{1,0:T(8,128)(2,1)S(1)}, u32[]{:S(2)}, u32[]{:S(2)}) collective-permute-start(bf16[136,1024]{1,0:T(8,128)(2,1)} %conv.1), channel_id=1, source_target_pairs={{0,48},{1,49},{2,50},{3,51},{4,52},{5,53},{6,54},{7,55},{8,56},{9,... | collective-permute-start | bytes 835592 | tf_op jit(solution)/shard_map/ppermute | solution.py:186
  44.4 1.9 %collective-permute-start.11 = (bf16[136,1024]{1,0:T(8,128)(2,1)}, bf16[136,1024]{1,0:T(8,128)(2,1)S(1)}, u32[]{:S(2)}, u32[]{:S(2)}) collective-permute-start(bf16[136,1024]{1,0:T(8,128)(2,1)} %conv.1), channel_id=1, source_target_pairs={{0,1},{1,0},{2,3},{3,2},{4,5},{5,4},{6,7},{7,6},{8,9},{9,8},{10,11... | collective-permute-start | bytes 835592 | tf_op jit(solution)/shard_map/ppermute | solution.py:186
  46.4 0.7 copy-done.4
  47.1 0.7 copy-done.6
  47.8 3.3 %collective-permute-start.8 = (bf16[1024,128]{1,0:T(8,128)(2,1)}, bf16[1024,128]{1,0:T(8,128)(2,1)S(1)}, u32[]{:S(2)}, u32[]{:S(2)}) collective-permute-start(bf16[1024,128]{1,0:T(8,128)(2,1)} %get-tuple-element.13.rest_3_), channel_id=1, source_target_pairs={{0,2},{1,3},{2,4},{3,5},{4,6},{5,7},{6,8},{7,9},{8,10},{9,11},{10,... | collective-permute-start | bytes 786440 | tf_op jit(solution)/shard_map/ppermute | solution.py:186
  51.1 4.1 %collective-permute-start.9 = (bf16[1024,128]{1,0:T(8,128)(2,1)}, bf16[1024,128]{1,0:T(8,128)(2,1)S(1)}, u32[]{:S(2)}, u32[]{:S(2)}) collective-permute-start(bf16[1024,128]{1,0:T(8,128)(2,1)} %get-tuple-element.14.rest_4_), channel_id=1, source_target_pairs={{0,14},{1,15},{2,0},{3,1},{4,2},{5,3},{6,4},{7,5},{8,6},{9,7},{10,... | collective-permute-start | bytes 786440 | tf_op jit(solution)/shard_map/ppermute | solution.py:186
  55.2 2.8 %collective-permute-start.2 = (bf16[136,1024]{1,0:T(8,128)(2,1)}, bf16[136,1024]{1,0:T(8,128)(2,1)S(1)}, u32[]{:S(2)}, u32[]{:S(2)}) collective-permute-start(bf16[136,1024]{1,0:T(8,128)(2,1)} %conv.1), channel_id=1, source_target_pairs={{0,32},{1,33},{2,34},{3,35},{4,36},{5,37},{6,38},{7,39},{8,40},{9,... | collective-permute-start | bytes 835592 | tf_op jit(solution)/shard_map/ppermute | solution.py:186
  58.0 3.8 %collective-permute-start.1 = (bf16[136,1024]{1,0:T(8,128)(2,1)}, bf16[136,1024]{1,0:T(8,128)(2,1)S(1)}, u32[]{:S(2)}, u32[]{:S(2)}) collective-permute-start(bf16[136,1024]{1,0:T(8,128)(2,1)} %conv.1), channel_id=1, source_target_pairs={{0,16},{1,17},{2,18},{3,19},{4,20},{5,21},{6,22},{7,23},{8,24},{9,... | collective-permute-start | bytes 835592 | tf_op jit(solution)/shard_map/ppermute | solution.py:186
  61.8 2.4 %collective-permute-start.14 = (bf16[136,1024]{1,0:T(8,128)(2,1)S(1)}, bf16[136,1024]{1,0:T(8,128)(2,1)S(1)}, u32[]{:S(2)}, u32[]{:S(2)}) collective-permute-start(bf16[136,1024]{1,0:T(8,128)(2,1)S(1)} %collective-permute-done.11), channel_id=1, source_target_pairs={{0,48},{1,49},{2,50},{3,51},{4,52},{5,53},{6,54},{7,55},{8,56},{9,... | collective-permute-start | bytes 835592 | tf_op jit(solution)/shard_map/ppermute | solution.py:186
  64.3 1.8 %collective-permute-done.8.refs_0_ = bf16[1024,128]{1,0:T(8,128)(2,1)S(1)} collective-permute-done((bf16[1024,128]{1,0:T(8,128)(2,1)}, bf16[1024,128]{1,0:T(8,128)(2,1)S(1)}, u32[]{:S(2)}, u32[]{:S(2)}) %collective-permute-start.8) | collective-permute-done | bytes 262176 | tf_op jit(solution)/shard_map/ppermute | solution.py:186
  66.0 2.7 %collective-permute-start.13 = (bf16[136,1024]{1,0:T(8,128)(2,1)S(1)}, bf16[136,1024]{1,0:T(8,128)(2,1)S(1)}, u32[]{:S(2)}, u32[]{:S(2)}) collective-permute-start(bf16[136,1024]{1,0:T(8,128)(2,1)S(1)} %collective-permute-done.11), channel_id=1, source_target_pairs={{0,32},{1,33},{2,34},{3,35},{4,36},{5,37},{6,38},{7,39},{8,40},{9,... | collective-permute-start | bytes 835592 | tf_op jit(solution)/shard_map/ppermute | solution.py:186
  68.8 3.8 %collective-permute-start.12 = (bf16[136,1024]{1,0:T(8,128)(2,1)S(1)}, bf16[136,1024]{1,0:T(8,128)(2,1)S(1)}, u32[]{:S(2)}, u32[]{:S(2)}) collective-permute-start(bf16[136,1024]{1,0:T(8,128)(2,1)S(1)} %collective-permute-done.11), channel_id=1, source_target_pairs={{0,16},{1,17},{2,18},{3,19},{4,20},{5,21},{6,22},{7,23},{8,24},{9,... | collective-permute-start | bytes 835592 | tf_op jit(solution)/shard_map/ppermute | solution.py:186
  72.6 0.1 pad_add_fusion
  72.7 2.1 %collective-permute-start.10 = (bf16[1024,128]{1,0:T(8,128)(2,1)}, bf16[1024,128]{1,0:T(8,128)(2,1)S(1)}, u32[]{:S(2)}, u32[]{:S(2)}) collective-permute-start(bf16[1024,128]{1,0:T(8,128)(2,1)} %get-tuple-element.15.rest_5_), channel_id=1, source_target_pairs={{0,2},{1,3},{2,4},{3,5},{4,6},{5,7},{6,8},{7,9},{8,10},{9,11},{10,... | collective-permute-start | bytes 786440 | tf_op jit(solution)/shard_map/ppermute | solution.py:186
  74.8 0.1 pad_maximum_fusion.a_ref
  75.0 0.0 copy-start.12
  75.0 0.3 collective-permute-done.14
  75.3 7.7 %collective-permute-done.13 = bf16[136,1024]{1,0:T(8,128)(2,1)S(1)} collective-permute-done((bf16[136,1024]{1,0:T(8,128)(2,1)S(1)}, bf16[136,1024]{1,0:T(8,128)(2,1)S(1)}, u32[]{:S(2)}, u32[]{:S(2)}) %collective-permute-start.13) | collective-permute-done | bytes 278560 | tf_op jit(solution)/shard_map/ppermute | solution.py:186
  83.0 0.1 pad_maximum_fusion.1.a_ref
  83.1 2.3 %collective-permute-done.10.rest_7_ = bf16[1024,128]{1,0:T(8,128)(2,1)S(1)} collective-permute-done((bf16[1024,128]{1,0:T(8,128)(2,1)}, bf16[1024,128]{1,0:T(8,128)(2,1)S(1)}, u32[]{:S(2)}, u32[]{:S(2)}) %collective-permute-start.10) | collective-permute-done | bytes 262176 | tf_op jit(solution)/shard_map/ppermute | solution.py:186
  85.5 2.1 %mm.2 = bf16[4,136,1024]{2,1,0:T(8,128)(2,1)S(1)} custom-call(s32[5]{0:T(128)S(1)} %get-tuple-element.27.where_ref, bf16[544,1024]{1,0:T(8,128)(2,1)S(1)} %pad_maximum_fusion.a_ref, bf16[1024,128]{1,0:T(8,128)(2,1)S(1)} %copy-done.12, bf16[1024,128]{1,0:T(8,128)(2,1)S(1)} %copy-done.9, bf16[1024,128]{1,0:T(8,128)(2,1)S(1)} %copy-done.11, ...), custom_call_target="tpu_custom_call" | custom-call | flops 1140000000 | bytes 5000000 | tf_op jit(solution)/shard_map/mm/pallas_call | solution.py:129
  87.6 2.1 %mm.3 = bf16[4,136,1024]{2,1,0:T(8,128)(2,1)S(1)} custom-call(s32[5]{0:T(128)S(1)} %get-tuple-element.28.where_ref, bf16[544,1024]{1,0:T(8,128)(2,1)S(1)} %pad_maximum_fusion.1.a_ref, bf16[1024,128]{1,0:T(8,128)(2,1)S(1)} %copy-done.12, bf16[1024,128]{1,0:T(8,128)(2,1)S(1)} %copy-done.9, bf16[1024,128]{1,0:T(8,128)(2,1)S(1)} %copy-done.11, ...), custom_call_target="tpu_custom_call" | custom-call | flops 1140000000 | bytes 5000000 | tf_op jit(solution)/shard_map/mm/pallas_call | solution.py:129
  89.7 0.2 broadcast_select_fusion.1
  89.8 4.0 %collective-permute-start.15 = (bf16[4,136,1024]{2,1,0:T(8,128)(2,1)S(1)}, bf16[4,136,1024]{2,1,0:T(8,128)(2,1)S(1)}, u32[]{:S(2)}, u32[]{:S(2)}) collective-permute-start(bf16[4,136,1024]{2,1,0:T(8,128)(2,1)S(1)} %get-tuple-element.24), channel_id=1, source_target_pairs={{0,64},{1,65},{2,66},{3,67},{4,68},{5,69},{6,70},{7,71},{8,72},{9,... | collective-permute-start | bytes 3342344 | tf_op jit(solution)/shard_map/ppermute | solution.py:186
  93.9 2.4 %collective-permute-done.15 = bf16[4,136,1024]{2,1,0:T(8,128)(2,1)S(1)} collective-permute-done((bf16[4,136,1024]{2,1,0:T(8,128)(2,1)S(1)}, bf16[4,136,1024]{2,1,0:T(8,128)(2,1)S(1)}, u32[]{:S(2)}, u32[]{:S(2)}) %collective-permute-start.15) | collective-permute-done | bytes 1114144 | tf_op jit(solution)/shard_map/ppermute | solution.py:186
  96.2 0.4 fusion
  96.7 8.5 %collective-permute-start.19 = (bf16[136,1024]{1,0:T(8,128)(2,1)S(1)}, bf16[136,1024]{1,0:T(8,128)(2,1)S(1)}, u32[]{:S(2)}, u32[]{:S(2)}) collective-permute-start(bf16[136,1024]{1,0:T(8,128)(2,1)S(1)} %get-tuple-element.20), channel_id=1, source_target_pairs={{0,48},{1,49},{2,50},{3,51},{4,52},{5,53},{6,54},{7,55},{8,56},{9,... | collective-permute-start | bytes 835592 | tf_op jit(solution)/shard_map/ppermute | solution.py:186
  105.2 1.9 %collective-permute-start.18 = (bf16[136,1024]{1,0:T(8,128)(2,1)S(1)}, bf16[136,1024]{1,0:T(8,128)(2,1)S(1)}, u32[]{:S(2)}, u32[]{:S(2)}) collective-permute-start(bf16[136,1024]{1,0:T(8,128)(2,1)S(1)} %get-tuple-element.21), channel_id=1, source_target_pairs={{0,32},{1,33},{2,34},{3,35},{4,36},{5,37},{6,38},{7,39},{8,40},{9,... | collective-permute-start | bytes 835592 | tf_op jit(solution)/shard_map/ppermute | solution.py:186
  107.1 7.6 %collective-permute-start.17 = (bf16[136,1024]{1,0:T(8,128)(2,1)S(1)}, bf16[136,1024]{1,0:T(8,128)(2,1)S(1)}, u32[]{:S(2)}, u32[]{:S(2)}) collective-permute-start(bf16[136,1024]{1,0:T(8,128)(2,1)S(1)} %get-tuple-element.22), channel_id=1, source_target_pairs={{0,16},{1,17},{2,18},{3,19},{4,20},{5,21},{6,22},{7,23},{8,24},{9,... | collective-permute-start | bytes 835592 | tf_op jit(solution)/shard_map/ppermute | solution.py:186
  114.7 1.9 %collective-permute-start.16 = (bf16[136,1024]{1,0:T(8,128)(2,1)S(1)}, bf16[136,1024]{1,0:T(8,128)(2,1)S(1)}, u32[]{:S(2)}, u32[]{:S(2)}) collective-permute-start(bf16[136,1024]{1,0:T(8,128)(2,1)S(1)} %get-tuple-element.19), channel_id=1, source_target_pairs={{0,0},{1,1},{2,2},{3,3},{4,4},{5,5},{6,6},{7,7},{8,8},{9,9},{10,10... | collective-permute-start | bytes 835592 | tf_op jit(solution)/shard_map/ppermute | solution.py:186
  116.7 3.1 %collective-permute-done.18 = bf16[136,1024]{1,0:T(8,128)(2,1)S(1)} collective-permute-done((bf16[136,1024]{1,0:T(8,128)(2,1)S(1)}, bf16[136,1024]{1,0:T(8,128)(2,1)S(1)}, u32[]{:S(2)}, u32[]{:S(2)}) %collective-permute-start.18) | collective-permute-done | bytes 278560 | tf_op jit(solution)/shard_map/ppermute | solution.py:186
  119.8 5.2 %collective-permute-done.16 = bf16[136,1024]{1,0:T(8,128)(2,1)S(1)} collective-permute-done((bf16[136,1024]{1,0:T(8,128)(2,1)S(1)}, bf16[136,1024]{1,0:T(8,128)(2,1)S(1)}, u32[]{:S(2)}, u32[]{:S(2)}) %collective-permute-start.16) | collective-permute-done | bytes 278560 | tf_op jit(solution)/shard_map/ppermute | solution.py:186
  125.0 0.9 add_convert_fusion.4
  125.9 1.9 %collective-permute-start.20 = (bf16[136,512]{1,0:T(8,128)(2,1)S(1)}, bf16[136,512]{1,0:T(8,128)(2,1)S(1)}, u32[]{:S(2)}, u32[]{:S(2)}) collective-permute-start(bf16[136,512]{1,0:T(8,128)(2,1)S(1)} %get-tuple-element.25), channel_id=1, source_target_pairs={{0,64},{1,65},{2,66},{3,67},{4,68},{5,69},{6,70},{7,71},{8,72},{9,... | collective-permute-start | bytes 417800 | tf_op jit(solution)/shard_map/ppermute | solution.py:186
  127.8 1.3 collective-permute-done.20.other_ref
  129.1 0.7 copy-done.15
  129.8 1.7 %join.1 = bf16[136,1024]{1,0:T(8,128)(2,1)} custom-call(s32[1]{0:T(128)} %bitcast.late_ref, bf16[136,512]{1,0:T(8,128)(2,1)} %get-tuple-element.26.keep_ref, bf16[136,512]{1,0:T(8,128)(2,1)} %copy-done.15), custom_call_target="tpu_custom_call" | custom-call | flops 1000 | bytes 600000 | tf_op jit(solution)/shard_map/join/pallas_call | solution.py:168
  (43 shorter events, 0.1 us)
Async XLA Ops:
  0.0 19.3 %collective-permute-start.4 = (bf16[1024,128]{1,0:T(8,128)(2,1)}, bf16[1024,128]{1,0:T(8,128)(2,1)S(1)}, u32[]{:S(2)}, u32[]{:S(2)}) collective-permute-start(bf16[1024,128]{1,0:T(8,128)(2,1)} %rest_0_.3), channel_id=1, source_target_pairs={{0,2},{1,3},{2,4},{3,5},{4,6},{5,7},{6,8},{7,9},{8,10},{9,11},{10,... | collective-permute-start | bytes 786440 | tf_op jit(solution)/shard_map/ppermute | solution.py:186
  4.9 18.2 %collective-permute-start.5 = (bf16[1024,128]{1,0:T(8,128)(2,1)}, bf16[1024,128]{1,0:T(8,128)(2,1)S(1)}, u32[]{:S(2)}, u32[]{:S(2)}) collective-permute-start(bf16[1024,128]{1,0:T(8,128)(2,1)} %rest_0_.3), channel_id=1, source_target_pairs={{0,14},{1,15},{2,0},{3,1},{4,2},{5,3},{6,4},{7,5},{8,6},{9,7},{10,... | collective-permute-start | bytes 786440 | tf_op jit(solution)/shard_map/ppermute | solution.py:186
  15.8 17.7 %collective-permute-start = (bf16[144,1024]{1,0:T(8,128)(2,1)}, bf16[144,1024]{1,0:T(8,128)(2,1)S(1)}, u32[]{:S(2)}, u32[]{:S(2)}) collective-permute-start(bf16[144,1024]{1,0:T(8,128)(2,1)} %pack.1), channel_id=1, source_target_pairs={{0,1},{1,2},{2,3},{3,4},{4,5},{5,6},{6,7},{7,8},{8,9},{9,10},{10,1... | collective-permute-start | bytes 884744 | tf_op jit(solution)/shard_map/ppermute | solution.py:204
  19.3 3.8 %copy-start.8 = (bf16[1024,128]{1,0:T(8,128)(2,1)}, bf16[1024,128]{1,0:T(8,128)(2,1)S(1)}, u32[]{:S(2)}) copy-start(bf16[1024,128]{1,0:T(8,128)(2,1)S(1)} %collective-permute-done.4.refs_0_) | copy-start | bytes 786436
  23.1 0.7 copy-start.10
  23.8 22.5 %collective-permute-start.6 = (bf16[1024,128]{1,0:T(8,128)(2,1)}, bf16[1024,128]{1,0:T(8,128)(2,1)S(1)}, u32[]{:S(2)}, u32[]{:S(2)}) collective-permute-start(bf16[1024,128]{1,0:T(8,128)(2,1)} %get-tuple-element.11.rest_1_), channel_id=1, source_target_pairs={{0,2},{1,3},{2,4},{3,5},{4,6},{5,7},{6,8},{7,9},{8,10},{9,11},{10,... | collective-permute-start | bytes 786440 | tf_op jit(solution)/shard_map/ppermute | solution.py:186
  28.4 18.0 %collective-permute-start.7 = (bf16[1024,128]{1,0:T(8,128)(2,1)}, bf16[1024,128]{1,0:T(8,128)(2,1)S(1)}, u32[]{:S(2)}, u32[]{:S(2)}) collective-permute-start(bf16[1024,128]{1,0:T(8,128)(2,1)} %get-tuple-element.12.rest_2_), channel_id=1, source_target_pairs={{0,14},{1,15},{2,0},{3,1},{4,2},{5,3},{6,4},{7,5},{8,6},{9,7},{10,... | collective-permute-start | bytes 786440 | tf_op jit(solution)/shard_map/ppermute | solution.py:186
  33.5 0.7 copy-start.14
  34.2 38.4 %copy-start.16 = (s32[4]{0:T(128)S(1)}, s32[4]{0:T(128)}, u32[]{:S(2)}) copy-start(s32[4]{0:T(128)} %constant.63.clone) | copy-start | bytes 52
  41.9 33.0 %copy-start.13 = (bf16[136,1024]{1,0:T(8,128)(2,1)S(1)}, bf16[136,1024]{1,0:T(8,128)(2,1)}, u32[]{:S(2)}) copy-start(bf16[136,1024]{1,0:T(8,128)(2,1)} %conv.1) | copy-start | bytes 835588
  41.9 16.1 %collective-permute-start.3 = (bf16[136,1024]{1,0:T(8,128)(2,1)}, bf16[136,1024]{1,0:T(8,128)(2,1)S(1)}, u32[]{:S(2)}, u32[]{:S(2)}) collective-permute-start(bf16[136,1024]{1,0:T(8,128)(2,1)} %conv.1), channel_id=1, source_target_pairs={{0,48},{1,49},{2,50},{3,51},{4,52},{5,53},{6,54},{7,55},{8,56},{9,... | collective-permute-start | bytes 835592 | tf_op jit(solution)/shard_map/ppermute | solution.py:186
  44.4 17.3 %collective-permute-start.11 = (bf16[136,1024]{1,0:T(8,128)(2,1)}, bf16[136,1024]{1,0:T(8,128)(2,1)S(1)}, u32[]{:S(2)}, u32[]{:S(2)}) collective-permute-start(bf16[136,1024]{1,0:T(8,128)(2,1)} %conv.1), channel_id=1, source_target_pairs={{0,1},{1,0},{2,3},{3,2},{4,5},{5,4},{6,7},{7,6},{8,9},{9,8},{10,11... | collective-permute-start | bytes 835592 | tf_op jit(solution)/shard_map/ppermute | solution.py:186
  46.4 0.7 copy-start.4
  47.1 0.7 copy-start.6
  47.8 18.2 %collective-permute-start.8 = (bf16[1024,128]{1,0:T(8,128)(2,1)}, bf16[1024,128]{1,0:T(8,128)(2,1)S(1)}, u32[]{:S(2)}, u32[]{:S(2)}) collective-permute-start(bf16[1024,128]{1,0:T(8,128)(2,1)} %get-tuple-element.13.rest_3_), channel_id=1, source_target_pairs={{0,2},{1,3},{2,4},{3,5},{4,6},{5,7},{6,8},{7,9},{8,10},{9,11},{10,... | collective-permute-start | bytes 786440 | tf_op jit(solution)/shard_map/ppermute | solution.py:186
  51.1 17.6 %collective-permute-start.9 = (bf16[1024,128]{1,0:T(8,128)(2,1)}, bf16[1024,128]{1,0:T(8,128)(2,1)S(1)}, u32[]{:S(2)}, u32[]{:S(2)}) collective-permute-start(bf16[1024,128]{1,0:T(8,128)(2,1)} %get-tuple-element.14.rest_4_), channel_id=1, source_target_pairs={{0,14},{1,15},{2,0},{3,1},{4,2},{5,3},{6,4},{7,5},{8,6},{9,7},{10,... | collective-permute-start | bytes 786440 | tf_op jit(solution)/shard_map/ppermute | solution.py:186
  55.2 17.5 %collective-permute-start.2 = (bf16[136,1024]{1,0:T(8,128)(2,1)}, bf16[136,1024]{1,0:T(8,128)(2,1)S(1)}, u32[]{:S(2)}, u32[]{:S(2)}) collective-permute-start(bf16[136,1024]{1,0:T(8,128)(2,1)} %conv.1), channel_id=1, source_target_pairs={{0,32},{1,33},{2,34},{3,35},{4,36},{5,37},{6,38},{7,39},{8,40},{9,... | collective-permute-start | bytes 835592 | tf_op jit(solution)/shard_map/ppermute | solution.py:186
  58.0 16.8 %collective-permute-start.1 = (bf16[136,1024]{1,0:T(8,128)(2,1)}, bf16[136,1024]{1,0:T(8,128)(2,1)S(1)}, u32[]{:S(2)}, u32[]{:S(2)}) collective-permute-start(bf16[136,1024]{1,0:T(8,128)(2,1)} %conv.1), channel_id=1, source_target_pairs={{0,16},{1,17},{2,18},{3,19},{4,20},{5,21},{6,22},{7,23},{8,24},{9,... | collective-permute-start | bytes 835592 | tf_op jit(solution)/shard_map/ppermute | solution.py:186
  61.8 13.5 %collective-permute-start.14 = (bf16[136,1024]{1,0:T(8,128)(2,1)S(1)}, bf16[136,1024]{1,0:T(8,128)(2,1)S(1)}, u32[]{:S(2)}, u32[]{:S(2)}) collective-permute-start(bf16[136,1024]{1,0:T(8,128)(2,1)S(1)} %collective-permute-done.11), channel_id=1, source_target_pairs={{0,48},{1,49},{2,50},{3,51},{4,52},{5,53},{6,54},{7,55},{8,56},{9,... | collective-permute-start | bytes 835592 | tf_op jit(solution)/shard_map/ppermute | solution.py:186
  66.0 6.7 %copy-start = (bf16[1024,128]{1,0:T(8,128)(2,1)}, bf16[1024,128]{1,0:T(8,128)(2,1)S(1)}, u32[]{:S(2)}) copy-start(bf16[1024,128]{1,0:T(8,128)(2,1)S(1)} %collective-permute-done.8.refs_0_) | copy-start | bytes 786436
  66.0 17.0 %collective-permute-start.13 = (bf16[136,1024]{1,0:T(8,128)(2,1)S(1)}, bf16[136,1024]{1,0:T(8,128)(2,1)S(1)}, u32[]{:S(2)}, u32[]{:S(2)}) collective-permute-start(bf16[136,1024]{1,0:T(8,128)(2,1)S(1)} %collective-permute-done.11), channel_id=1, source_target_pairs={{0,32},{1,33},{2,34},{3,35},{4,36},{5,37},{6,38},{7,39},{8,40},{9,... | collective-permute-start | bytes 835592 | tf_op jit(solution)/shard_map/ppermute | solution.py:186
  68.7 4.0 %copy-start.2 = (bf16[1024,128]{1,0:T(8,128)(2,1)}, bf16[1024,128]{1,0:T(8,128)(2,1)S(1)}, u32[]{:S(2)}) copy-start(bf16[1024,128]{1,0:T(8,128)(2,1)S(1)} %collective-permute-done.9.refs_1_) | copy-start | bytes 786436
  68.8 14.3 %collective-permute-start.12 = (bf16[136,1024]{1,0:T(8,128)(2,1)S(1)}, bf16[136,1024]{1,0:T(8,128)(2,1)S(1)}, u32[]{:S(2)}, u32[]{:S(2)}) collective-permute-start(bf16[136,1024]{1,0:T(8,128)(2,1)S(1)} %collective-permute-done.11), channel_id=1, source_target_pairs={{0,16},{1,17},{2,18},{3,19},{4,20},{5,21},{6,22},{7,23},{8,24},{9,... | collective-permute-start | bytes 835592 | tf_op jit(solution)/shard_map/ppermute | solution.py:186
  72.7 12.7 %collective-permute-start.10 = (bf16[1024,128]{1,0:T(8,128)(2,1)}, bf16[1024,128]{1,0:T(8,128)(2,1)S(1)}, u32[]{:S(2)}, u32[]{:S(2)}) collective-permute-start(bf16[1024,128]{1,0:T(8,128)(2,1)} %get-tuple-element.15.rest_5_), channel_id=1, source_target_pairs={{0,2},{1,3},{2,4},{3,5},{4,6},{5,7},{6,8},{7,9},{8,10},{9,11},{10,... | collective-permute-start | bytes 786440 | tf_op jit(solution)/shard_map/ppermute | solution.py:186
  74.9 10.5 %copy-start.1 = (bf16[1024,128]{1,0:T(8,128)(2,1)S(1)}, bf16[1024,128]{1,0:T(8,128)(2,1)}, u32[]{:S(2)}) copy-start(bf16[1024,128]{1,0:T(8,128)(2,1)} %get-tuple-element.15.rest_5_) | copy-start | bytes 786436
  74.9 10.5 %copy-start.3 = (bf16[1024,128]{1,0:T(8,128)(2,1)S(1)}, bf16[1024,128]{1,0:T(8,128)(2,1)}, u32[]{:S(2)}) copy-start(bf16[1024,128]{1,0:T(8,128)(2,1)} %get-tuple-element.16.rest_6_) | copy-start | bytes 786436
  75.0 10.5 %copy-start.5 = (bf16[1024,128]{1,0:T(8,128)(2,1)S(1)}, bf16[1024,128]{1,0:T(8,128)(2,1)}, u32[]{:S(2)}) copy-start(bf16[1024,128]{1,0:T(8,128)(2,1)} %get-tuple-element.13.rest_3_) | copy-start | bytes 786436
  75.0 10.5 %copy-start.7 = (bf16[1024,128]{1,0:T(8,128)(2,1)S(1)}, bf16[1024,128]{1,0:T(8,128)(2,1)}, u32[]{:S(2)}) copy-start(bf16[1024,128]{1,0:T(8,128)(2,1)} %get-tuple-element.14.rest_4_) | copy-start | bytes 786436
  75.0 10.5 %copy-start.9 = (bf16[1024,128]{1,0:T(8,128)(2,1)S(1)}, bf16[1024,128]{1,0:T(8,128)(2,1)}, u32[]{:S(2)}) copy-start(bf16[1024,128]{1,0:T(8,128)(2,1)} %get-tuple-element.11.rest_1_) | copy-start | bytes 786436
  75.0 10.5 %copy-start.11 = (bf16[1024,128]{1,0:T(8,128)(2,1)S(1)}, bf16[1024,128]{1,0:T(8,128)(2,1)}, u32[]{:S(2)}) copy-start(bf16[1024,128]{1,0:T(8,128)(2,1)} %get-tuple-element.12.rest_2_) | copy-start | bytes 786436
  75.0 10.5 %copy-start.12 = (bf16[1024,128]{1,0:T(8,128)(2,1)S(1)}, bf16[1024,128]{1,0:T(8,128)(2,1)}, u32[]{:S(2)}) copy-start(bf16[1024,128]{1,0:T(8,128)(2,1)} %rest_0_.3) | copy-start | bytes 786436
  89.8 6.4 %collective-permute-start.15 = (bf16[4,136,1024]{2,1,0:T(8,128)(2,1)S(1)}, bf16[4,136,1024]{2,1,0:T(8,128)(2,1)S(1)}, u32[]{:S(2)}, u32[]{:S(2)}) collective-permute-start(bf16[4,136,1024]{2,1,0:T(8,128)(2,1)S(1)} %get-tuple-element.24), channel_id=1, source_target_pairs={{0,64},{1,65},{2,66},{3,67},{4,68},{5,69},{6,70},{7,71},{8,72},{9,... | collective-permute-start | bytes 3342344 | tf_op jit(solution)/shard_map/ppermute | solution.py:186
  96.7 20.0 %collective-permute-start.19 = (bf16[136,1024]{1,0:T(8,128)(2,1)S(1)}, bf16[136,1024]{1,0:T(8,128)(2,1)S(1)}, u32[]{:S(2)}, u32[]{:S(2)}) collective-permute-start(bf16[136,1024]{1,0:T(8,128)(2,1)S(1)} %get-tuple-element.20), channel_id=1, source_target_pairs={{0,48},{1,49},{2,50},{3,51},{4,52},{5,53},{6,54},{7,55},{8,56},{9,... | collective-permute-start | bytes 835592 | tf_op jit(solution)/shard_map/ppermute | solution.py:186
  105.2 14.6 %collective-permute-start.18 = (bf16[136,1024]{1,0:T(8,128)(2,1)S(1)}, bf16[136,1024]{1,0:T(8,128)(2,1)S(1)}, u32[]{:S(2)}, u32[]{:S(2)}) collective-permute-start(bf16[136,1024]{1,0:T(8,128)(2,1)S(1)} %get-tuple-element.21), channel_id=1, source_target_pairs={{0,32},{1,33},{2,34},{3,35},{4,36},{5,37},{6,38},{7,39},{8,40},{9,... | collective-permute-start | bytes 835592 | tf_op jit(solution)/shard_map/ppermute | solution.py:186
  107.1 12.7 %collective-permute-start.17 = (bf16[136,1024]{1,0:T(8,128)(2,1)S(1)}, bf16[136,1024]{1,0:T(8,128)(2,1)S(1)}, u32[]{:S(2)}, u32[]{:S(2)}) collective-permute-start(bf16[136,1024]{1,0:T(8,128)(2,1)S(1)} %get-tuple-element.22), channel_id=1, source_target_pairs={{0,16},{1,17},{2,18},{3,19},{4,20},{5,21},{6,22},{7,23},{8,24},{9,... | collective-permute-start | bytes 835592 | tf_op jit(solution)/shard_map/ppermute | solution.py:186
  114.7 10.3 %collective-permute-start.16 = (bf16[136,1024]{1,0:T(8,128)(2,1)S(1)}, bf16[136,1024]{1,0:T(8,128)(2,1)S(1)}, u32[]{:S(2)}, u32[]{:S(2)}) collective-permute-start(bf16[136,1024]{1,0:T(8,128)(2,1)S(1)} %get-tuple-element.19), channel_id=1, source_target_pairs={{0,0},{1,1},{2,2},{3,3},{4,4},{5,5},{6,6},{7,7},{8,8},{9,9},{10,10... | collective-permute-start | bytes 835592 | tf_op jit(solution)/shard_map/ppermute | solution.py:186
  125.9 3.2 %collective-permute-start.20 = (bf16[136,512]{1,0:T(8,128)(2,1)S(1)}, bf16[136,512]{1,0:T(8,128)(2,1)S(1)}, u32[]{:S(2)}, u32[]{:S(2)}) collective-permute-start(bf16[136,512]{1,0:T(8,128)(2,1)S(1)} %get-tuple-element.25), channel_id=1, source_target_pairs={{0,64},{1,65},{2,66},{3,67},{4,68},{5,69},{6,70},{7,71},{8,72},{9,... | collective-permute-start | bytes 417800 | tf_op jit(solution)/shard_map/ppermute | solution.py:186
  129.1 0.7 copy-start.15

commit v5 on v3

--- a/solution.py
+++ b/solution.py
@@ -171,6 +171,7 @@
         out_specs=vmem,
         out_shape=jax.ShapeDtypeStruct((ROWS, 1024), BF),
         cost_estimate=pl.CostEstimate(flops=1000, bytes_accessed=600000, transcendentals=0),
+        compiler_params=pltpu.CompilerParams(vmem_limit_bytes=56 * 1024 * 1024),
         name="join",
     )(late, keep, other)
 

time: 132 us -> 132 us (level)
  no operation moved by 1% of the time
where the time goes in v5:
time: 132 us; the launch traced here: 131 us
  starting transfers between devices  82.2 us (62%)
  waiting for transfers between devices  27.1 us (21%)
  Pallas kernels  15.9 us (12%)
  local copies, waits for them, and re-layouts  3.54 us (3%)
  other arithmetic  1.69 us (1%)
    ppermute x20, starting transfers between devices, permute(): return lax.ppermute(block, ('tp', 'cp'), pairs)  79.3 us
    ppermute x20, waiting for transfers between devices, permute(): return lax.ppermute(block, ('tp', 'cp'), pairs)  27.1 us
    pallas_call x1, Pallas kernels, run_conv(): pl.pallas_call(conv_kernel, grid=(1024 // CONV,), in_specs=[pl.BlockSpec(...  7.68 us
    pallas_call x2, Pallas kernels, run_mm(): pl.pallas_call(mm_kernel, in_specs=[pl.BlockSpec(memory_space=pltpu.SMEM)...  4.16 us
    unnamed x34, local copies, waits for them, and re-layouts  3.54 us
    ppermute x1, starting transfers between devices, local(): halo = lax.ppermute(packed, 'cp', [(i, i + 1) for i in range(NX * NZ - 1)])  2.93 us
  transfers between devices with their start and end apart: 21, of which 10 were waited for; matrix products, arithmetic and copies ran while one was open for 0% of the time, Pallas kernels for 8%

profile of v5, /device:TPU:24, one launch (start us, length us, event | category | flops | bytes accessed | tf_op | source)
XLA Modules:
  0.0 131.0 jit_solution(17440628613861875206)
XLA Ops:
  0.0 5.2 %collective-permute-start.4 = (bf16[1024,128]{1,0:T(8,128)(2,1)}, bf16[1024,128]{1,0:T(8,128)(2,1)S(1)}, u32[]{:S(2)}, u32[]{:S(2)}) collective-permute-start(bf16[1024,128]{1,0:T(8,128)(2,1)} %rest_0_.3), channel_id=1, source_target_pairs={{0,2},{1,3},{2,4},{3,5},{4,6},{5,7},{6,8},{7,9},{8,10},{9,11},{10,... | collective-permute-start | bytes 786440 | tf_op jit(solution)/shard_map/ppermute | solution.py:187
  5.2 8.6 %collective-permute-start.5 = (bf16[1024,128]{1,0:T(8,128)(2,1)}, bf16[1024,128]{1,0:T(8,128)(2,1)S(1)}, u32[]{:S(2)}, u32[]{:S(2)}) collective-permute-start(bf16[1024,128]{1,0:T(8,128)(2,1)} %rest_0_.3), channel_id=1, source_target_pairs={{0,14},{1,15},{2,0},{3,1},{4,2},{5,3},{6,4},{7,5},{8,6},{9,7},{10,... | collective-permute-start | bytes 786440 | tf_op jit(solution)/shard_map/ppermute | solution.py:187
  13.8 2.3 %pack.1 = bf16[144,1024]{1,0:T(8,128)(2,1)} custom-call(bf16[3,136,1024]{2,1,0:T(8,128)(2,1)} %x_ref.3, f32[3,3,1024]{2,1,0:T(4,128)} %taps_ref.3), custom_call_target="tpu_custom_call" | custom-call | flops 3000000 | bytes 6000000 | tf_op jit(solution)/shard_map/pack/pallas_call | solution.py:77
  16.1 2.9 %collective-permute-start = (bf16[144,1024]{1,0:T(8,128)(2,1)}, bf16[144,1024]{1,0:T(8,128)(2,1)S(1)}, u32[]{:S(2)}, u32[]{:S(2)}) collective-permute-start(bf16[144,1024]{1,0:T(8,128)(2,1)} %pack.1), channel_id=1, source_target_pairs={{0,1},{1,2},{2,3},{3,4},{4,5},{5,6},{6,7},{7,8},{8,9},{9,10},{10,1... | collective-permute-start | bytes 884744 | tf_op jit(solution)/shard_map/ppermute | solution.py:205
  19.0 1.6 %collective-permute-done.4.refs_0_ = bf16[1024,128]{1,0:T(8,128)(2,1)S(1)} collective-permute-done((bf16[1024,128]{1,0:T(8,128)(2,1)}, bf16[1024,128]{1,0:T(8,128)(2,1)S(1)}, u32[]{:S(2)}, u32[]{:S(2)}) %collective-permute-start.4) | collective-permute-done | bytes 262176 | tf_op jit(solution)/shard_map/ppermute | solution.py:187
  20.6 4.7 %collective-permute-done.5.refs_1_ = bf16[1024,128]{1,0:T(8,128)(2,1)S(1)} collective-permute-done((bf16[1024,128]{1,0:T(8,128)(2,1)}, bf16[1024,128]{1,0:T(8,128)(2,1)S(1)}, u32[]{:S(2)}, u32[]{:S(2)}) %collective-permute-start.5) | collective-permute-done | bytes 262176 | tf_op jit(solution)/shard_map/ppermute | solution.py:187
  25.3 0.7 copy-done.10
  26.0 3.9 %collective-permute-start.6 = (bf16[1024,128]{1,0:T(8,128)(2,1)}, bf16[1024,128]{1,0:T(8,128)(2,1)S(1)}, u32[]{:S(2)}, u32[]{:S(2)}) collective-permute-start(bf16[1024,128]{1,0:T(8,128)(2,1)} %get-tuple-element.11.rest_1_), channel_id=1, source_target_pairs={{0,2},{1,3},{2,4},{3,5},{4,6},{5,7},{6,8},{7,9},{8,10},{9,11},{10,... | collective-permute-start | bytes 786440 | tf_op jit(solution)/shard_map/ppermute | solution.py:187
  29.9 4.4 %collective-permute-start.7 = (bf16[1024,128]{1,0:T(8,128)(2,1)}, bf16[1024,128]{1,0:T(8,128)(2,1)S(1)}, u32[]{:S(2)}, u32[]{:S(2)}) collective-permute-start(bf16[1024,128]{1,0:T(8,128)(2,1)} %get-tuple-element.12.rest_2_), channel_id=1, source_target_pairs={{0,14},{1,15},{2,0},{3,1},{4,2},{5,3},{6,4},{7,5},{8,6},{9,7},{10,... | collective-permute-start | bytes 786440 | tf_op jit(solution)/shard_map/ppermute | solution.py:187
  34.3 0.7 copy-done.14
  35.0 7.7 %conv.1 = bf16[136,1024]{1,0:T(8,128)(2,1)} custom-call(bf16[3,136,1024]{2,1,0:T(8,128)(2,1)} %x_ref.3, bf16[144,1024]{1,0:T(8,128)(2,1)} %copy-done.14, f32[3,3,1024]{2,1,0:T(4,128)} %taps_ref.3, f32[128,1024]{1,0:T(8,128)} %long_ref.1, f32[1,1024]{1,0:T(1,128)} %bitcast.11), custom_call_target="tpu_custom_call" | custom-call | flops 36000000 | bytes 20000000 | tf_op jit(solution)/shard_map/conv/pallas_call | solution.py:93
  42.7 4.8 %collective-permute-start.3 = (bf16[136,1024]{1,0:T(8,128)(2,1)}, bf16[136,1024]{1,0:T(8,128)(2,1)S(1)}, u32[]{:S(2)}, u32[]{:S(2)}) collective-permute-start(bf16[136,1024]{1,0:T(8,128)(2,1)} %conv.1), channel_id=1, source_target_pairs={{0,48},{1,49},{2,50},{3,51},{4,52},{5,53},{6,54},{7,55},{8,56},{9,... | collective-permute-start | bytes 835592 | tf_op jit(solution)/shard_map/ppermute | solution.py:187
  47.5 2.0 %collective-permute-start.11 = (bf16[136,1024]{1,0:T(8,128)(2,1)}, bf16[136,1024]{1,0:T(8,128)(2,1)S(1)}, u32[]{:S(2)}, u32[]{:S(2)}) collective-permute-start(bf16[136,1024]{1,0:T(8,128)(2,1)} %conv.1), channel_id=1, source_target_pairs={{0,1},{1,0},{2,3},{3,2},{4,5},{5,4},{6,7},{7,6},{8,9},{9,8},{10,11... | collective-permute-start | bytes 835592 | tf_op jit(solution)/shard_map/ppermute | solution.py:187
  49.6 0.7 copy-done.4
  50.3 0.7 copy-done.6
  51.0 3.2 %collective-permute-start.8 = (bf16[1024,128]{1,0:T(8,128)(2,1)}, bf16[1024,128]{1,0:T(8,128)(2,1)S(1)}, u32[]{:S(2)}, u32[]{:S(2)}) collective-permute-start(bf16[1024,128]{1,0:T(8,128)(2,1)} %get-tuple-element.13.rest_3_), channel_id=1, source_target_pairs={{0,2},{1,3},{2,4},{3,5},{4,6},{5,7},{6,8},{7,9},{8,10},{9,11},{10,... | collective-permute-start | bytes 786440 | tf_op jit(solution)/shard_map/ppermute | solution.py:187
  54.2 4.7 %collective-permute-start.9 = (bf16[1024,128]{1,0:T(8,128)(2,1)}, bf16[1024,128]{1,0:T(8,128)(2,1)S(1)}, u32[]{:S(2)}, u32[]{:S(2)}) collective-permute-start(bf16[1024,128]{1,0:T(8,128)(2,1)} %get-tuple-element.14.rest_4_), channel_id=1, source_target_pairs={{0,14},{1,15},{2,0},{3,1},{4,2},{5,3},{6,4},{7,5},{8,6},{9,7},{10,... | collective-permute-start | bytes 786440 | tf_op jit(solution)/shard_map/ppermute | solution.py:187
  59.0 3.2 %collective-permute-start.2 = (bf16[136,1024]{1,0:T(8,128)(2,1)}, bf16[136,1024]{1,0:T(8,128)(2,1)S(1)}, u32[]{:S(2)}, u32[]{:S(2)}) collective-permute-start(bf16[136,1024]{1,0:T(8,128)(2,1)} %conv.1), channel_id=1, source_target_pairs={{0,32},{1,33},{2,34},{3,35},{4,36},{5,37},{6,38},{7,39},{8,40},{9,... | collective-permute-start | bytes 835592 | tf_op jit(solution)/shard_map/ppermute | solution.py:187
  62.1 2.4 %collective-permute-start.1 = (bf16[136,1024]{1,0:T(8,128)(2,1)}, bf16[136,1024]{1,0:T(8,128)(2,1)S(1)}, u32[]{:S(2)}, u32[]{:S(2)}) collective-permute-start(bf16[136,1024]{1,0:T(8,128)(2,1)} %conv.1), channel_id=1, source_target_pairs={{0,16},{1,17},{2,18},{3,19},{4,20},{5,21},{6,22},{7,23},{8,24},{9,... | collective-permute-start | bytes 835592 | tf_op jit(solution)/shard_map/ppermute | solution.py:187
  64.6 4.2 %collective-permute-start.14 = (bf16[136,1024]{1,0:T(8,128)(2,1)S(1)}, bf16[136,1024]{1,0:T(8,128)(2,1)S(1)}, u32[]{:S(2)}, u32[]{:S(2)}) collective-permute-start(bf16[136,1024]{1,0:T(8,128)(2,1)S(1)} %collective-permute-done.11), channel_id=1, source_target_pairs={{0,48},{1,49},{2,50},{3,51},{4,52},{5,53},{6,54},{7,55},{8,56},{9,... | collective-permute-start | bytes 835592 | tf_op jit(solution)/shard_map/ppermute | solution.py:187
  68.8 0.5 collective-permute-done.8.refs_0_
  69.3 2.7 %collective-permute-start.13 = (bf16[136,1024]{1,0:T(8,128)(2,1)S(1)}, bf16[136,1024]{1,0:T(8,128)(2,1)S(1)}, u32[]{:S(2)}, u32[]{:S(2)}) collective-permute-start(bf16[136,1024]{1,0:T(8,128)(2,1)S(1)} %collective-permute-done.11), channel_id=1, source_target_pairs={{0,32},{1,33},{2,34},{3,35},{4,36},{5,37},{6,38},{7,39},{8,40},{9,... | collective-permute-start | bytes 835592 | tf_op jit(solution)/shard_map/ppermute | solution.py:187
  72.0 3.1 %collective-permute-start.12 = (bf16[136,1024]{1,0:T(8,128)(2,1)S(1)}, bf16[136,1024]{1,0:T(8,128)(2,1)S(1)}, u32[]{:S(2)}, u32[]{:S(2)}) collective-permute-start(bf16[136,1024]{1,0:T(8,128)(2,1)S(1)} %collective-permute-done.11), channel_id=1, source_target_pairs={{0,16},{1,17},{2,18},{3,19},{4,20},{5,21},{6,22},{7,23},{8,24},{9,... | collective-permute-start | bytes 835592 | tf_op jit(solution)/shard_map/ppermute | solution.py:187
  75.2 0.1 pad_add_fusion
  75.3 2.4 %collective-permute-start.10 = (bf16[1024,128]{1,0:T(8,128)(2,1)}, bf16[1024,128]{1,0:T(8,128)(2,1)S(1)}, u32[]{:S(2)}, u32[]{:S(2)}) collective-permute-start(bf16[1024,128]{1,0:T(8,128)(2,1)} %get-tuple-element.15.rest_5_), channel_id=1, source_target_pairs={{0,2},{1,3},{2,4},{3,5},{4,6},{5,7},{6,8},{7,9},{8,10},{9,11},{10,... | collective-permute-start | bytes 786440 | tf_op jit(solution)/shard_map/ppermute | solution.py:187
  77.7 0.1 pad_maximum_fusion.a_ref
  77.8 0.0 copy-start.12
  77.8 3.8 %collective-permute-done.14 = bf16[136,1024]{1,0:T(8,128)(2,1)S(1)} collective-permute-done((bf16[136,1024]{1,0:T(8,128)(2,1)S(1)}, bf16[136,1024]{1,0:T(8,128)(2,1)S(1)}, u32[]{:S(2)}, u32[]{:S(2)}) %collective-permute-start.14) | collective-permute-done | bytes 278560 | tf_op jit(solution)/shard_map/ppermute | solution.py:187
  81.7 1.2 collective-permute-done.12
  82.9 0.1 pad_maximum_fusion.1.a_ref
  83.0 5.6 %collective-permute-done.10.rest_7_ = bf16[1024,128]{1,0:T(8,128)(2,1)S(1)} collective-permute-done((bf16[1024,128]{1,0:T(8,128)(2,1)}, bf16[1024,128]{1,0:T(8,128)(2,1)S(1)}, u32[]{:S(2)}, u32[]{:S(2)}) %collective-permute-start.10) | collective-permute-done | bytes 262176 | tf_op jit(solution)/shard_map/ppermute | solution.py:187
  88.6 2.1 %mm.2 = bf16[4,136,1024]{2,1,0:T(8,128)(2,1)S(1)} custom-call(s32[5]{0:T(128)S(1)} %get-tuple-element.27.where_ref, bf16[544,1024]{1,0:T(8,128)(2,1)S(1)} %pad_maximum_fusion.a_ref, bf16[1024,128]{1,0:T(8,128)(2,1)S(1)} %copy-done.12, bf16[1024,128]{1,0:T(8,128)(2,1)S(1)} %copy-done.9, bf16[1024,128]{1,0:T(8,128)(2,1)S(1)} %copy-done.11, ...), custom_call_target="tpu_custom_call" | custom-call | flops 1140000000 | bytes 5000000 | tf_op jit(solution)/shard_map/mm/pallas_call | solution.py:129
  90.7 2.1 %mm.3 = bf16[4,136,1024]{2,1,0:T(8,128)(2,1)S(1)} custom-call(s32[5]{0:T(128)S(1)} %get-tuple-element.28.where_ref, bf16[544,1024]{1,0:T(8,128)(2,1)S(1)} %pad_maximum_fusion.1.a_ref, bf16[1024,128]{1,0:T(8,128)(2,1)S(1)} %copy-done.12, bf16[1024,128]{1,0:T(8,128)(2,1)S(1)} %copy-done.9, bf16[1024,128]{1,0:T(8,128)(2,1)S(1)} %copy-done.11, ...), custom_call_target="tpu_custom_call" | custom-call | flops 1140000000 | bytes 5000000 | tf_op jit(solution)/shard_map/mm/pallas_call | solution.py:129
  92.8 0.2 broadcast_select_fusion.1
  92.9 1.9 %collective-permute-start.15 = (bf16[4,136,1024]{2,1,0:T(8,128)(2,1)S(1)}, bf16[4,136,1024]{2,1,0:T(8,128)(2,1)S(1)}, u32[]{:S(2)}, u32[]{:S(2)}) collective-permute-start(bf16[4,136,1024]{2,1,0:T(8,128)(2,1)S(1)} %get-tuple-element.24), channel_id=1, source_target_pairs={{0,64},{1,65},{2,66},{3,67},{4,68},{5,69},{6,70},{7,71},{8,72},{9,... | collective-permute-start | bytes 3342344 | tf_op jit(solution)/shard_map/ppermute | solution.py:187
  94.9 2.7 %collective-permute-done.15 = bf16[4,136,1024]{2,1,0:T(8,128)(2,1)S(1)} collective-permute-done((bf16[4,136,1024]{2,1,0:T(8,128)(2,1)S(1)}, bf16[4,136,1024]{2,1,0:T(8,128)(2,1)S(1)}, u32[]{:S(2)}, u32[]{:S(2)}) %collective-permute-start.15) | collective-permute-done | bytes 1114144 | tf_op jit(solution)/shard_map/ppermute | solution.py:187
  97.6 0.4 fusion
  98.0 2.1 %collective-permute-start.19 = (bf16[136,1024]{1,0:T(8,128)(2,1)S(1)}, bf16[136,1024]{1,0:T(8,128)(2,1)S(1)}, u32[]{:S(2)}, u32[]{:S(2)}) collective-permute-start(bf16[136,1024]{1,0:T(8,128)(2,1)S(1)} %get-tuple-element.20), channel_id=1, source_target_pairs={{0,48},{1,49},{2,50},{3,51},{4,52},{5,53},{6,54},{7,55},{8,56},{9,... | collective-permute-start | bytes 835592 | tf_op jit(solution)/shard_map/ppermute | solution.py:187
  100.2 7.1 %collective-permute-start.18 = (bf16[136,1024]{1,0:T(8,128)(2,1)S(1)}, bf16[136,1024]{1,0:T(8,128)(2,1)S(1)}, u32[]{:S(2)}, u32[]{:S(2)}) collective-permute-start(bf16[136,1024]{1,0:T(8,128)(2,1)S(1)} %get-tuple-element.21), channel_id=1, source_target_pairs={{0,32},{1,33},{2,34},{3,35},{4,36},{5,37},{6,38},{7,39},{8,40},{9,... | collective-permute-start | bytes 835592 | tf_op jit(solution)/shard_map/ppermute | solution.py:187
  107.2 5.2 %collective-permute-start.17 = (bf16[136,1024]{1,0:T(8,128)(2,1)S(1)}, bf16[136,1024]{1,0:T(8,128)(2,1)S(1)}, u32[]{:S(2)}, u32[]{:S(2)}) collective-permute-start(bf16[136,1024]{1,0:T(8,128)(2,1)S(1)} %get-tuple-element.22), channel_id=1, source_target_pairs={{0,16},{1,17},{2,18},{3,19},{4,20},{5,21},{6,22},{7,23},{8,24},{9,... | collective-permute-start | bytes 835592 | tf_op jit(solution)/shard_map/ppermute | solution.py:187
  112.4 3.6 %collective-permute-start.16 = (bf16[136,1024]{1,0:T(8,128)(2,1)S(1)}, bf16[136,1024]{1,0:T(8,128)(2,1)S(1)}, u32[]{:S(2)}, u32[]{:S(2)}) collective-permute-start(bf16[136,1024]{1,0:T(8,128)(2,1)S(1)} %get-tuple-element.19), channel_id=1, source_target_pairs={{0,0},{1,1},{2,2},{3,3},{4,4},{5,5},{6,6},{7,7},{8,8},{9,9},{10,10... | collective-permute-start | bytes 835592 | tf_op jit(solution)/shard_map/ppermute | solution.py:187
  116.0 1.7 %collective-permute-done.17 = bf16[136,1024]{1,0:T(8,128)(2,1)S(1)} collective-permute-done((bf16[136,1024]{1,0:T(8,128)(2,1)S(1)}, bf16[136,1024]{1,0:T(8,128)(2,1)S(1)}, u32[]{:S(2)}, u32[]{:S(2)}) %collective-permute-start.17) | collective-permute-done | bytes 278560 | tf_op jit(solution)/shard_map/ppermute | solution.py:187
  117.8 4.3 %collective-permute-done.16 = bf16[136,1024]{1,0:T(8,128)(2,1)S(1)} collective-permute-done((bf16[136,1024]{1,0:T(8,128)(2,1)S(1)}, bf16[136,1024]{1,0:T(8,128)(2,1)S(1)}, u32[]{:S(2)}, u32[]{:S(2)}) %collective-permute-start.16) | collective-permute-done | bytes 278560 | tf_op jit(solution)/shard_map/ppermute | solution.py:187
  122.1 0.9 add_convert_fusion.4
  123.0 4.6 %collective-permute-start.20 = (bf16[136,512]{1,0:T(8,128)(2,1)S(1)}, bf16[136,512]{1,0:T(8,128)(2,1)S(1)}, u32[]{:S(2)}, u32[]{:S(2)}) collective-permute-start(bf16[136,512]{1,0:T(8,128)(2,1)S(1)} %get-tuple-element.25), channel_id=1, source_target_pairs={{0,64},{1,65},{2,66},{3,67},{4,68},{5,69},{6,70},{7,71},{8,72},{9,... | collective-permute-start | bytes 417800 | tf_op jit(solution)/shard_map/ppermute | solution.py:187
  127.6 1.0 collective-permute-done.20.other_ref
  128.6 0.7 copy-done.15
  129.2 1.7 %join.1 = bf16[136,1024]{1,0:T(8,128)(2,1)} custom-call(s32[1]{0:T(128)} %bitcast.late_ref, bf16[136,512]{1,0:T(8,128)(2,1)} %get-tuple-element.26.keep_ref, bf16[136,512]{1,0:T(8,128)(2,1)} %copy-done.15), custom_call_target="tpu_custom_call" | custom-call | flops 1000 | bytes 600000 | tf_op jit(solution)/shard_map/join/pallas_call | solution.py:168
  (43 shorter events, 0.1 us)
Async XLA Ops:
  0.0 20.6 %collective-permute-start.4 = (bf16[1024,128]{1,0:T(8,128)(2,1)}, bf16[1024,128]{1,0:T(8,128)(2,1)S(1)}, u32[]{:S(2)}, u32[]{:S(2)}) collective-permute-start(bf16[1024,128]{1,0:T(8,128)(2,1)} %rest_0_.3), channel_id=1, source_target_pairs={{0,2},{1,3},{2,4},{3,5},{4,6},{5,7},{6,8},{7,9},{8,10},{9,11},{10,... | collective-permute-start | bytes 786440 | tf_op jit(solution)/shard_map/ppermute | solution.py:187
  5.2 20.1 %collective-permute-start.5 = (bf16[1024,128]{1,0:T(8,128)(2,1)}, bf16[1024,128]{1,0:T(8,128)(2,1)S(1)}, u32[]{:S(2)}, u32[]{:S(2)}) collective-permute-start(bf16[1024,128]{1,0:T(8,128)(2,1)} %rest_0_.3), channel_id=1, source_target_pairs={{0,14},{1,15},{2,0},{3,1},{4,2},{5,3},{6,4},{7,5},{8,6},{9,7},{10,... | collective-permute-start | bytes 786440 | tf_op jit(solution)/shard_map/ppermute | solution.py:187
  16.1 18.2 %collective-permute-start = (bf16[144,1024]{1,0:T(8,128)(2,1)}, bf16[144,1024]{1,0:T(8,128)(2,1)S(1)}, u32[]{:S(2)}, u32[]{:S(2)}) collective-permute-start(bf16[144,1024]{1,0:T(8,128)(2,1)} %pack.1), channel_id=1, source_target_pairs={{0,1},{1,2},{2,3},{3,4},{4,5},{5,6},{6,7},{7,8},{8,9},{9,10},{10,1... | collective-permute-start | bytes 884744 | tf_op jit(solution)/shard_map/ppermute | solution.py:205
  20.6 4.7 %copy-start.8 = (bf16[1024,128]{1,0:T(8,128)(2,1)}, bf16[1024,128]{1,0:T(8,128)(2,1)S(1)}, u32[]{:S(2)}) copy-start(bf16[1024,128]{1,0:T(8,128)(2,1)S(1)} %collective-permute-done.4.refs_0_) | copy-start | bytes 786436
  25.3 0.7 copy-start.10
  26.0 23.6 %collective-permute-start.6 = (bf16[1024,128]{1,0:T(8,128)(2,1)}, bf16[1024,128]{1,0:T(8,128)(2,1)S(1)}, u32[]{:S(2)}, u32[]{:S(2)}) collective-permute-start(bf16[1024,128]{1,0:T(8,128)(2,1)} %get-tuple-element.11.rest_1_), channel_id=1, source_target_pairs={{0,2},{1,3},{2,4},{3,5},{4,6},{5,7},{6,8},{7,9},{8,10},{9,11},{10,... | collective-permute-start | bytes 786440 | tf_op jit(solution)/shard_map/ppermute | solution.py:187
  29.9 19.7 %collective-permute-start.7 = (bf16[1024,128]{1,0:T(8,128)(2,1)}, bf16[1024,128]{1,0:T(8,128)(2,1)S(1)}, u32[]{:S(2)}, u32[]{:S(2)}) collective-permute-start(bf16[1024,128]{1,0:T(8,128)(2,1)} %get-tuple-element.12.rest_2_), channel_id=1, source_target_pairs={{0,14},{1,15},{2,0},{3,1},{4,2},{5,3},{6,4},{7,5},{8,6},{9,7},{10,... | collective-permute-start | bytes 786440 | tf_op jit(solution)/shard_map/ppermute | solution.py:187
  34.3 0.7 copy-start.14
  35.0 40.1 %copy-start.16 = (s32[4]{0:T(128)S(1)}, s32[4]{0:T(128)}, u32[]{:S(2)}) copy-start(s32[4]{0:T(128)} %constant.63.clone) | copy-start | bytes 52
  42.7 35.0 %copy-start.13 = (bf16[136,1024]{1,0:T(8,128)(2,1)S(1)}, bf16[136,1024]{1,0:T(8,128)(2,1)}, u32[]{:S(2)}) copy-start(bf16[136,1024]{1,0:T(8,128)(2,1)} %conv.1) | copy-start | bytes 835588
  42.7 19.4 %collective-permute-start.3 = (bf16[136,1024]{1,0:T(8,128)(2,1)}, bf16[136,1024]{1,0:T(8,128)(2,1)S(1)}, u32[]{:S(2)}, u32[]{:S(2)}) collective-permute-start(bf16[136,1024]{1,0:T(8,128)(2,1)} %conv.1), channel_id=1, source_target_pairs={{0,48},{1,49},{2,50},{3,51},{4,52},{5,53},{6,54},{7,55},{8,56},{9,... | collective-permute-start | bytes 835592 | tf_op jit(solution)/shard_map/ppermute | solution.py:187
  47.5 17.1 %collective-permute-start.11 = (bf16[136,1024]{1,0:T(8,128)(2,1)}, bf16[136,1024]{1,0:T(8,128)(2,1)S(1)}, u32[]{:S(2)}, u32[]{:S(2)}) collective-permute-start(bf16[136,1024]{1,0:T(8,128)(2,1)} %conv.1), channel_id=1, source_target_pairs={{0,1},{1,0},{2,3},{3,2},{4,5},{5,4},{6,7},{7,6},{8,9},{9,8},{10,11... | collective-permute-start | bytes 835592 | tf_op jit(solution)/shard_map/ppermute | solution.py:187
  49.5 0.7 copy-start.4
  50.3 0.7 copy-start.6
  51.0 18.3 %collective-permute-start.8 = (bf16[1024,128]{1,0:T(8,128)(2,1)}, bf16[1024,128]{1,0:T(8,128)(2,1)S(1)}, u32[]{:S(2)}, u32[]{:S(2)}) collective-permute-start(bf16[1024,128]{1,0:T(8,128)(2,1)} %get-tuple-element.13.rest_3_), channel_id=1, source_target_pairs={{0,2},{1,3},{2,4},{3,5},{4,6},{5,7},{6,8},{7,9},{8,10},{9,11},{10,... | collective-permute-start | bytes 786440 | tf_op jit(solution)/shard_map/ppermute | solution.py:187
  54.2 17.8 %collective-permute-start.9 = (bf16[1024,128]{1,0:T(8,128)(2,1)}, bf16[1024,128]{1,0:T(8,128)(2,1)S(1)}, u32[]{:S(2)}, u32[]{:S(2)}) collective-permute-start(bf16[1024,128]{1,0:T(8,128)(2,1)} %get-tuple-element.14.rest_4_), channel_id=1, source_target_pairs={{0,14},{1,15},{2,0},{3,1},{4,2},{5,3},{6,4},{7,5},{8,6},{9,7},{10,... | collective-permute-start | bytes 786440 | tf_op jit(solution)/shard_map/ppermute | solution.py:187
  59.0 16.3 %collective-permute-start.2 = (bf16[136,1024]{1,0:T(8,128)(2,1)}, bf16[136,1024]{1,0:T(8,128)(2,1)S(1)}, u32[]{:S(2)}, u32[]{:S(2)}) collective-permute-start(bf16[136,1024]{1,0:T(8,128)(2,1)} %conv.1), channel_id=1, source_target_pairs={{0,32},{1,33},{2,34},{3,35},{4,36},{5,37},{6,38},{7,39},{8,40},{9,... | collective-permute-start | bytes 835592 | tf_op jit(solution)/shard_map/ppermute | solution.py:187
  62.1 15.5 %collective-permute-start.1 = (bf16[136,1024]{1,0:T(8,128)(2,1)}, bf16[136,1024]{1,0:T(8,128)(2,1)S(1)}, u32[]{:S(2)}, u32[]{:S(2)}) collective-permute-start(bf16[136,1024]{1,0:T(8,128)(2,1)} %conv.1), channel_id=1, source_target_pairs={{0,16},{1,17},{2,18},{3,19},{4,20},{5,21},{6,22},{7,23},{8,24},{9,... | collective-permute-start | bytes 835592 | tf_op jit(solution)/shard_map/ppermute | solution.py:187
  64.6 17.1 %collective-permute-start.14 = (bf16[136,1024]{1,0:T(8,128)(2,1)S(1)}, bf16[136,1024]{1,0:T(8,128)(2,1)S(1)}, u32[]{:S(2)}, u32[]{:S(2)}) collective-permute-start(bf16[136,1024]{1,0:T(8,128)(2,1)S(1)} %collective-permute-done.11), channel_id=1, source_target_pairs={{0,48},{1,49},{2,50},{3,51},{4,52},{5,53},{6,54},{7,55},{8,56},{9,... | collective-permute-start | bytes 835592 | tf_op jit(solution)/shard_map/ppermute | solution.py:187
  69.3 6.0 %copy-start = (bf16[1024,128]{1,0:T(8,128)(2,1)}, bf16[1024,128]{1,0:T(8,128)(2,1)S(1)}, u32[]{:S(2)}) copy-start(bf16[1024,128]{1,0:T(8,128)(2,1)S(1)} %collective-permute-done.8.refs_0_) | copy-start | bytes 786436
  69.3 12.4 %collective-permute-start.13 = (bf16[136,1024]{1,0:T(8,128)(2,1)S(1)}, bf16[136,1024]{1,0:T(8,128)(2,1)S(1)}, u32[]{:S(2)}, u32[]{:S(2)}) collective-permute-start(bf16[136,1024]{1,0:T(8,128)(2,1)S(1)} %collective-permute-done.11), channel_id=1, source_target_pairs={{0,32},{1,33},{2,34},{3,35},{4,36},{5,37},{6,38},{7,39},{8,40},{9,... | collective-permute-start | bytes 835592 | tf_op jit(solution)/shard_map/ppermute | solution.py:187
  72.0 3.2 %copy-start.2 = (bf16[1024,128]{1,0:T(8,128)(2,1)}, bf16[1024,128]{1,0:T(8,128)(2,1)S(1)}, u32[]{:S(2)}) copy-start(bf16[1024,128]{1,0:T(8,128)(2,1)S(1)} %collective-permute-done.9.refs_1_) | copy-start | bytes 786436
  72.0 10.9 %collective-permute-start.12 = (bf16[136,1024]{1,0:T(8,128)(2,1)S(1)}, bf16[136,1024]{1,0:T(8,128)(2,1)S(1)}, u32[]{:S(2)}, u32[]{:S(2)}) collective-permute-start(bf16[136,1024]{1,0:T(8,128)(2,1)S(1)} %collective-permute-done.11), channel_id=1, source_target_pairs={{0,16},{1,17},{2,18},{3,19},{4,20},{5,21},{6,22},{7,23},{8,24},{9,... | collective-permute-start | bytes 835592 | tf_op jit(solution)/shard_map/ppermute | solution.py:187
  75.3 13.3 %collective-permute-start.10 = (bf16[1024,128]{1,0:T(8,128)(2,1)}, bf16[1024,128]{1,0:T(8,128)(2,1)S(1)}, u32[]{:S(2)}, u32[]{:S(2)}) collective-permute-start(bf16[1024,128]{1,0:T(8,128)(2,1)} %get-tuple-element.15.rest_5_), channel_id=1, source_target_pairs={{0,2},{1,3},{2,4},{3,5},{4,6},{5,7},{6,8},{7,9},{8,10},{9,11},{10,... | collective-permute-start | bytes 786440 | tf_op jit(solution)/shard_map/ppermute | solution.py:187
  77.8 10.8 %copy-start.1 = (bf16[1024,128]{1,0:T(8,128)(2,1)S(1)}, bf16[1024,128]{1,0:T(8,128)(2,1)}, u32[]{:S(2)}) copy-start(bf16[1024,128]{1,0:T(8,128)(2,1)} %get-tuple-element.15.rest_5_) | copy-start | bytes 786436
  77.8 10.8 %copy-start.3 = (bf16[1024,128]{1,0:T(8,128)(2,1)S(1)}, bf16[1024,128]{1,0:T(8,128)(2,1)}, u32[]{:S(2)}) copy-start(bf16[1024,128]{1,0:T(8,128)(2,1)} %get-tuple-element.16.rest_6_) | copy-start | bytes 786436
  77.8 10.8 %copy-start.5 = (bf16[1024,128]{1,0:T(8,128)(2,1)S(1)}, bf16[1024,128]{1,0:T(8,128)(2,1)}, u32[]{:S(2)}) copy-start(bf16[1024,128]{1,0:T(8,128)(2,1)} %get-tuple-element.13.rest_3_) | copy-start | bytes 786436
  77.8 10.8 %copy-start.7 = (bf16[1024,128]{1,0:T(8,128)(2,1)S(1)}, bf16[1024,128]{1,0:T(8,128)(2,1)}, u32[]{:S(2)}) copy-start(bf16[1024,128]{1,0:T(8,128)(2,1)} %get-tuple-element.14.rest_4_) | copy-start | bytes 786436
  77.8 10.8 %copy-start.9 = (bf16[1024,128]{1,0:T(8,128)(2,1)S(1)}, bf16[1024,128]{1,0:T(8,128)(2,1)}, u32[]{:S(2)}) copy-start(bf16[1024,128]{1,0:T(8,128)(2,1)} %get-tuple-element.11.rest_1_) | copy-start | bytes 786436
  77.8 10.8 %copy-start.11 = (bf16[1024,128]{1,0:T(8,128)(2,1)S(1)}, bf16[1024,128]{1,0:T(8,128)(2,1)}, u32[]{:S(2)}) copy-start(bf16[1024,128]{1,0:T(8,128)(2,1)} %get-tuple-element.12.rest_2_) | copy-start | bytes 786436
  77.8 10.8 %copy-start.12 = (bf16[1024,128]{1,0:T(8,128)(2,1)S(1)}, bf16[1024,128]{1,0:T(8,128)(2,1)}, u32[]{:S(2)}) copy-start(bf16[1024,128]{1,0:T(8,128)(2,1)} %rest_0_.3) | copy-start | bytes 786436
  92.9 4.6 %collective-permute-start.15 = (bf16[4,136,1024]{2,1,0:T(8,128)(2,1)S(1)}, bf16[4,136,1024]{2,1,0:T(8,128)(2,1)S(1)}, u32[]{:S(2)}, u32[]{:S(2)}) collective-permute-start(bf16[4,136,1024]{2,1,0:T(8,128)(2,1)S(1)} %get-tuple-element.24), channel_id=1, source_target_pairs={{0,64},{1,65},{2,66},{3,67},{4,68},{5,69},{6,70},{7,71},{8,72},{9,... | collective-permute-start | bytes 3342344 | tf_op jit(solution)/shard_map/ppermute | solution.py:187
  98.0 18.0 %collective-permute-start.19 = (bf16[136,1024]{1,0:T(8,128)(2,1)S(1)}, bf16[136,1024]{1,0:T(8,128)(2,1)S(1)}, u32[]{:S(2)}, u32[]{:S(2)}) collective-permute-start(bf16[136,1024]{1,0:T(8,128)(2,1)S(1)} %get-tuple-element.20), channel_id=1, source_target_pairs={{0,48},{1,49},{2,50},{3,51},{4,52},{5,53},{6,54},{7,55},{8,56},{9,... | collective-permute-start | bytes 835592 | tf_op jit(solution)/shard_map/ppermute | solution.py:187
  100.2 15.9 %collective-permute-start.18 = (bf16[136,1024]{1,0:T(8,128)(2,1)S(1)}, bf16[136,1024]{1,0:T(8,128)(2,1)S(1)}, u32[]{:S(2)}, u32[]{:S(2)}) collective-permute-start(bf16[136,1024]{1,0:T(8,128)(2,1)S(1)} %get-tuple-element.21), channel_id=1, source_target_pairs={{0,32},{1,33},{2,34},{3,35},{4,36},{5,37},{6,38},{7,39},{8,40},{9,... | collective-permute-start | bytes 835592 | tf_op jit(solution)/shard_map/ppermute | solution.py:187
  107.2 10.6 %collective-permute-start.17 = (bf16[136,1024]{1,0:T(8,128)(2,1)S(1)}, bf16[136,1024]{1,0:T(8,128)(2,1)S(1)}, u32[]{:S(2)}, u32[]{:S(2)}) collective-permute-start(bf16[136,1024]{1,0:T(8,128)(2,1)S(1)} %get-tuple-element.22), channel_id=1, source_target_pairs={{0,16},{1,17},{2,18},{3,19},{4,20},{5,21},{6,22},{7,23},{8,24},{9,... | collective-permute-start | bytes 835592 | tf_op jit(solution)/shard_map/ppermute | solution.py:187
  112.4 9.7 %collective-permute-start.16 = (bf16[136,1024]{1,0:T(8,128)(2,1)S(1)}, bf16[136,1024]{1,0:T(8,128)(2,1)S(1)}, u32[]{:S(2)}, u32[]{:S(2)}) collective-permute-start(bf16[136,1024]{1,0:T(8,128)(2,1)S(1)} %get-tuple-element.19), channel_id=1, source_target_pairs={{0,0},{1,1},{2,2},{3,3},{4,4},{5,5},{6,6},{7,7},{8,8},{9,9},{10,10... | collective-permute-start | bytes 835592 | tf_op jit(solution)/shard_map/ppermute | solution.py:187
  123.0 5.6 %collective-permute-start.20 = (bf16[136,512]{1,0:T(8,128)(2,1)S(1)}, bf16[136,512]{1,0:T(8,128)(2,1)S(1)}, u32[]{:S(2)}, u32[]{:S(2)}) collective-permute-start(bf16[136,512]{1,0:T(8,128)(2,1)S(1)} %get-tuple-element.25), channel_id=1, source_target_pairs={{0,64},{1,65},{2,66},{3,67},{4,68},{5,69},{6,70},{7,71},{8,72},{9,... | collective-permute-start | bytes 417800 | tf_op jit(solution)/shard_map/ppermute | solution.py:187
  128.6 0.7 copy-start.15
